TPU v7x, 32 devices: a whole 2x2x4 slice. The times are simulated.
32 devices in a mesh: dp: 16 (over z, x, core), tensor: 2 (over y).
Axes of the slice: x: 2, y: 2, z: 4, core: 2. Of those that a mesh axis runs over, the one named last changes fastest.
Arguments:
- latents: bfloat16 [32, 1024, 1152], P('dp', 'tensor'), may hold values from -6 to 6
- condition: bfloat16 [32, 1152], P('dp'), may hold values from -6 to 6
- cotangent: bfloat16 [32, 1024, 1152], P('dp', 'tensor'), may hold values from -6 to 6
- group_counts: int32 [16], P('dp'), may hold values from 1 to 2, as said below
- heads_weight: bfloat16 [1, 1152, 3, 1152], P(None, None, None, 'tensor'), may hold values from -0.1875 to 0.1875
- heads_bias: bfloat16 [1, 2, 1152], P(None, None, 'tensor'), may hold values from -3 to 3
- merge_weight: bfloat16 [1, 1152, 1152], P(None, 'tensor'), may hold values from -0.75 to 0.75
- merge_bias: bfloat16 [1, 1152], replicated, may hold values from -3 to 3
- up_weight: bfloat16 [1, 1152, 4608], P(None, None, 'tensor'), may hold values from -0.1875 to 0.1875
- up_bias: bfloat16 [1, 4608], P(None, 'tensor'), may hold values from -3 to 3
- down_weight: bfloat16 [1, 4608, 1152], P(None, 'tensor'), may hold values from -0.09375 to 0.09375
- down_bias: bfloat16 [1, 1152], replicated, may hold values from -3 to 3
- modulate_weight: bfloat16 [1, 1152, 6, 1152], P(None, None, None, 'tensor'), may hold values from -0.1875 to 0.1875
- modulate_bias: bfloat16 [1, 6, 1152], P(None, None, 'tensor'), may hold values from -3 to 3
Outputs:
- block_output: bfloat16 [32, 1024, 1152], P('dp', 'tensor')
- latent_grad: float32 [32, 1024, 1152], P('dp', 'tensor')
- condition_grad: float32 [32, 1152], P('dp')
- heads_weight_grad: float32 [1, 1152, 3, 1152], P(None, 'dp', None, 'tensor')
- heads_bias_grad: float32 [1, 2, 1152], P(None, None, 'tensor')
- merge_weight_grad: float32 [1, 1152, 1152], P(None, 'tensor', 'dp')
- merge_bias_grad: float32 [1, 1152], P(None, 'tensor')
- up_weight_grad: float32 [1, 1152, 4608], P(None, 'dp', 'tensor')
- up_bias_grad: float32 [1, 4608], P(None, 'tensor')
- down_weight_grad: float32 [1, 4608, 1152], P(None, 'tensor', 'dp')
- down_bias_grad: float32 [1, 1152], P(None, 'tensor')
- modulate_weight_grad: float32 [1, 1152, 6, 1152], P(None, 'dp', None, 'tensor')
- modulate_bias_grad: float32 [1, 6, 1152], P(None, None, 'tensor')
Inputs may be any that keep to these rules, and one draw needn't show every extreme that they name: Data group g holds the slots g * 2 to g * 2 + 1; its first group_counts[g] slots hold latents, the others are empty and their cotangent is not used. Some groups hold one latent and some hold 2.
All inputs are finite; a program needn't handle non-finite values.
Results may differ from a plain program's by a relative error of at most 0.02.
Values may be sent and summed in bfloat16 or wider, within the bound.
A program may use at most 320 MiB of HBM per device.

v0:
```python
import jax
import jax.numpy as jnp
from jax import lax
from jax.sharding import PartitionSpec as P

HEAD_DIM = 72
QUERY_BLOCK = 512


epsilon = 1e-06


def normalize(stream):
    average = jnp.mean(stream, -1, keepdims=True)
    centered = stream - average
    variance = jnp.mean(centered * centered, -1, keepdims=True)
    inverse = lax.rsqrt(variance + epsilon)
    return (centered * inverse, inverse)


def normalize_back(grad_norm, normed, inverse):
    first_mean = jnp.mean(grad_norm, -1, keepdims=True)
    second_mean = jnp.mean(grad_norm * normed, -1, keepdims=True)
    return inverse * (grad_norm - first_mean - normed * second_mean)


def gelu_tanh(values):
    return jax.nn.gelu(values, approximate=True)


def column_sums(operand):
    return jnp.sum(operand.astype(jnp.float32), 0)


def outer_rows(operand, other):
    return lax.dot_general(
        operand, other, (((0,), (0,)), ((), ())), preferred_element_type=jnp.float32
    )


def times_transposed(operand, weight):
    return lax.dot_general(
        operand, weight, (((1,), (1,)), ((), ())), preferred_element_type=jnp.float32
    )


def gather_tokens(values):
    return lax.all_gather(values, "tensor", axis=0, tiled=True)


def gather_grads(values):
    return lax.all_gather(values, "tensor", axis=0, tiled=True)


def scatter_branch(operand, weight):

    def partial_rows(first_row, row_count):
        return jnp.dot(operand, weight, preferred_element_type=jnp.float32)

    return lax.psum_scatter(
        partial_rows(
            jnp.int32(0), operand.shape[0] // lax.axis_size("tensor") * lax.axis_size("tensor")
        ).astype(jnp.bfloat16),
        "tensor",
        scatter_dimension=0,
        tiled=True,
    ).astype(jnp.float32)


def scatter_inputs(operand, weight):

    def partial_rows(first_row, row_count):
        return times_transposed(operand, weight)

    return lax.psum_scatter(
        partial_rows(
            jnp.int32(0), operand.shape[0] // lax.axis_size("tensor") * lax.axis_size("tensor")
        ).astype(jnp.bfloat16),
        "tensor",
        scatter_dimension=0,
        tiled=True,
    ).astype(jnp.float32)


def stack_member(layer_tuples, member):
    return jnp.stack([entry_tuple[member] for entry_tuple in layer_tuples])


def attend_forward(queries, key_rows, value_rows):
    length, heads_here = (queries.shape[0], queries.shape[1])
    blocks = length // QUERY_BLOCK
    score_scale = HEAD_DIM ** (-0.5)

    def one_block(query_block):
        scores = (
            jnp.einsum("qhd,khd->hqk", query_block, key_rows, preferred_element_type=jnp.float32)
            * score_scale
        )
        row_max = jnp.max(scores, -1, keepdims=True)
        exponent = jnp.exp(scores - row_max)
        row_total = jnp.sum(exponent, -1, keepdims=True)
        attn_probs = (exponent / row_total).astype(jnp.bfloat16)
        attended = jnp.einsum(
            "hqk,khd->qhd", attn_probs, value_rows, preferred_element_type=jnp.float32
        )
        return (attended.astype(jnp.bfloat16), (row_max + jnp.log(row_total))[:, :, 0])

    attended, logsum = lax.map(
        one_block, queries.reshape(blocks, QUERY_BLOCK, heads_here, HEAD_DIM)
    )
    return (attended.reshape(length, heads_here * HEAD_DIM), logsum)


def attend_backward(queries, key_rows, value_rows, logsum, grad_attended):
    length, heads_here = (queries.shape[0], queries.shape[1])
    blocks = length // QUERY_BLOCK
    score_scale = HEAD_DIM ** (-0.5)
    block_shape = (blocks, QUERY_BLOCK, heads_here, HEAD_DIM)

    def one_block(running, inputs_here):
        grad_keys, grad_values = running
        query_block, grad_block, logsum_block = inputs_here
        scores = (
            jnp.einsum("qhd,khd->hqk", query_block, key_rows, preferred_element_type=jnp.float32)
            * score_scale
        )
        attn_probs = jnp.exp(scores - logsum_block[:, :, None])
        grad_values = grad_values + jnp.einsum(
            "hqk,qhd->khd",
            attn_probs.astype(jnp.bfloat16),
            grad_block,
            preferred_element_type=jnp.float32,
        )
        grad_probs = jnp.einsum(
            "qhd,khd->hqk", grad_block, value_rows, preferred_element_type=jnp.float32
        )
        row_dot = jnp.sum(attn_probs * grad_probs, -1, keepdims=True)
        grad_scores = (attn_probs * (grad_probs - row_dot)).astype(jnp.bfloat16)
        grad_queries = (
            jnp.einsum("hqk,khd->qhd", grad_scores, key_rows, preferred_element_type=jnp.float32)
            * score_scale
        )
        grad_keys = (
            grad_keys
            + jnp.einsum(
                "hqk,qhd->khd", grad_scores, query_block, preferred_element_type=jnp.float32
            )
            * score_scale
        )
        return ((grad_keys, grad_values), grad_queries.astype(jnp.bfloat16))

    zeros_kv = jnp.zeros((length, heads_here, HEAD_DIM), jnp.float32)
    scanned = (queries.reshape(block_shape), grad_attended.reshape(block_shape), logsum)
    (grad_keys, grad_values), grad_queries = lax.scan(one_block, (zeros_kv, zeros_kv), scanned)
    flat_shape = (length, heads_here * HEAD_DIM)
    return (
        grad_queries.reshape(flat_shape),
        grad_keys.astype(jnp.bfloat16).reshape(flat_shape),
        grad_values.astype(jnp.bfloat16).reshape(flat_shape),
    )


def forward_layer(stream, modulation, layer_weights, heads_here):
    (
        flat_heads,
        heads_offset,
        merge_weight,
        merge_bias,
        up_weight,
        up_bias,
        down_weight,
        down_bias,
    ) = layer_weights
    length = stream.shape[0] * lax.axis_size("tensor")
    columns = flat_heads.shape[1] // 3
    norm_first, inverse_first = normalize(stream)
    normed_first = (norm_first * (1.0 + modulation[1]) + modulation[0]).astype(jnp.bfloat16)
    gathered_first = gather_tokens(normed_first)
    projected = (
        jnp.dot(gathered_first, flat_heads, preferred_element_type=jnp.float32) + heads_offset
    ).astype(jnp.bfloat16)
    split_shape = (length, heads_here, HEAD_DIM)
    queries = projected[:, :columns].reshape(split_shape)
    key_rows = projected[:, columns : 2 * columns].reshape(split_shape)
    value_rows = projected[:, 2 * columns :].reshape(split_shape)
    attended, logsum = attend_forward(queries, key_rows, value_rows)
    branch_first = scatter_branch(attended, merge_weight) + merge_bias.astype(jnp.float32)
    stream_mid = stream + modulation[2] * branch_first
    norm_second, inverse_second = normalize(stream_mid)
    normed_second = (norm_second * (1.0 + modulation[4]) + modulation[3]).astype(jnp.bfloat16)
    gathered_second = gather_tokens(normed_second)
    hidden_pre = jnp.dot(
        gathered_second, up_weight, preferred_element_type=jnp.float32
    ) + up_bias.astype(jnp.float32)
    hidden = gelu_tanh(hidden_pre).astype(jnp.bfloat16)
    branch_second = scatter_branch(hidden, down_weight) + down_bias.astype(jnp.float32)
    stream_next = stream_mid + modulation[5] * branch_second
    first_input, second_input = (gathered_first, gathered_second)
    kept = (
        norm_first,
        inverse_first,
        first_input,
        queries,
        key_rows,
        value_rows,
        logsum,
        attended,
        branch_first,
        norm_second,
        inverse_second,
        second_input,
        hidden_pre,
        hidden,
        branch_second,
    )
    return (stream_next, kept)


def backward_layer(grad_stream, modulation, layer_weights, kept):
    (
        flat_heads,
        heads_offset,
        merge_weight,
        merge_bias,
        up_weight,
        up_bias,
        down_weight,
        down_bias,
    ) = layer_weights
    (
        norm_first,
        inverse_first,
        first_input,
        queries,
        key_rows,
        value_rows,
        logsum,
        attended,
        branch_first,
        norm_second,
        inverse_second,
        second_input,
        hidden_pre,
        hidden,
        branch_second,
    ) = kept
    model_width = flat_heads.shape[0]
    columns = flat_heads.shape[1] // 3
    grad_branch_second = (modulation[5] * grad_stream).astype(jnp.bfloat16)
    grad_gate_second = jnp.sum(grad_stream * branch_second, 0)
    grad_down_bias = column_sums(grad_branch_second)
    gathered_grad = gather_grads(grad_branch_second)
    down_grad = outer_rows(hidden, gathered_grad)
    grad_hidden = times_transposed(gathered_grad, down_weight)
    grad_pre = jax.vjp(gelu_tanh, hidden_pre)[1](grad_hidden)[0].astype(jnp.bfloat16)
    up_bias_grad = column_sums(grad_pre)
    up_grad = outer_rows(second_input, grad_pre)
    grad_normed_second = scatter_inputs(grad_pre, up_weight)
    grad_shift_second = jnp.sum(grad_normed_second, 0)
    grad_scale_second = jnp.sum(grad_normed_second * norm_second, 0)
    grad_mid = grad_stream + normalize_back(
        grad_normed_second * (1.0 + modulation[4]), norm_second, inverse_second
    )
    grad_branch_first = (modulation[2] * grad_mid).astype(jnp.bfloat16)
    grad_gate_first = jnp.sum(grad_mid * branch_first, 0)
    grad_merge_bias = column_sums(grad_branch_first)
    gathered_grad = gather_grads(grad_branch_first)
    merge_grad = outer_rows(attended, gathered_grad)
    grad_attended = times_transposed(gathered_grad, merge_weight).astype(jnp.bfloat16)
    grad_queries, grad_keys, grad_values = attend_backward(
        queries, key_rows, value_rows, logsum, grad_attended
    )
    grad_projected = jnp.concatenate([grad_queries, grad_keys, grad_values], 1)
    heads_bias_grad = jnp.stack([column_sums(grad_queries), column_sums(grad_values)])
    heads_grad = outer_rows(first_input, grad_projected).reshape(model_width, 3, columns)
    grad_normed_first = scatter_inputs(grad_projected, flat_heads)
    grad_shift_first = jnp.sum(grad_normed_first, 0)
    grad_scale_first = jnp.sum(grad_normed_first * norm_first, 0)
    grad_before = grad_mid + normalize_back(
        grad_normed_first * (1.0 + modulation[1]), norm_first, inverse_first
    )
    extra = jnp.stack(
        [
            grad_shift_first,
            grad_scale_first,
            grad_gate_first,
            grad_shift_second,
            grad_scale_second,
            grad_gate_second,
            grad_merge_bias,
            grad_down_bias,
        ]
    )
    return (
        grad_before,
        (heads_grad, heads_bias_grad, merge_grad, up_grad, up_bias_grad, down_grad),
        extra,
    )


def per_device(
    latents,
    condition,
    cotangent,
    group_counts,
    heads_weight,
    heads_bias,
    merge_weight,
    merge_bias,
    up_weight,
    up_bias,
    down_weight,
    down_bias,
    modulate_weight,
    modulate_bias,
):
    slot_count = latents.shape[0]
    model_width = latents.shape[2]
    layer_count = heads_weight.shape[0]
    columns = heads_weight.shape[3]
    heads_here = columns // HEAD_DIM
    silu_cond = jax.nn.silu(condition.astype(jnp.float32)).astype(jnp.bfloat16)
    local_mod = jnp.einsum(
        "sd,bdkc->sbkc", silu_cond, modulate_weight, preferred_element_type=jnp.float32
    ) + modulate_bias.astype(jnp.float32)
    modulation_all = lax.all_gather(local_mod, "tensor", axis=3, tiled=True)
    flat_heads = heads_weight.reshape(layer_count, model_width, 3 * columns)
    zero_bias = jnp.zeros((layer_count, columns), heads_bias.dtype)
    heads_offset = (
        jnp.stack([heads_bias[:, 0], zero_bias, heads_bias[:, 1]], 1)
        .reshape(layer_count, 3 * columns)
        .astype(jnp.float32)
    )
    per_layer = [
        (
            flat_heads[0],
            heads_offset[0],
            merge_weight[0],
            merge_bias[0],
            up_weight[0],
            up_bias[0],
            down_weight[0],
            down_bias[0],
        )
    ]
    layer_sums = [None] * layer_count
    modulate_sum = jnp.zeros(modulate_weight.shape, jnp.float32)
    modulate_bias_sum = jnp.zeros(modulate_bias.shape, jnp.float32)
    merge_bias_sum = jnp.zeros((layer_count, columns), jnp.float32)
    down_bias_sum = jnp.zeros((layer_count, columns), jnp.float32)
    output_list, latent_list, condition_list = ([], [], [])
    for slot_index in range(slot_count):
        live_flag = (slot_index < group_counts[0]).astype(jnp.float32)
        stream = latents[slot_index].astype(jnp.float32)
        layer_index = 0
        stream, kept = forward_layer(
            stream, modulation_all[slot_index, layer_index], per_layer[layer_index], heads_here
        )
        saved_layers = [kept]
        output_list.append(stream.astype(jnp.bfloat16))
        grad_stream = cotangent[slot_index].astype(jnp.float32) * live_flag
        extras = [None] * layer_count
        for layer_index in reversed(range(layer_count)):
            grad_stream, layer_grads, extra = backward_layer(
                grad_stream,
                modulation_all[slot_index, layer_index],
                per_layer[layer_index],
                saved_layers[layer_index],
            )
            if layer_sums[layer_index] is None:
                layer_sums[layer_index] = layer_grads
            else:
                layer_sums[layer_index] = jax.tree.map(
                    jnp.add, layer_sums[layer_index], layer_grads
                )
            extras[layer_index] = extra
        latent_list.append(grad_stream)
        shared = lax.psum_scatter(
            jnp.stack(extras).astype(jnp.bfloat16), "tensor", scatter_dimension=2, tiled=True
        ).astype(jnp.float32)
        grad_mod = shared[:, :6].astype(jnp.bfloat16)
        modulate_sum = modulate_sum + jnp.einsum(
            "d,bkc->bdkc", silu_cond[slot_index], grad_mod, preferred_element_type=jnp.float32
        )
        modulate_bias_sum = modulate_bias_sum + grad_mod.astype(jnp.float32)
        merge_bias_sum = merge_bias_sum + shared[:, 6]
        down_bias_sum = down_bias_sum + shared[:, 7]
        cond_partial = jnp.einsum(
            "bdkc,bkc->d", modulate_weight, grad_mod, preferred_element_type=jnp.float32
        )
        cond_total = lax.psum(cond_partial, "tensor")
        silu_grad = jax.vjp(jax.nn.silu, condition[slot_index].astype(jnp.float32))[1](cond_total)[
            0
        ]
        condition_list.append(silu_grad)
    weight_grads = (
        lax.psum_scatter(
            stack_member(layer_sums, 0).astype(jnp.bfloat16), "dp", scatter_dimension=1, tiled=True
        ).astype(jnp.float32),
        lax.psum_scatter(
            stack_member(layer_sums, 2).astype(jnp.bfloat16), "dp", scatter_dimension=2, tiled=True
        ).astype(jnp.float32),
        lax.psum_scatter(
            stack_member(layer_sums, 3).astype(jnp.bfloat16), "dp", scatter_dimension=1, tiled=True
        ).astype(jnp.float32),
        lax.psum_scatter(
            stack_member(layer_sums, 5).astype(jnp.bfloat16), "dp", scatter_dimension=2, tiled=True
        ).astype(jnp.float32),
        lax.psum_scatter(
            modulate_sum.astype(jnp.bfloat16), "dp", scatter_dimension=1, tiled=True
        ).astype(jnp.float32),
    )
    bias_grads = lax.psum(
        (
            stack_member(layer_sums, 1),
            merge_bias_sum,
            stack_member(layer_sums, 4),
            down_bias_sum,
            modulate_bias_sum,
        ),
        "dp",
    )
    block_output = jnp.stack(output_list)
    latent_grad = jnp.stack(latent_list)
    condition_grad = jnp.stack(condition_list)
    return (
        block_output,
        latent_grad,
        condition_grad,
        weight_grads[0],
        bias_grads[0],
        weight_grads[1],
        bias_grads[1],
        weight_grads[2],
        bias_grads[2],
        weight_grads[3],
        bias_grads[3],
        weight_grads[4],
        bias_grads[4],
    )


def solution(mesh):
    in_specs = (
        P("dp", "tensor", None),
        P("dp", None),
        P("dp", "tensor", None),
        P("dp"),
        P(None, None, None, "tensor"),
        P(None, None, "tensor"),
        P(None, "tensor", None),
        P(),
        P(None, None, "tensor"),
        P(None, "tensor"),
        P(None, "tensor", None),
        P(),
        P(None, None, None, "tensor"),
        P(None, None, "tensor"),
    )
    out_specs = (
        P("dp", "tensor", None),
        P("dp", "tensor", None),
        P("dp", None),
        P(None, "dp", None, "tensor"),
        P(None, None, "tensor"),
        P(None, "tensor", "dp"),
        P(None, "tensor"),
        P(None, "dp", "tensor"),
        P(None, "tensor"),
        P(None, "tensor", "dp"),
        P(None, "tensor"),
        P(None, "dp", None, "tensor"),
        P(None, None, "tensor"),
    )
    return jax.shard_map(
        per_device, mesh=mesh, in_specs=in_specs, out_specs=out_specs, check_vma=False
    )
```

profile of v0, /device:TPU:0, one launch (start us, length us, event | category | flops | bytes accessed | tf_op | source)
XLA Modules:
  0.0 1545.8 jit_solution(13240592745490626447)
XLA Ops:
  13.9 17.0 %all-gather = f32[2,6,1152]{1,0,2:T(2,128)S(1)} all-gather(f32[2,6,576]{1,0,2:T(2,128)S(1)} %copy.63), channel_id=2, replica_groups=mesh['dp'=16,'tensor'=2] {'tensor'}, dimensions={2}, use_global_device_ids=true | all-gather | bytes 82944 | tf_op jit(solution)/shard_map/all_gather | solution.py:326
  30.9 51.7 %slice_reduce_fusion.5 = (f32[1152]{0:T(1024)}, f32[1152]{0:T(1024)}, f32[1152]{0:T(1024)}, f32[1152]{0:T(1024)}, f32[1152]{0:T(1024)}, /*index=5*/f32[1152]{0:T...) fusion(f32[2,1,6,1152]{2,0,3,1:T(2,128)S(1)} %bitcast.478), kind=kLoop, calls=%fused_computation.277 | loop fusion | flops 4608 | bytes 110592 | tf_op jit(solution)/shard_map/slice | solution.py:197
  86.8 37.1 %all-gather.10.cloned.1.call-done = bf16[1024,1152]{1,0:T(8,128)(2,1)} async-done(((bf16[512,1152]{1,0:T(8,128)(2,1)}), bf16[1024,1152]{1,0:T(8,128)(2,1)}) %all-gather.10.cloned.1.call-update) | async-done | bytes 2359312 | tf_op jit(solution)/shard_map/all_gather | solution.py:48
  123.9 7.6 add_convert_fusion.2
  140.9 24.4 %while.54 = (s32[]{:T(128)}, bf16[2,512,8,72]{1,3,2,0:T(8,128)(2,1)}, f32[2,8,512]{2,1,0:T(8,128)S(1)}, bf16[2,512,8,72]{1,3,2,0:T(8,128)(2,1)}, bf16[1024,8,72]...) while((s32[]{:T(128)}, bf16[2,512,8,72]{1,3,2,0:T(8,128)(2,1)}, ...), condition=%wide.region_5.6_spmd, body=%wide.region_2.5_spmd.sunk | while | flops 1245999104 | bytes 58721388 | solution.py:108
  173.9 34.2 %reduce-scatter.24.cloned.1.call-done = bf16[512,1152]{1,0:T(8,128)(2,1)} async-done(((bf16[1024,1152]{1,0:T(8,128)(2,1)}), bf16[512,1152]{1,0:T(8,128)(2,1)}) %reduce-scatter.24.cloned.1.call-update) | async-done | bytes 1179664 | tf_op jit(solution)/shard_map/reduce_scatter | solution.py:60
  213.2 11.4 reduce-scatter.28.cloned.1.call-start
  224.6 24.8 %all-gather.14.cloned.1.call-done = bf16[1024,1152]{1,0:T(8,128)(2,1)} async-done(((bf16[512,1152]{1,0:T(8,128)(2,1)}), bf16[1024,1152]{1,0:T(8,128)(2,1)}) %all-gather.14.cloned.1.call-update) | async-done | bytes 2359312 | tf_op jit(solution)/shard_map/all_gather | solution.py:48
  249.4 7.6 add_convert_fusion.1
  266.4 24.4 %while.55 = (s32[]{:T(128)}, bf16[2,512,8,72]{1,3,2,0:T(8,128)(2,1)}, f32[2,8,512]{2,1,0:T(8,128)S(1)}, bf16[2,512,8,72]{1,3,2,0:T(8,128)(2,1)}, bf16[1024,8,72]...) while((s32[]{:T(128)}, bf16[2,512,8,72]{1,3,2,0:T(8,128)(2,1)}, ...), condition=%wide.region_15.16_spmd, body=%wide.region_12.15_spmd.sunk | while | flops 1245999104 | bytes 58721388 | solution.py:108
  299.4 34.2 %reduce-scatter.28.cloned.1.call-done = bf16[512,1152]{1,0:T(8,128)(2,1)} async-done(((bf16[1024,1152]{1,0:T(8,128)(2,1)}), bf16[512,1152]{1,0:T(8,128)(2,1)}) %reduce-scatter.28.cloned.1.call-update) | async-done | bytes 1179664 | tf_op jit(solution)/shard_map/reduce_scatter | solution.py:60
  343.1 31.9 %all-gather.12.cloned.1.call-done = bf16[1024,1152]{1,0:T(8,128)(2,1)} async-done(((bf16[512,1152]{1,0:T(8,128)(2,1)}), bf16[1024,1152]{1,0:T(8,128)(2,1)}) %all-gather.12.cloned.1.call-update) | async-done | bytes 2359312 | tf_op jit(solution)/shard_map/all_gather | solution.py:48
  375.1 11.4 fusion.114
  386.5 26.7 %all-gather.18.cloned.1.call-done = bf16[1024,1152]{1,0:T(8,128)(2,1)} async-done(((bf16[512,1152]{1,0:T(8,128)(2,1)}), bf16[1024,1152]{1,0:T(8,128)(2,1)}) %all-gather.18.cloned.1.call-update) | async-done | bytes 2359312 | tf_op jit(solution)/shard_map/all_gather | solution.py:52
  413.1 15.4 convert_reduce_fusion.1
  430.7 10.0 fusion.116
  441.2 13.4 fusion.122
  455.4 20.2 %reduce-scatter.32.cloned.1.call-done = bf16[512,1152]{1,0:T(8,128)(2,1)} async-done(((bf16[1024,1152]{1,0:T(8,128)(2,1)}), bf16[512,1152]{1,0:T(8,128)(2,1)}) %reduce-scatter.32.cloned.1.call-update) | async-done | bytes 1179664 | tf_op jit(solution)/shard_map/reduce_scatter | solution.py:75
  475.6 37.1 %reduce-scatter.26.cloned.1.call-done = bf16[512,1152]{1,0:T(8,128)(2,1)} async-done(((bf16[1024,1152]{1,0:T(8,128)(2,1)}), bf16[512,1152]{1,0:T(8,128)(2,1)}) %reduce-scatter.26.cloned.1.call-update) | async-done | bytes 1179664 | tf_op jit(solution)/shard_map/reduce_scatter | solution.py:60
  527.6 29.1 %all-gather.16.cloned.1.call-done = bf16[1024,1152]{1,0:T(8,128)(2,1)} async-done(((bf16[512,1152]{1,0:T(8,128)(2,1)}), bf16[1024,1152]{1,0:T(8,128)(2,1)}) %all-gather.16.cloned.1.call-update) | async-done | bytes 2359312 | tf_op jit(solution)/shard_map/all_gather | solution.py:48
  556.7 11.5 fusion.112
  568.2 26.6 %all-gather.22.cloned.1.call-done = bf16[1024,1152]{1,0:T(8,128)(2,1)} async-done(((bf16[512,1152]{1,0:T(8,128)(2,1)}), bf16[1024,1152]{1,0:T(8,128)(2,1)}) %all-gather.22.cloned.1.call-update) | async-done | bytes 2359312 | tf_op jit(solution)/shard_map/all_gather | solution.py:52
  594.8 15.4 convert_reduce_fusion
  612.4 10.0 fusion.119
  622.7 9.7 all-gather.20.cloned.1.call-done
  641.4 13.4 fusion.125
  656.2 113.3 %while.56 = (s32[]{:T(128)}, f32[1024,8,72]{0,2,1:T(8,128)}, f32[1024,8,72]{0,2,1:T(8,128)}, bf16[2,512,8,72]{1,3,2,0:T(8,128)(2,1)}, bf16[2,512,8,72]{1,3,2,0:T...) while((s32[]{:T(128)}, f32[1024,8,72]{0,2,1:T(8,128)}, ...), condition=%wide.region_25.26_spmd.clone, body=%wide.region_23.25_spmd.clone.sunk | while | flops 3073765376 | bytes 201640240 | solution.py:154
  656.3 9.4 fusion.332
  665.6 11.4 multiply_reduce_fusion.14
  677.0 16.0 %multiply_convert_fusion.14 = bf16[8,512,1024]{2,1,0:T(8,128)(2,1)} fusion(f32[8,512,1024]{2,1,0:T(8,128)} %get-tuple-element.763, f32[8,512,1024]{2,1,0:T(8,128)} %fusion.332, f32[8,512]{1,0:T(8,128)S(1)} %get-tuple-element.764, f32[8,512]{1,0:T(8,128)S(1)} %dynamic-slice_bitcast_fusion.4), kind=kLoop, calls=%fused_computation.28.clone.1 | loop fusion | flops 20971520 | bytes 41975808 | tf_op jit(solution)/shard_map/while/body/eval_jaxpr/convert_element_type | solution.py:138
  699.8 7.3 fusion.333
  712.6 9.3 fusion.332
  722.0 11.3 multiply_reduce_fusion.14
  733.3 15.3 multiply_convert_fusion.14
  748.6 7.4 bitcast_add_fusion.8
  756.0 7.2 fusion.333
  783.5 35.2 %reduce-scatter.34.cloned.1.call-done = bf16[512,1152]{1,0:T(8,128)(2,1)} async-done(((bf16[1024,1152]{1,0:T(8,128)(2,1)}), bf16[512,1152]{1,0:T(8,128)(2,1)}) %reduce-scatter.34.cloned.1.call-update) | async-done | bytes 1179664 | tf_op jit(solution)/shard_map/reduce_scatter | solution.py:75
  818.8 7.0 fusion.174
  829.7 36.2 %all-gather.24.cloned.1.call-done = bf16[1024,1152]{1,0:T(8,128)(2,1)} async-done(((bf16[512,1152]{1,0:T(8,128)(2,1)}), bf16[1024,1152]{1,0:T(8,128)(2,1)}) %all-gather.24.cloned.1.call-update) | async-done | bytes 2359312 | tf_op jit(solution)/shard_map/all_gather | solution.py:52
  874.9 112.2 %while.57 = (s32[]{:T(128)}, f32[1024,8,72]{0,2,1:T(8,128)}, f32[1024,8,72]{0,2,1:T(8,128)}, bf16[2,512,8,72]{1,3,2,0:T(8,128)(2,1)}, bf16[2,512,8,72]{1,3,2,0:T...) while((s32[]{:T(128)}, f32[1024,8,72]{0,2,1:T(8,128)}, ...), condition=%wide.region_34.35_spmd.clone, body=%wide.region_32.34_spmd.clone.sunk | while | flops 3073765376 | bytes 201640240 | solution.py:154
  874.9 9.3 fusion.343
  884.2 11.3 multiply_reduce_fusion.15
  895.6 15.3 multiply_convert_fusion.15
  917.7 7.1 fusion.344
  930.3 9.3 fusion.343
  939.6 11.3 multiply_reduce_fusion.15
  951.0 15.3 multiply_convert_fusion.15
  966.3 7.5 bitcast_add_fusion.10
  973.8 7.1 fusion.344
  1000.8 13.4 fusion.229
  1025.2 9.7 reduce-scatter.38.cloned.1.call-done
  1052.0 13.9 fusion.72
  1065.9 24.0 %copy.87 = bf16[1,2304,1152]{1,0,2:T(2,128)(2,1)} copy(bf16[1,2304,1152]{2,1,0:T(8,128)(2,1)} %fusion.72) | data formatting | bytes 10616832
  1089.9 7.2 copy.103
  1097.3 8.9 fusion.242
  1106.3 10.0 fusion.73
  1117.6 7.4 fusion.186
  1125.0 9.5 fusion.95
  1134.5 11.3 copy.83
  1145.8 12.3 reshape.752
  1196.1 63.3 %reduce-scatter.40.cloned.1.call-done = bf16[1,72,2304]{2,1,0:T(8,128)(2,1)} async-done(((bf16[1,1152,2304]{2,1,0:T(8,128)(2,1)}), bf16[1,72,2304]{2,1,0:T(8,128)(2,1)}) %reduce-scatter.40.cloned.1.call-update) | async-done | bytes 331792 | tf_op jit(solution)/shard_map/reduce_scatter | solution.py:403
  1270.8 8.0 all-reduce.3
  1278.9 59.6 %all-reduce.2 = (f32[1,2,576]{2,1,0:T(2,128)}, f32[1,576]{1,0:T(1,128)}, f32[1,2304]{1,0:T(1,128)}, f32[1,576]{1,0:T(1,128)}, f32[1,6,576]{2,0,1:T(1,128)}) all-reduce(f32[1,2,576]{2,1,0:T(2,128)S(1)} %maximum_add_fusion, f32[1,576]{1,0:T(1,128)S(1)} %get-tuple-element.567, ...), channel_id=1, replica_groups=mesh['dp'=16,'tensor'=2] {'dp'}, use_global_device_ids=true, to_apply=%region_63.64 | all-reduce | flops 8064 | bytes 64512 | tf_op jit(solution)/shard_map/psum | solution.py:413
  1341.2 193.4 %all-reduce.7.cloned.1.call-done = (bf16[1,576,1152]{2,1,0:T(8,128)(2,1)}, bf16[1,1152,6,576]{3,1,2,0:T(8,128)(2,1)}) async-done(((bf16[1,576,1152]{2,1,0:T(8,128)(2,1)}, bf16[1,1152,6,576]{3,1,2,0:T(8,128)(2,1)}), (bf16[1,576,1152]{2,1,0:T(8,128)(2,1)}, bf16[1,1152,6,576]{3,1,2,0:T(8,128)(2,1)})) %all-reduce.7.cloned.1.call-update) | async-done | bytes 9289744
  (509 shorter events, 301.0 us)
Async XLA Ops:
  7.2 162.4 %copy-start = (bf16[1,576,1152]{2,1,0:T(8,128)(2,1)S(1)}, bf16[1,576,1152]{2,1,0:T(8,128)(2,1)}, u32[]{:S(2)}) copy-start(bf16[1,576,1152]{2,1,0:T(8,128)(2,1)} %param.28) | copy-start | bytes 3981316
  7.2 116.7 %all-gather.10.cloned.1.call-start = ((), (), s32[]{:S(2)}) async-start(), calls=%async_computation.13 | async-start | bytes 3538944 | tf_op jit(solution)/shard_map/all_gather | solution.py:48
  30.9 51.7 %copy-start.5 = (bf16[2,512,1152]{2,1,0:T(8,128)(2,1)S(1)}, bf16[2,512,1152]{2,1,0:T(8,128)(2,1)}, u32[]{:S(2)}) copy-start(bf16[2,512,1152]{2,1,0:T(8,128)(2,1)} %param.22) | copy-start | bytes 7077892
  86.2 121.9 %reduce-scatter.24.cloned.1.call-start = ((), (), s32[]{:S(2)}) async-start(), calls=%async_computation.14 | async-start | bytes 3538944 | tf_op jit(solution)/shard_map/reduce_scatter | solution.py:60
  86.7 37.1 %copy-start.109 = (f32[1728]{0:T(1024)}, f32[1728]{0:T(1024)S(1)}, u32[]{:S(2)}) copy-start(f32[1728]{0:T(1024)S(1)} %reshape.730) | copy-start | bytes 20740
  173.2 34.9 %copy-start.54 = (f32[1152]{0:T(1024)S(1)}, f32[1152]{0:T(1024)}, u32[]{:S(2)}) copy-start(f32[1152]{0:T(1024)} %get-tuple-element.453) | copy-start | bytes 13828
  173.2 38.4 %copy-start.56 = (f32[1152]{0:T(1024)S(1)}, f32[1152]{0:T(1024)}, u32[]{:S(2)}) copy-start(f32[1152]{0:T(1024)} %get-tuple-element.447) | copy-start | bytes 13828
  173.2 38.4 %copy-start.80 = (f32[1152]{0:T(1024)S(1)}, f32[1152]{0:T(1024)}, u32[]{:S(2)}) copy-start(f32[1152]{0:T(1024)} %get-tuple-element.446) | copy-start | bytes 13828
  173.2 76.2 %all-gather.14.cloned.1.call-start = ((), (), s32[]{:S(2)}) async-start(), calls=%async_computation.17 | async-start | bytes 3538944 | tf_op jit(solution)/shard_map/all_gather | solution.py:48
  173.9 39.3 %copy-start.44 = (f32[1152]{0:T(1024)}, f32[1152]{0:T(1024)S(1)}, u32[]{:S(2)}) copy-start(f32[1152]{0:T(1024)S(1)} %convert_reduce_fusion.12) | copy-start | bytes 13828
  173.9 39.3 %copy-start.76 = (f32[512]{0:T(512)}, f32[512]{0:T(512)S(1)}, u32[]{:S(2)}) copy-start(f32[512]{0:T(512)S(1)} %broadcast_multiply_fusion.9) | copy-start | bytes 6148
  211.6 37.8 %copy-start.110 = (f32[1728]{0:T(1024)S(1)}, f32[1728]{0:T(1024)}, u32[]{:S(2)}) copy-start(f32[1728]{0:T(1024)} %copy-done.109) | copy-start | bytes 20740
  211.6 37.8 %copy-start.86 = (f32[512]{0:T(512)}, f32[512]{0:T(512)S(1)}, u32[]{:S(2)}) copy-start(f32[512]{0:T(512)S(1)} %add_rsqrt_fusion.1) | copy-start | bytes 6148
  213.2 120.4 %reduce-scatter.28.cloned.1.call-start = ((), (), s32[]{:S(2)}) async-start(), calls=%async_computation.18 | async-start | bytes 3538944 | tf_op jit(solution)/shard_map/reduce_scatter | solution.py:60
  298.7 34.9 %copy-start.19 = (bf16[512,1152]{1,0:T(8,128)(2,1)S(1)}, bf16[512,1152]{1,0:T(8,128)(2,1)}, u32[]{:S(2)}) copy-start(bf16[512,1152]{1,0:T(8,128)(2,1)} %reduce-scatter.24.cloned.1.call-done) | copy-start | bytes 3538948
  298.7 34.9 %copy-start.45 = (f32[1152]{0:T(1024)S(1)}, f32[1152]{0:T(1024)}, u32[]{:S(2)}) copy-start(f32[1152]{0:T(1024)} %copy-done.44) | copy-start | bytes 13828
  298.7 34.9 %copy-start.52 = (f32[1152]{0:T(1024)S(1)}, f32[1152]{0:T(1024)}, u32[]{:S(2)}) copy-start(f32[1152]{0:T(1024)} %get-tuple-element.448) | copy-start | bytes 13828
  298.7 34.9 %copy-start.55 = (f32[1152]{0:T(1024)S(1)}, f32[1152]{0:T(1024)}, u32[]{:S(2)}) copy-start(f32[1152]{0:T(1024)} %get-tuple-element.453) | copy-start | bytes 13828
  298.7 76.3 %all-gather.12.cloned.1.call-start = ((), (), s32[]{:S(2)}) async-start(), calls=%async_computation.15 | async-start | bytes 3538944 | tf_op jit(solution)/shard_map/all_gather | solution.py:48
  338.8 74.3 %all-gather.18.cloned.1.call-start = ((), (), s32[]{:S(2)}) async-start(), calls=%async_computation.21 | async-start | bytes 3538944 | tf_op jit(solution)/shard_map/all_gather | solution.py:52
  343.0 132.6 %reduce-scatter.32.cloned.1.call-start = ((), (), s32[]{:S(2)}) async-start(), calls=%async_computation.22 | async-start | bytes 3538944 | tf_op jit(solution)/shard_map/reduce_scatter | solution.py:75
  343.1 298.3 %copy-start.101 = (f32[2304]{0:T(1024)}, f32[2304]{0:T(1024)S(1)}, u32[]{:S(2)}) copy-start(f32[2304]{0:T(1024)S(1)} %convert_reduce_fusion.8) | copy-start | bytes 27652
  440.8 71.9 %reduce-scatter.26.cloned.1.call-start = ((), (), s32[]{:S(2)}) async-start(), calls=%async_computation.16 | async-start | bytes 3538944 | tf_op jit(solution)/shard_map/reduce_scatter | solution.py:60
  454.7 102.0 %all-gather.16.cloned.1.call-start = ((), (), s32[]{:S(2)}) async-start(), calls=%async_computation.19 | async-start | bytes 3538944 | tf_op jit(solution)/shard_map/all_gather | solution.py:48
  455.4 63.2 %copy-start.64 = (f32[1152]{0:T(1024)}, f32[1152]{0:T(1024)S(1)}, u32[]{:S(2)}) copy-start(f32[1152]{0:T(1024)S(1)} %convert_reduce_fusion.11) | copy-start | bytes 13828
  455.4 63.2 %copy-start.71 = (f32[512]{0:T(512)}, f32[512]{0:T(512)S(1)}, u32[]{:S(2)}) copy-start(f32[512]{0:T(512)S(1)} %broadcast_multiply_fusion.8) | copy-start | bytes 6148
  455.4 63.2 %copy-start.61 = (f32[1152]{0:T(1024)S(1)}, f32[1152]{0:T(1024)}, u32[]{:S(2)}) copy-start(f32[1152]{0:T(1024)} %get-tuple-element.444) | copy-start | bytes 13828
  455.4 63.2 %copy-start.78 = (f32[1152]{0:T(1024)S(1)}, f32[1152]{0:T(1024)}, u32[]{:S(2)}) copy-start(f32[1152]{0:T(1024)} %get-tuple-element.443) | copy-start | bytes 13828
  520.5 74.3 %all-gather.22.cloned.1.call-start = ((), (), s32[]{:S(2)}) async-start(), calls=%async_computation.25 | async-start | bytes 3538944 | tf_op jit(solution)/shard_map/all_gather | solution.py:52
  526.6 105.8 %all-gather.20.cloned.1.call-start = ((), (), s32[]{:S(2)}) async-start(), calls=%async_computation.23 | async-start | bytes 3538944 | tf_op jit(solution)/shard_map/all_gather | solution.py:52
  527.4 256.1 %reduce-scatter.36.cloned.1.call-start = ((), (), s32[]{:S(2)}) async-start(), calls=%async_computation.26 | async-start | bytes 3538944 | tf_op jit(solution)/shard_map/reduce_scatter | solution.py:75
  622.5 161.0 %reduce-scatter.30.cloned.1.call-start = ((), (), s32[]{:S(2)}) async-start(), calls=%async_computation.20 | async-start | bytes 3538944 | tf_op jit(solution)/shard_map/reduce_scatter | solution.py:60
  654.8 163.9 %reduce-scatter.34.cloned.1.call-start = ((), (), s32[]{:S(2)}) async-start(), calls=%async_computation.24 | async-start | bytes 3538944 | tf_op jit(solution)/shard_map/reduce_scatter | solution.py:75
  748.6 14.6 slice-start.2
  783.3 35.5 %copy-start.20 = (bf16[512,1152]{1,0:T(8,128)(2,1)S(1)}, bf16[512,1152]{1,0:T(8,128)(2,1)}, u32[]{:S(2)}) copy-start(bf16[512,1152]{1,0:T(8,128)(2,1)} %reduce-scatter.24.cloned.1.call-done) | copy-start | bytes 3538948
  783.3 35.5 %copy-start.46 = (f32[1152]{0:T(1024)S(1)}, f32[1152]{0:T(1024)}, u32[]{:S(2)}) copy-start(f32[1152]{0:T(1024)} %copy-done.44) | copy-start | bytes 13828
  783.3 35.5 %copy-start.53 = (f32[1152]{0:T(1024)S(1)}, f32[1152]{0:T(1024)}, u32[]{:S(2)}) copy-start(f32[1152]{0:T(1024)} %get-tuple-element.448) | copy-start | bytes 13828
  783.3 35.5 %copy-start.59 = (f32[1152]{0:T(1024)S(1)}, f32[1152]{0:T(1024)}, u32[]{:S(2)}) copy-start(f32[1152]{0:T(1024)} %copy-done.58) | copy-start | bytes 13828
  783.3 35.5 %copy-start.62 = (f32[1152]{0:T(1024)S(1)}, f32[1152]{0:T(1024)}, u32[]{:S(2)}) copy-start(f32[1152]{0:T(1024)} %get-tuple-element.444) | copy-start | bytes 13828
  783.3 35.5 %copy-start.65 = (f32[1152]{0:T(1024)S(1)}, f32[1152]{0:T(1024)}, u32[]{:S(2)}) copy-start(f32[1152]{0:T(1024)} %copy-done.64) | copy-start | bytes 13828
  783.3 35.5 %copy-start.68 = (f32[1152]{0:T(1024)S(1)}, f32[1152]{0:T(1024)}, u32[]{:S(2)}) copy-start(f32[1152]{0:T(1024)} %get-tuple-element.445) | copy-start | bytes 13828
  783.3 35.5 %copy-start.72 = (f32[512]{0:T(512)S(1)}, f32[512]{0:T(512)}, u32[]{:S(2)}) copy-start(f32[512]{0:T(512)} %copy-done.71) | copy-start | bytes 6148
  783.3 35.5 %copy-start.74 = (f32[512]{0:T(512)S(1)}, f32[512]{0:T(512)}, u32[]{:S(2)}) copy-start(f32[512]{0:T(512)} %copy-done.73) | copy-start | bytes 6148
  783.3 35.5 %copy-start.82 = (f32[512]{0:T(512)S(1)}, f32[512]{0:T(512)}, u32[]{:S(2)}) copy-start(f32[512]{0:T(512)} %copy-done.81) | copy-start | bytes 6148
  783.3 35.5 %copy-start.84 = (f32[512]{0:T(512)S(1)}, f32[512]{0:T(512)}, u32[]{:S(2)}) copy-start(f32[512]{0:T(512)} %copy-done.83) | copy-start | bytes 6148
  783.4 82.5 %all-gather.24.cloned.1.call-start = ((), (), s32[]{:S(2)}) async-start(), calls=%async_computation.27 | async-start | bytes 3538944 | tf_op jit(solution)/shard_map/all_gather | solution.py:52
  829.6 205.4 %reduce-scatter.38.cloned.1.call-start = ((), (), s32[]{:S(2)}) async-start(), calls=%async_computation.28 | async-start | bytes 3538944 | tf_op jit(solution)/shard_map/reduce_scatter | solution.py:75
  966.3 14.6 slice-start.4
  966.3 14.6 slice-start.5
  966.3 14.6 slice-start.6
  1000.2 164.2 %reduce-scatter.42.cloned.1.call-start = ((), (), s32[]{:S(2)}) async-start(), calls=%async_computation.30 | async-start | bytes 442368
  1020.7 15.8 %copy-start.57 = (f32[1152]{0:T(1024)S(1)}, f32[1152]{0:T(1024)}, u32[]{:S(2)}) copy-start(f32[1152]{0:T(1024)} %get-tuple-element.447) | copy-start | bytes 13828
  1020.7 15.8 %copy-start.77 = (f32[512]{0:T(512)S(1)}, f32[512]{0:T(512)}, u32[]{:S(2)}) copy-start(f32[512]{0:T(512)} %copy-done.76) | copy-start | bytes 6148
  1020.7 15.8 %copy-start.87 = (f32[512]{0:T(512)S(1)}, f32[512]{0:T(512)}, u32[]{:S(2)}) copy-start(f32[512]{0:T(512)} %copy-done.86) | copy-start | bytes 6148
  1024.8 14.6 copy-start.23
  1024.8 14.6 copy-start.47
  1024.8 14.7 copy-start.60
  1024.8 14.7 copy-start.75
  1024.8 14.7 copy-start.85
  1024.8 147.7 %reduce-scatter.44.cloned.1.call-start = ((), (), s32[]{:S(2)}) async-start(), calls=%async_computation.31 | async-start | bytes 442368
  1051.9 141.1 %reduce-scatter.48.cloned.1.call-start = ((), (), s32[]{:S(2)}) async-start(), calls=%async_computation.33 | async-start | bytes 5640192
  1097.1 162.3 %reduce-scatter.40.cloned.1.call-start = ((), (), s32[]{:S(2)}) async-start(), calls=%async_computation.29 | async-start | bytes 5640192 | tf_op jit(solution)/shard_map/reduce_scatter | solution.py:403
  1116.3 222.9 %reduce-scatter.46.cloned.1.call-start = ((), (), s32[]{:S(2)}) async-start(), calls=%async_computation.32 | async-start | bytes 4386816
  1158.1 376.4 %all-reduce.7.cloned.1.call-start = ((), (), s32[]{:S(2)}) async-start(), calls=%async_computation.34 | async-start | bytes 20348928
  (100 other events, 547.6 us)
Sparse Core Ops, SparseCore 0:
  86.3 37.5 all-gather.9
  173.3 34.7 reduce-scatter.23
  213.3 36.0 all-gather.13
  298.9 34.6 reduce-scatter.27
  338.9 36.0 all-gather.11
  377.0 36.0 all-gather.17
  440.9 34.7 reduce-scatter.31
  478.0 34.6 reduce-scatter.25
  520.6 36.0 all-gather.15
  558.7 36.0 all-gather.21
  596.3 36.0 all-gather.19
  634.5 34.7 reduce-scatter.35
  671.6 34.6 reduce-scatter.29
  783.5 35.1 reduce-scatter.33
  829.7 36.0 all-gather.23
  1000.2 34.6 reduce-scatter.37
  1037.6 12.0 reduce-scatter.41
  1052.4 12.0 reduce-scatter.43
  1097.2 79.5 reduce-scatter.47
  1180.6 78.7 reduce-scatter.39
  1263.3 71.5 reduce-scatter.45
  1338.7 195.7 all-reduce.6
where the time goes:
time: 1560 us; the launch traced here: 1550 us
  waiting for transfers between devices  651 us (42%)
  matrix products  430 us (28%)
  other arithmetic  206 us (13%)
  local copies, waits for them, and re-layouts  141 us (9%)
  blocking collectives  84.7 us (5%)
  between operations  17.7 us (1%)
    unnamed x27, waiting for transfers between devices  194 us
    all_gather x4, waiting for transfers between devices, gather_tokens(): return lax.all_gather(values, 'tensor', axis=0, tiled=True)  123 us
    reduce_scatter x4, waiting for transfers between devices, scatter_branch(): lax.psum_scatter(partial_rows(jnp.int32(0), operand.shape[0] // lax.axis_...  105 us
    unnamed x266, local copies, waits for them, and re-layouts  103 us
    all_gather x4, waiting for transfers between devices, gather_grads(): return lax.all_gather(values, 'tensor', axis=0, tiled=True)  99.1 us
    dot_general x8, matrix products, outer_rows(): lax.dot_general(operand, other, (((0,), (0,)), ((), ())), preferred_eleme...  73.7 us
    dot_general x8, matrix products, times_transposed(): lax.dot_general(operand, weight, (((1,), (1,)), ((), ())), preferred_elem...  71.4 us
    reduce_scatter x4, waiting for transfers between devices, scatter_inputs(): lax.psum_scatter(partial_rows(jnp.int32(0), operand.shape[0] // lax.axis_...  65.2 us
  transfers between devices with their start and end apart: 22, of which 16 were waited for; matrix products, arithmetic and copies ran while one was open for 27% of the time, Pallas kernels for 0%

commit v1 on v0

--- a/solution.py
+++ b/solution.py
@@ -1,6 +1,11 @@
+import functools
+import math
+
 import jax
 import jax.numpy as jnp
 from jax import lax
+from jax.experimental import pallas as pl
+from jax.experimental.pallas import tpu as pltpu
 from jax.sharding import PartitionSpec as P
 
 HEAD_DIM = 72
@@ -440,6 +445,476 @@
     )
 
 
+F32 = jnp.float32
+BF16 = jnp.bfloat16
+SCORE_SCALE = HEAD_DIM ** (-0.5)
+SCORE_LOG2 = SCORE_SCALE * math.log2(math.e)
+VMEM_BYTES = 60 * 2**20
+
+
+def dot_dims(left, right, left_dim, right_dim):
+    return lax.dot_general(
+        left, right, (((left_dim,), (right_dim,)), ((), ())), preferred_element_type=F32
+    )
+
+
+def head_slice(part, head, width):
+    return slice(part * width + head * HEAD_DIM, part * width + (head + 1) * HEAD_DIM)
+
+
+def attend_kernel(heads, qkv_ref, out_ref, logsum_ref):
+    width = heads * HEAD_DIM
+    rows_here = out_ref.shape[0]
+    rows = pl.ds(pl.multiple_of(pl.program_id(0) * rows_here, rows_here), rows_here)
+    for head in range(heads):
+        queries = qkv_ref[rows, head_slice(0, head, width)]
+        scores = dot_dims(qkv_ref[:, head_slice(1, head, width)], queries, 1, 1)
+        top = jnp.max(scores, 0, keepdims=True)
+        exponent = jnp.exp2((scores - top) * SCORE_LOG2)
+        total = jnp.sum(exponent, 0, keepdims=True)
+        mixed = dot_dims(qkv_ref[:, head_slice(2, head, width)], exponent.astype(BF16), 0, 0)
+        out_ref[:, head_slice(0, head, width)] = (mixed / total).T.astype(BF16)
+        logsum_ref[head : head + 1, :] = top * SCORE_LOG2 + jnp.log2(total)
+
+
+def attend(qkv, query_rows=512):
+    tokens, width = qkv.shape[0], qkv.shape[1] // 3
+    heads = width // HEAD_DIM
+    return pl.pallas_call(
+        functools.partial(attend_kernel, heads),
+        grid=(tokens // query_rows,),
+        in_specs=[pl.BlockSpec((tokens, 3 * width), lambda i: (0, 0))],
+        out_specs=[
+            pl.BlockSpec((query_rows, width), lambda i: (i, 0)),
+            pl.BlockSpec((heads, query_rows), lambda i: (0, i)),
+        ],
+        out_shape=[
+            jax.ShapeDtypeStruct((tokens, width), BF16),
+            jax.ShapeDtypeStruct((heads, tokens), F32),
+        ],
+        compiler_params=pltpu.CompilerParams(vmem_limit_bytes=VMEM_BYTES),
+        cost_estimate=pl.CostEstimate(
+            flops=4 * heads * tokens * tokens * 256, bytes_accessed=8 * tokens * width,
+            transcendentals=heads * tokens * tokens,
+        ),
+    )(qkv)
+
+
+def attend_back_kernel(
+    heads, key_rows, steps,
+    qkv_ref, out_ref, grad_ref, logsum_ref, grads_ref, pairs_ref, dot_ref, query_ref,
+):
+    step = pl.program_id(0)
+    width = heads * HEAD_DIM
+    half = heads // 2
+    rows = pl.ds(pl.multiple_of(step * key_rows, key_rows), key_rows)
+
+    @pl.when(step == 0)
+    def _():
+        owner = lax.broadcasted_iota(jnp.int32, (heads, width), 1)
+        first = lax.broadcasted_iota(jnp.int32, (heads, width), 0) * HEAD_DIM
+        member = ((owner >= first) & (owner < first + HEAD_DIM)).astype(BF16)
+        product = grad_ref[...].astype(F32) * out_ref[...].astype(F32)
+        high = product.astype(BF16)
+        low = (product - high.astype(F32)).astype(BF16)
+        dot_ref[...] = dot_dims(member, high, 1, 1) + dot_dims(member, low, 1, 1)
+        query_ref[...] = jnp.zeros_like(query_ref)
+
+    def store(part, head, rows, value):
+        grads_ref[rows, head_slice(part, head, width)] = value
+        pairs_ref[head // half, rows, head_slice(part, head % half, half * HEAD_DIM)] = value
+
+    for head in range(heads):
+        queries = qkv_ref[:, head_slice(0, head, width)]
+        keys = qkv_ref[rows, head_slice(1, head, width)]
+        grad = grad_ref[:, head_slice(0, head, width)]
+        scores = dot_dims(keys, queries, 1, 1)
+        probs = jnp.exp2(scores * SCORE_LOG2 - logsum_ref[head : head + 1, :])
+        grad_probs = dot_dims(qkv_ref[rows, head_slice(2, head, width)], grad, 1, 1)
+        grad_scores = (probs * (grad_probs - dot_ref[head : head + 1, :])).astype(BF16)
+        grad_values = jnp.dot(probs.astype(BF16), grad, preferred_element_type=F32)
+        store(2, head, rows, grad_values.astype(BF16))
+        grad_keys = jnp.dot(grad_scores, queries, preferred_element_type=F32) * SCORE_SCALE
+        store(1, head, rows, grad_keys.astype(BF16))
+        query_ref[head] += dot_dims(keys, grad_scores, 0, 0)
+
+    @pl.when(step == steps - 1)
+    def _():
+        for head in range(heads):
+            store(0, head, slice(None), (query_ref[head] * SCORE_SCALE).T.astype(BF16))
+
+
+def attend_back(qkv, attended, grad_attended, logsum, key_rows=512):
+    tokens, width = attended.shape
+    heads = width // HEAD_DIM
+    steps = tokens // key_rows
+    whole = lambda *shape: pl.BlockSpec(shape, lambda i: (0,) * len(shape))
+    return pl.pallas_call(
+        functools.partial(attend_back_kernel, heads, key_rows, steps),
+        grid=(steps,),
+        in_specs=[
+            whole(tokens, 3 * width), whole(tokens, width), whole(tokens, width),
+            whole(heads, tokens),
+        ],
+        out_specs=[whole(tokens, 3 * width), whole(2, tokens, 3 * width // 2)],
+        out_shape=[
+            jax.ShapeDtypeStruct((tokens, 3 * width), BF16),
+            jax.ShapeDtypeStruct((2, tokens, 3 * width // 2), BF16),
+        ],
+        scratch_shapes=[
+            pltpu.VMEM((heads, tokens), F32),
+            pltpu.VMEM((heads, HEAD_DIM, tokens), F32),
+        ],
+        compiler_params=pltpu.CompilerParams(vmem_limit_bytes=VMEM_BYTES),
+        cost_estimate=pl.CostEstimate(
+            flops=10 * heads * tokens * tokens * 256, bytes_accessed=22 * tokens * width,
+            transcendentals=heads * tokens * tokens,
+        ),
+    )(qkv, attended, grad_attended, logsum)
+
+
+GELU_OUTER = math.sqrt(2 / math.pi)
+GELU_CUBIC = 0.044715
+
+
+def gelu_and_slope(values):
+    square = values * values
+    tanh = jnp.tanh(values * (GELU_OUTER + GELU_OUTER * GELU_CUBIC * square))
+    half = 0.5 + 0.5 * tanh
+    inner = 0.5 * GELU_OUTER + 1.5 * GELU_OUTER * GELU_CUBIC * square
+    return values * half, half + values * (1.0 - tanh * tanh) * inner
+
+
+def feed_kernel(
+    token_rows, carried, normed_ref, grad_ref, up_ref, bias_ref, down_ref, *refs
+):
+    if carried:
+        branch_in, normed_in = refs[:2]
+        refs = refs[2:]
+    branch_ref, back_ref, hidden_ref, pre_ref, bias_grad_ref = refs
+    chunk = pl.program_id(0)
+    bias_grad_ref[...] = jnp.zeros_like(bias_grad_ref)
+
+    def block(index, _):
+        rows = pl.ds(pl.multiple_of(index * token_rows, token_rows), token_rows)
+        pre = jnp.dot(normed_ref[rows, :], up_ref[...], preferred_element_type=F32)
+        grad_hidden = dot_dims(grad_ref[rows, :], down_ref[...], 1, 1)
+        hidden, slope = gelu_and_slope(pre + bias_ref[...])
+        hidden = hidden.astype(BF16)
+        grad_pre = (grad_hidden * slope).astype(BF16)
+        bias_grad_ref[...] += jnp.sum(grad_pre.astype(F32), 0, keepdims=True)
+        hidden_ref[0, rows, :] = hidden
+        pre_ref[0, rows, :] = grad_pre
+        branch = jnp.dot(hidden, down_ref[...], preferred_element_type=F32)
+        back = dot_dims(grad_pre, up_ref[...], 1, 1)
+
+        @pl.when(chunk == 0)
+        def _():
+            branch_ref[rows, :] = branch + branch_in[rows, :] if carried else branch
+            back_ref[rows, :] = back + normed_in[rows, :] if carried else back
+
+        @pl.when(chunk > 0)
+        def _():
+            branch_ref[rows, :] += branch
+            back_ref[rows, :] += back
+
+        return 0
+
+    lax.fori_loop(0, normed_ref.shape[0] // token_rows, block, 0)
+
+
+def feed(normed, grad, up, bias, down, carried=(), token_rows=256):
+    tokens, model_width = normed.shape
+    hidden_here = up.shape[1]
+    width = hidden_here // 2
+    whole = lambda: pl.BlockSpec((tokens, model_width), lambda j: (0, 0))
+    pair = lambda: pl.BlockSpec((1, tokens, width), lambda j: (j, 0, 0))
+    return pl.pallas_call(
+        functools.partial(feed_kernel, token_rows, len(carried) > 0),
+        grid=(2,),
+        in_specs=[
+            whole(), whole(),
+            pl.BlockSpec((model_width, width), lambda j: (0, j)),
+            pl.BlockSpec((1, width), lambda j: (0, j)),
+            pl.BlockSpec((width, model_width), lambda j: (j, 0)),
+        ] + [whole() for _ in carried],
+        out_specs=[
+            whole(), whole(), pair(), pair(), pl.BlockSpec((1, width), lambda j: (0, j)),
+        ],
+        out_shape=[
+            jax.ShapeDtypeStruct((tokens, model_width), F32),
+            jax.ShapeDtypeStruct((tokens, model_width), F32),
+            jax.ShapeDtypeStruct((2, tokens, width), BF16),
+            jax.ShapeDtypeStruct((2, tokens, width), BF16),
+            jax.ShapeDtypeStruct((1, hidden_here), F32),
+        ],
+        compiler_params=pltpu.CompilerParams(vmem_limit_bytes=VMEM_BYTES),
+        cost_estimate=pl.CostEstimate(
+            flops=8 * tokens * model_width * hidden_here,
+            bytes_accessed=30 * tokens * model_width, transcendentals=tokens * hidden_here,
+        ),
+    )(normed, grad, up, bias, down, *carried)
+
+
+def bit_pairs(size, bit):
+    return [(index, index ^ bit) for index in range(size)]
+
+
+def swap(values, axis, bit):
+    return lax.ppermute(values, axis, bit_pairs(lax.axis_size(axis), bit))
+
+
+def pick(values, index, axis):
+    return lax.dynamic_index_in_dim(values, index, axis, keepdims=False)
+
+
+def after(values, *others):
+    return lax.optimization_barrier((values,) + others)[0]
+
+
+def place(first, second, index, axis=0):
+    return jnp.where(
+        index == 0,
+        jnp.concatenate([first, second], axis),
+        jnp.concatenate([second, first], axis),
+    )
+
+
+def fetch_other(weight, place_bits, behind=()):
+    near, core = place_bits
+    pieces = weight.shape[0] // 4
+    first = lax.dynamic_slice_in_dim(weight, (2 * near + core) * pieces, pieces, 0)
+    got = swap(after(first, *behind), "tensor", 1)
+    got_near = swap(got, "dp", 4)
+    got_core = swap(got, "dp", 1)
+    got_both = swap(got_near, "dp", 1)
+    whole = jnp.zeros(weight.shape, weight.dtype)
+    for piece, near_here, core_here in (
+        (got, near, core), (got_near, 1 - near, core),
+        (got_core, near, 1 - core), (got_both, 1 - near, 1 - core),
+    ):
+        whole = lax.dynamic_update_slice_in_dim(
+            whole, piece, (2 * near_here + core_here) * pieces, 0
+        )
+    return whole, got
+
+
+def scatter_rows(values, bits, order):
+    steps = {"far": (bits[0], 8), "near": (bits[1], 4), "x": (bits[2], 2)}
+    axes = ["far", "near", "x"]
+    for name in order:
+        index, mask = steps[name]
+        axis = axes.index(name)
+        axes.remove(name)
+        sent = swap(pick(values, 1 - index, axis), "dp", mask)
+        kept = pick(values, index, axis)
+        values = (kept.astype(F32) + sent.astype(F32)).astype(BF16)
+    return values
+
+
+def slot_device(
+    latents,
+    condition,
+    cotangent,
+    group_counts,
+    heads_weight,
+    heads_bias,
+    merge_weight,
+    merge_bias,
+    up_weight,
+    up_bias,
+    down_weight,
+    down_bias,
+    modulate_weight,
+    modulate_bias,
+):
+    side = lax.axis_index("tensor")
+    place_dp = lax.axis_index("dp")
+    core, x_bit, near, far = (lax.rem(place_dp // step, 2) for step in (1, 2, 4, 8))
+    bits = (far, near, x_bit)
+    half, model_width = latents.shape[1:]
+    columns = heads_weight.shape[3]
+    features = modulate_weight.shape[3]
+    hidden_here = up_weight.shape[2]
+    heads_own = heads_weight[0].reshape(model_width, 3 * columns)
+    merge_own, up_own, down_own = merge_weight[0], up_weight[0], down_weight[0]
+
+    latent_own = pick(latents, side, 0)
+    latent_other = swap(pick(latents, 1 - side, 0), "tensor", 1)
+    silu_cond = jax.nn.silu(condition.astype(F32)).astype(BF16)
+    local_mod = jnp.einsum(
+        "sd,dkc->skc", silu_cond, modulate_weight[0], preferred_element_type=F32
+    ) + modulate_bias[0].astype(F32)
+    mod_other = swap(pick(local_mod, 1 - side, 0), "tensor", 1)
+    shift1, scale1, gate1, shift2, scale2, gate2 = place(
+        pick(local_mod, side, 0), mod_other, side, 1
+    )
+    silu_all = lax.all_gather(silu_cond, "dp", axis=0, tiled=True)
+    bias_pack = swap(jnp.concatenate([heads_bias.reshape(-1), up_bias.reshape(-1)]), "tensor", 1)
+
+    def heads_offset(pair):
+        return jnp.concatenate([pair[0], jnp.zeros_like(pair[0]), pair[1]]).astype(F32)
+
+    offset_own = heads_offset(heads_bias[0])
+    offset_other = heads_offset(bias_pack[: 2 * columns].reshape(2, columns))
+    up_bias_own = up_bias.astype(F32)
+    up_bias_other = bias_pack[2 * columns :].reshape(1, hidden_here).astype(F32)
+    cotangent_sent = pick(cotangent, 1 - side, 0)
+    fetch_bits = (near, core)
+    heads_other, heads_piece = fetch_other(heads_own, fetch_bits)
+    merge_other, merge_piece = fetch_other(merge_own, fetch_bits, (latent_other,))
+    up_other, up_piece = fetch_other(up_own, fetch_bits, (heads_piece,))
+    cotangent_other = swap(after(cotangent_sent, merge_piece), "tensor", 1)
+    down_other, _ = fetch_other(down_own, fetch_bits, (up_piece,))
+    live_flag = (side < group_counts[0]).astype(F32)
+
+    stream = jnp.concatenate([latent_own, latent_other], 0).astype(F32)
+    norm1, inverse1 = normalize(stream)
+    normed1 = (norm1 * (1.0 + scale1) + shift1).astype(BF16)
+    normed1_peer = swap(normed1, "dp", 1)
+    qkv_own = (jnp.dot(normed1, heads_own, preferred_element_type=F32) + offset_own).astype(BF16)
+    attended_own, logsum_own = attend(qkv_own)
+    qkv_other = (
+        jnp.dot(normed1, heads_other, preferred_element_type=F32) + offset_other
+    ).astype(BF16)
+    attended_other, logsum_other = attend(qkv_other)
+    branch1 = (
+        jnp.dot(attended_own, merge_own, preferred_element_type=F32)
+        + jnp.dot(attended_other, merge_other, preferred_element_type=F32)
+        + merge_bias[0].astype(F32)
+    )
+    mid = stream + gate1 * branch1
+    norm2, inverse2 = normalize(mid)
+    normed2 = (norm2 * (1.0 + scale2) + shift2).astype(BF16)
+
+    grad = jnp.concatenate([pick(cotangent, side, 0), cotangent_other], 0).astype(F32) * live_flag
+    grad_b2 = (gate2 * grad).astype(BF16)
+    branch2, back2, hidden_own, pre_own, up_sums_own = feed(
+        normed2, grad_b2, up_own, up_bias_own, down_own
+    )
+    branch2, back2, hidden_other, pre_other, up_sums_other = feed(
+        normed2, grad_b2, up_other, up_bias_other, down_other, (branch2, back2)
+    )
+    branch2 = branch2 + down_bias[0].astype(F32)
+    output = (mid + gate2 * branch2).astype(BF16)
+    output_other = swap(output[half:], "tensor", 1)
+    block_output = place(output[None, :half], output_other[None], side)
+
+    normed2_peer = swap(normed2, "dp", 1)
+    grad_b2_peer = swap(grad_b2, "dp", 1)
+
+    def feature_grad(rows, rows_peer, own, other):
+        mine = jnp.concatenate([pick(own, core, 0), pick(other, core, 0)], 1)
+        peer = jnp.concatenate(
+            [swap(pick(own, 1 - core, 0), "dp", 1), swap(pick(other, 1 - core, 0), "dp", 1)], 1
+        )
+        return (dot_dims(rows, mine, 0, 0) + dot_dims(rows_peer, peer, 0, 0)).astype(BF16)
+
+    def reduce_blocks(total, order):
+        width = total.shape[1] // 2
+        total = scatter_rows(total.reshape(2, 2, 2, -1, 2 * width), bits, order)
+        sent = swap(total[:, width:], "tensor", 1)
+        return total[:, :width].astype(F32) + sent.astype(F32)
+
+    def join_cores(total):
+        total = total.astype(BF16).reshape((2, -1) + total.shape[1:])
+        sent = swap(pick(total, 1 - core, 0), "dp", 1)
+        return place(pick(total, core, 0), sent, core, total.ndim - 2).astype(F32)
+
+    down_total = feature_grad(grad_b2, grad_b2_peer, hidden_own, hidden_other)
+    up_total = feature_grad(normed2, normed2_peer, pre_own, pre_other)
+    down_grad = join_cores(reduce_blocks(down_total, ("x", "near", "far")))
+    up_grad = join_cores(reduce_blocks(up_total, ("near", "x", "far")))
+
+    grad_gate2 = jnp.sum(grad * branch2, 0)
+    down_bias_sum = column_sums(grad_b2)
+    grad_shift2 = jnp.sum(back2, 0)
+    grad_scale2 = jnp.sum(back2 * norm2, 0)
+    grad_mid = grad + normalize_back(back2 * (1.0 + scale2), norm2, inverse2)
+    grad_b1 = (gate1 * grad_mid).astype(BF16)
+    grad_gate1 = jnp.sum(grad_mid * branch1, 0)
+    merge_bias_sum = column_sums(grad_b1)
+    grad_att_own = times_transposed(grad_b1, merge_own).astype(BF16)
+    grad_att_other = times_transposed(grad_b1, merge_other).astype(BF16)
+    merge_total = outer_rows(
+        grad_b1, jnp.concatenate([attended_own, attended_other], 1)
+    ).astype(BF16).reshape(8, 2, -1, 2 * columns)
+    merge_sent = swap(pick(merge_total, 1 - core, 1), "dp", 1)
+    merge_total = (pick(merge_total, core, 1).astype(F32) + merge_sent.astype(F32)).astype(BF16)
+    merge_grad = reduce_blocks(merge_total.reshape(-1, 2 * columns), ("near", "x", "far"))
+    grad_att_own = after(grad_att_own, down_total, up_total, merge_total)
+
+    grads_own, pairs_own = attend_back(qkv_own, attended_own, grad_att_own, logsum_own)
+    grad_att_other = after(grad_att_other, grads_own)
+    grads_other, pairs_other = attend_back(qkv_other, attended_other, grad_att_other, logsum_other)
+    heads_grad = reduce_blocks(
+        feature_grad(normed1, normed1_peer, pairs_own, pairs_other), ("x", "near", "far")
+    )
+    heads_grad = join_cores(heads_grad.reshape(heads_grad.shape[0], 3, columns // 2))
+    grad_n1 = times_transposed(grads_own, heads_own) + times_transposed(grads_other, heads_other)
+    grad_shift1 = jnp.sum(grad_n1, 0)
+    grad_scale1 = jnp.sum(grad_n1 * norm1, 0)
+    grad_latent = grad_mid + normalize_back(grad_n1 * (1.0 + scale1), norm1, inverse1)
+    latent_sent = swap(grad_latent[half:].astype(BF16), "tensor", 1).astype(F32)
+    latent_grad = place(grad_latent[None, :half], latent_sent[None], side)
+
+    def query_value_sums(grads):
+        return jnp.concatenate(
+            [column_sums(grads[:, :columns]), column_sums(grads[:, 2 * columns :])]
+        )
+
+    def by_side(rows):
+        rows = rows.reshape(rows.shape[:-1] + (2, features))
+        return pick(rows, side, rows.ndim - 2), pick(rows, 1 - side, rows.ndim - 2)
+
+    grad_mod = jnp.stack(
+        [grad_shift1, grad_scale1, grad_gate1, grad_shift2, grad_scale2, grad_gate2]
+    ).astype(BF16)
+    grad_mod_own, grad_mod_sent = by_side(grad_mod)
+    grad_mod_slots = place(
+        grad_mod_own[None], swap(grad_mod_sent, "tensor", 1)[None], side
+    )
+    merge_own_sum, merge_other_sum = by_side(merge_bias_sum)
+    down_own_sum, down_other_sum = by_side(down_bias_sum)
+    bias_own = jnp.concatenate(
+        [query_value_sums(grads_own), merge_own_sum, up_sums_own[0], down_own_sum]
+    )
+    bias_other = jnp.concatenate(
+        [query_value_sums(grads_other), merge_other_sum, up_sums_other[0], down_other_sum]
+    )
+    bias_total = bias_own + swap(bias_other, "tensor", 1)
+    bias_total = jnp.sum(lax.all_gather(bias_total, "dp", axis=0), 0)
+    grad_mod_all = lax.all_gather(grad_mod_slots, "dp", axis=0, tiled=True)
+    rows_here = model_width // lax.axis_size("dp")
+    silu_rows = lax.dynamic_slice_in_dim(silu_all, place_dp * rows_here, rows_here, 1)
+    modulate_grad = jnp.einsum("sd,skc->dkc", silu_rows, grad_mod_all, preferred_element_type=F32)
+    modulate_bias_grad = jnp.sum(grad_mod_all.astype(F32), 0)
+    cond_partial = jnp.einsum(
+        "dkc,skc->sd", modulate_weight[0], grad_mod_slots, preferred_element_type=F32
+    )
+    cond_total = cond_partial + swap(cond_partial, "tensor", 1)
+    condition_grad = jax.vjp(jax.nn.silu, condition.astype(F32))[1](cond_total)[0]
+    edges = (0, 2 * columns, 2 * columns + features, 2 * columns + features + hidden_here, None)
+    heads_bias_grad, merge_bias_grad, up_bias_grad, down_bias_grad = (
+        bias_total[first:last] for first, last in zip(edges, edges[1:])
+    )
+    return (
+        block_output,
+        latent_grad,
+        condition_grad,
+        heads_grad[None],
+        heads_bias_grad.reshape(1, 2, columns),
+        merge_grad.T[None],
+        merge_bias_grad[None],
+        up_grad[None],
+        up_bias_grad[None],
+        down_grad.T[None],
+        down_bias_grad[None],
+        modulate_grad[None],
+        modulate_bias_grad[None],
+    )
+
+
 def solution(mesh):
     in_specs = (
         P("dp", "tensor", None),
@@ -472,6 +947,7 @@
         P(None, "dp", None, "tensor"),
         P(None, None, "tensor"),
     )
+    whole_slots = mesh.shape["tensor"] == 2 and mesh.shape["dp"] == 16
     return jax.shard_map(
-        per_device, mesh=mesh, in_specs=in_specs, out_specs=out_specs, check_vma=False
-    )
+        slot_device if whole_slots else per_device, mesh=mesh, in_specs=in_specs, out_specs=out_specs, check_vma=False
+    )

time: 1560 us -> 837 us (0.54)
  waiting for transfers between devices: 651 us -> 216 us
  matrix products: 430 us -> 146 us
  Pallas kernels: 0 us -> 187 us
  other arithmetic: 206 us -> 71.4 us
  blocking collectives: 84.7 us -> 56.9 us
  local copies, waits for them, and re-layouts: 141 us -> 116 us
  starting transfers between devices: 14.8 us -> 33.5 us
    reduce_scatter x9 -> x0, waiting for transfers between devices: 234 us -> none  [the longest x4 105 us: scatter_branch(): lax.psum_scatter(partial_rows(jnp.int32(0), operand.shape[0] // lax.axis_...]
    all_gather x8 -> x0, waiting for transfers between devices: 222 us -> none  [the longest x4 123 us: gather_tokens(): return lax.all_gather(values, 'tensor', axis=0, tiled=True)]
    ppermute x0 -> x54, waiting for transfers between devices: none -> 216 us  [swap(): return lax.ppermute(values, axis, bit_pairs(lax.axis_size(axis), bit))]
    unnamed x27 -> x0, waiting for transfers between devices: 194 us -> none
    pallas_call x0 -> x6, Pallas kernels: none -> 187 us  [the longest x2 88.4 us: feed(): pl.pallas_call(functools.partial(feed_kernel, token_rows, len(carried) >...]
    dot_general x39 -> x13, matrix products: 285 us -> 113 us  [the longest x6 70.1 us: dot_dims(): lax.dot_general(left, right, (((left_dim,), (right_dim,)), ((), ())), pre...]
    unnamed x266 -> x114, local copies, waits for them, and re-layouts: 103 us -> 3.38 us
    dot_general x8 -> x1, matrix products: 73.7 us -> 3.31 us  [outer_rows(): lax.dot_general(operand, other, (((0,), (0,)), ((), ())), preferred_eleme...]
  transfers between devices with their start and end apart: 22 -> 54, of which waited for: 16 -> 17; matrix products, arithmetic and copies ran while one was open for 27% -> 39% of each run, Pallas kernels for 0% -> 23%
where the time goes in v1:
time: 837 us; the launch traced here: 829 us
  waiting for transfers between devices  216 us (26%)
  Pallas kernels  187 us (22%)
  matrix products  146 us (17%)
  local copies, waits for them, and re-layouts  116 us (14%)
  other arithmetic  71.4 us (9%)
  blocking collectives  56.9 us (7%)
  starting transfers between devices  33.5 us (4%)
    ppermute x54, waiting for transfers between devices, swap(): return lax.ppermute(values, axis, bit_pairs(lax.axis_size(axis), bit))  216 us
    pallas_call x2, Pallas kernels, feed(): pl.pallas_call(functools.partial(feed_kernel, token_rows, len(carried) >...  88.4 us
    dot_general x6, matrix products, dot_dims(): lax.dot_general(left, right, (((left_dim,), (right_dim,)), ((), ())), pre...  70.1 us
    pallas_call x2, Pallas kernels, attend_back(): pl.pallas_call(functools.partial(attend_back_kernel, heads, key_rows, ste...  62 us
    pallas_call x2, Pallas kernels, attend(): pl.pallas_call(functools.partial(attend_kernel, heads), grid=(tokens // q...  36.5 us
    ppermute x54, starting transfers between devices, swap(): return lax.ppermute(values, axis, bit_pairs(lax.axis_size(axis), bit))  33.5 us
    dot_general x4, matrix products, times_transposed(): lax.dot_general(operand, weight, (((1,), (1,)), ((), ())), preferred_elem...  29.2 us
    squeeze x20, local copies, waits for them, and re-layouts, pick(): return lax.dynamic_index_in_dim(values, index, axis, keepdims=False)  28.9 us
  transfers between devices with their start and end apart: 54, of which 17 were waited for; matrix products, arithmetic and copies ran while one was open for 39% of the time, Pallas kernels for 23%

profile of v1, /device:TPU:0, one launch (start us, length us, event | category | flops | bytes accessed | tf_op | source)
XLA Modules:
  0.0 829.4 jit_solution(17243522672866875238)
XLA Ops:
  5.2 3.0 collective-permute-start.2
  8.2 2.8 dynamic-slice_bitcast_fusion.21
  11.7 5.6 fusion.61
  25.2 3.4 dynamic-slice_bitcast_fusion.19
  31.8 2.5 dynamic-slice_bitcast_fusion.16
  40.3 16.9 %collective-permute-done.6 = bf16[3456]{0:T(1024)(128)(2,1)} collective-permute-done((bf16[3456]{0:T(1024)(128)(2,1)}, bf16[3456]{0:T(1024)(128)(2,1)}, u32[]{:S(2)}, u32[]{:S(2)}) %collective-permute-start.6) | collective-permute-done | bytes 6944 | tf_op jit(solution)/shard_map/ppermute | solution.py:664
  75.7 3.2 fusion.16
  78.9 8.6 %add_convert_fusion.1.qkv_ref = bf16[1024,1728]{1,0:T(8,128)(2,1)} fusion(bf16[1024,1152]{1,0:T(8,128)(2,1)} %fusion.16, bf16[1152,1728]{0,1:T(8,128)(2,1)S(1)} %bitcast.226, f32[1728]{0:T(1024)S(1)} %copy-done.43), kind=kOutput, calls=%fused_computation.12 | convolution fusion | flops 4080402432 | bytes 9886464 | tf_op jit(solution)/shard_map/dot_general | solution.py:775
  87.5 18.6 %shard_map.237 = (bf16[1024,576]{1,0:T(8,128)(2,1)}, f32[8,1024]{1,0:T(8,128)}) custom-call(bf16[1024,1728]{1,0:T(8,128)(2,1)} %add_convert_fusion.1.qkv_ref), custom_call_target="tpu_custom_call" | custom-call | flops 8589934592 | bytes 4718592 | tf_op jit(solution)/shard_map/pallas_call | solution.py:483
  106.5 5.7 fusion.59
  126.2 2.7 broadcast_in_dim.78
  128.9 2.5 constant_dynamic-update-slice_fusion.7
  131.4 13.9 %collective-permute-done.11 = bf16[512,1152]{1,0:T(8,128)(2,1)S(1)} collective-permute-done((bf16[512,1152]{1,0:T(8,128)(2,1)S(1)}, bf16[512,1152]{1,0:T(8,128)(2,1)S(1)}, u32[]{:S(2)}, u32[]{:S(2)}) %collective-permute-start.11) | collective-permute-done | bytes 1179680 | tf_op jit(solution)/shard_map/ppermute | solution.py:664
  149.8 9.6 %add_convert_fusion.qkv_ref = bf16[1024,1728]{1,0:T(8,128)(2,1)} fusion(bf16[1024,1152]{1,0:T(8,128)(2,1)} %fusion.16, bf16[1152,1728]{1,0:T(8,128)(2,1)} %constant_dynamic-update-slice_fusion.12, f32[1728]{0:T(1024)S(1)} %copy-done.42), kind=kOutput, calls=%fused_computation.11 | convolution fusion | flops 4080402432 | bytes 9886464 | tf_op jit(solution)/shard_map/dot_general | solution.py:778
  159.4 17.9 %shard_map.238 = (bf16[1024,576]{1,0:T(8,128)(2,1)}, f32[8,1024]{1,0:T(8,128)}) custom-call(bf16[1024,1728]{1,0:T(8,128)(2,1)} %add_convert_fusion.qkv_ref), custom_call_target="tpu_custom_call" | custom-call | flops 8589934592 | bytes 4718592 | tf_op jit(solution)/shard_map/pallas_call | solution.py:483
  177.3 7.8 fusion.96
  188.1 43.4 %shard_map.239 = (f32[1024,1152]{1,0:T(8,128)}, f32[1024,1152]{1,0:T(8,128)}, bf16[2,1024,1152]{2,1,0:T(8,128)(2,1)}, bf16[2,1024,1152]{2,1,0:T(8,128)(2,1)}, f32[1,2304]{1,0:T(1,128)}) custom-call(bf16[1024,1152]{1,0:T(8,128)(2,1)} %add_convert_fusion.3.normed_ref, bf16[1024,1152]{1,0:T(8,128)(2,1)} %get-tuple-element.138.grad_ref, ...), custom_call_target="tpu_custom_call" | custom-call | flops 21743271936 | bytes 35389440 | tf_op jit(solution)/shard_map/pallas_call | solution.py:632
  233.2 5.0 dynamic-slice_bitcast_fusion.3
  241.2 2.8 broadcast_in_dim.79
  244.0 2.5 constant_dynamic-update-slice_fusion.3
  246.5 2.5 constant_dynamic-update-slice_fusion.6
  249.2 15.3 %collective-permute-done.17 = bf16[576,1152]{1,0:T(8,128)(2,1)S(1)} collective-permute-done((bf16[576,1152]{1,0:T(8,128)(2,1)}, bf16[576,1152]{1,0:T(8,128)(2,1)S(1)}, u32[]{:S(2)}, u32[]{:S(2)}) %collective-permute-start.17) | collective-permute-done | bytes 1327136 | tf_op jit(solution)/shard_map/ppermute | solution.py:664
  271.9 45.1 %shard_map.240 = (f32[1024,1152]{1,0:T(8,128)}, f32[1024,1152]{1,0:T(8,128)}, bf16[2,1024,1152]{2,1,0:T(8,128)(2,1)}, bf16[2,1024,1152]{2,1,0:T(8,128)(2,1)}, f32[1,2304]{1,0:T(1,128)}) custom-call(bf16[1024,1152]{1,0:T(8,128)(2,1)} %add_convert_fusion.3.normed_ref, bf16[1024,1152]{1,0:T(8,128)(2,1)} %get-tuple-element.138.grad_ref, ...), custom_call_target="tpu_custom_call" | custom-call | flops 21743271936 | bytes 35389440 | tf_op jit(solution)/shard_map/pallas_call | solution.py:632
  317.0 4.9 multiply_reduce_fusion.1
  322.7 8.8 %multiply_reduce_fusion = (bf16[1152]{0:T(1024)(128)(2,1)S(1)}, bf16[1024,1152]{1,0:T(8,128)(2,1)}, f32[1152]{0:T(1024)S(1)}, bf16[1024,1152]{1,0:T(8,128)(2,1)S(1)}, f32[1024,1152]{1,0:T(8,128)}) fusion(f32[1024,1152]{1,0:T(8,128)} %get-tuple-element.45, f32[1152]{0:T(1024)S(1)} %copy-done.35, f32[]{:T(128)S(6)} %convert_element_type.332, ...), kind=kLoop, calls=%fused_computation.51 | loop fusion | flops 27129600 | bytes 25993988 | tf_op jit(solution)/shard_map/reduce_sum | solution.py:829
  331.6 3.3 convolution_convert_fusion
  335.0 3.3 convolution_convert_fusion.2.grad_ref
  341.8 2.6 dynamic-slice_bitcast_fusion.6
  344.7 3.0 slice_bitcast_fusion.1
  349.2 12.4 %fusion.23 = f32[1152,2304]{1,0:T(8,128)} fusion(bf16[1024,1152]{1,0:T(8,128)(2,1)} %get-tuple-element.138.grad_ref, bf16[1024,1152]{1,0:T(8,128)(2,1)S(1)} %copy-done.19, bf16[1024,1152]{1,0:T(8,128)(2,1)} %get-tuple-element.156), kind=kOutput, calls=%fused_computation.34 | convolution fusion | flops 5445255168 | bytes 17694720 | tf_op jit(solution)/shard_map/dot_general | solution.py:456
  364.4 9.9 %fusion.30 = f32[1152,2304]{1,0:T(8,128)} fusion(bf16[1024,1152]{1,0:T(8,128)(2,1)} %add_convert_fusion.3.normed_ref, bf16[1024,1152]{1,0:T(8,128)(2,1)S(1)} %copy-done.18, bf16[1024,1152]{1,0:T(8,128)(2,1)S(1)} %copy-done.16), kind=kOutput, calls=%fused_computation.41 | convolution fusion | flops 5445255168 | bytes 17694720 | tf_op jit(solution)/shard_map/dot_general | solution.py:456
  374.4 5.4 convolution_convert_fusion.1.grad_ref
  384.3 3.5 maximum_select_fusion.1
  388.1 5.0 collective-permute-done.41
  394.4 2.6 collective-permute-start.42
  397.0 14.2 %fusion.1 = bf16[1152,2304]{1,0:T(8,128)(2,1)} fusion(f32[1152,2304]{1,0:T(8,128)} %fusion.30, bf16[1024,1152]{1,0:T(8,128)(2,1)} %collective-permute-done.24, bf16[1024,1152]{1,0:T(8,128)(2,1)} %collective-permute-done.26, bf16[1024,1152]{1,0:T(8,128)(2,1)} %collective-permute-done.25), kind=kOutput, calls=%fused_computation.3 | convolution fusion | flops 5450563584 | bytes 23003136 | tf_op jit(solution)/shard_map/dot_general | solution.py:456
  411.2 10.7 %fusion = bf16[1152,2304]{1,0:T(8,128)(2,1)} fusion(f32[1152,2304]{1,0:T(8,128)} %fusion.23, bf16[1024,1152]{1,0:T(8,128)(2,1)S(1)} %collective-permute-done.21, bf16[1024,1152]{1,0:T(8,128)(2,1)} %collective-permute-done.23, bf16[1024,1152]{1,0:T(8,128)(2,1)S(1)} %collective-permute-done.22), kind=kOutput, calls=%fused_computation.2 | convolution fusion | flops 5450563584 | bytes 23003136 | tf_op jit(solution)/shard_map/dot_general | solution.py:456
  421.9 31.2 %shard_map.241 = (bf16[1024,1728]{1,0:T(8,128)(2,1)}, bf16[2,1024,864]{2,1,0:T(8,128)(2,1)}) custom-call(bf16[1024,1728]{1,0:T(8,128)(2,1)} %add_convert_fusion.1.qkv_ref, bf16[1024,576]{1,0:T(8,128)(2,1)} %get-tuple-element.37.out_ref, bf16[1024,576]{1,0:T(8,128)(2,1)} %convolution_convert_fusion.2.grad_ref, f32[8,1024]{1,0:T(8,128)} %get-tuple-element.52.logsum_ref), custom_call_target="tpu_custom_call" | custom-call | flops 21474836480 | bytes 12976128 | tf_op jit(solution)/shard_map/pallas_call | solution.py:552
  453.1 10.2 %fusion.100 = f32[1024,1152]{1,0:T(8,128)} fusion(bf16[1024,1728]{1,0:T(8,128)(2,1)} %get-tuple-element.53, bf16[1152,1728]{0,1:T(8,128)(2,1)} %bitcast.225), kind=kOutput, calls=%fused_computation.258 | convolution fusion | flops 4076863488 | bytes 12238848 | tf_op jit(solution)/shard_map/dot_general | solution.py:47
  463.4 30.8 %shard_map.242 = (bf16[1024,1728]{1,0:T(8,128)(2,1)}, bf16[2,1024,864]{2,1,0:T(8,128)(2,1)}) custom-call(bf16[1024,1728]{1,0:T(8,128)(2,1)} %add_convert_fusion.qkv_ref, bf16[1024,576]{1,0:T(8,128)(2,1)} %get-tuple-element.38.out_ref, bf16[1024,576]{1,0:T(8,128)(2,1)} %convolution_convert_fusion.1.grad_ref, f32[8,1024]{1,0:T(8,128)} %get-tuple-element.55.logsum_ref), custom_call_target="tpu_custom_call" | custom-call | flops 21474836480 | bytes 12976128 | tf_op jit(solution)/shard_map/pallas_call | solution.py:552
  496.4 10.2 %fusion.21 = (bf16[1152]{0:T(1024)(128)(2,1)S(1)}, f32[1024]{0:T(1024)S(1)}, f32[1024]{0:T(1024)S(1)}, bf16[1152]{0:T(1024)(128)(2,1)S(1)}, f32[1024,1152]{1,0:T(8,128)S(1)}) fusion(f32[1024]{0:T(1024)S(1)} %copy-done.34, f32[1024]{0:T(1024)S(1)} %copy-done.31, bf16[512,1152]{1,0:T(8,128)(2,1)} %collective-permute-done, ...), kind=kOutput, calls=%fused_computation.32 | convolution fusion | flops 4093374464 | bytes 19342336 | tf_op jit(solution)/shard_map/dot_general | solution.py:47
  506.6 5.5 multiply_reduce_fusion.2
  515.8 3.4 dynamic-slice_bitcast_fusion
  519.2 3.5 dynamic-slice_bitcast_fusion.1
  524.3 5.8 constant_dynamic-slice_fusion.7
  530.1 4.2 copy.70
  534.4 11.1 %fusion.38 = f32[1152,1728]{0,1:T(8,128)} fusion(bf16[1024,1152]{1,0:T(8,128)(2,1)} %fusion.16, bf16[1024,864]{1,0:T(8,128)(2,1)} %get-tuple-element.162, bf16[1024,864]{1,0:T(8,128)(2,1)} %get-tuple-element.191), kind=kOutput, calls=%fused_computation.69 | convolution fusion | flops 4083941376 | bytes 13860864 | tf_op jit(solution)/shard_map/dot_general | solution.py:456
  548.5 19.5 %all_gather.15 = bf16[32,6,576]{2,1,0:T(8,128)(2,1)S(1)} all-gather(bf16[2,6,576]{2,1,0:T(8,128)(2,1)S(1)} %maximum_select_fusion.6), channel_id=1, replica_groups=mesh['dp'=16,'tensor'=2] {'dp'}, dimensions={0}, use_global_device_ids=true | all-gather | bytes 235008 | tf_op jit(solution)/shard_map/all_gather | solution.py:887
  568.0 4.5 fusion.51
  577.4 17.8 %all-gather.2 = bf16[16,2,1152]{2,1,0:T(2,128)(2,1)S(1)} all-gather(bf16[1,2,1152]{2,1,0:T(2,128)(2,1)S(1)} %get-tuple-element.185), channel_id=1, replica_groups=mesh['dp'=16,'tensor'=2] {'dp'}, dimensions={0}, use_global_device_ids=true | all-gather | bytes 78336 | tf_op jit(solution)/shard_map/all_gather | solution.py:752
  597.0 19.7 %all-gather.1 = f32[16,1,4608]{2,1,0:T(1,128)S(1)} all-gather(f32[1,1,4608]{2,1,0:T(1,128)S(1)} %reshape.351), channel_id=2, replica_groups=mesh['dp'=16,'tensor'=2] {'dp'}, dimensions={0}, use_global_device_ids=true | all-gather | bytes 313344 | tf_op jit(solution)/shard_map/all_gather | solution.py:886
  625.5 5.0 maximum_select_fusion
  630.6 11.8 %fusion.6 = bf16[1152,1728]{0,1:T(8,128)(2,1)} fusion(f32[1152,1728]{0,1:T(8,128)} %fusion.38, bf16[1024,1152]{1,0:T(8,128)(2,1)} %collective-permute-done.31, bf16[1024,864]{0,1:T(8,128)(2,1)} %collective-permute-done.33, bf16[1024,864]{0,1:T(8,128)(2,1)} %collective-permute-done.32), kind=kOutput, calls=%fused_computation.9 | convolution fusion | flops 4087922688 | bytes 17842176 | tf_op jit(solution)/shard_map/dot_general | solution.py:456
  642.4 6.6 copy.72
  652.5 31.2 %collective-permute-done.49 = bf16[2,2,144,2304]{3,2,1,0:T(8,128)(2,1)} collective-permute-done((bf16[2,2,144,2304]{3,2,1,0:T(8,128)(2,1)}, bf16[2,2,144,2304]{3,2,1,0:T(8,128)(2,1)}, u32[]{:S(2)}, u32[]{:S(2)}) %collective-permute-start.49) | collective-permute-done | bytes 2654240 | tf_op jit(solution)/shard_map/ppermute | solution.py:664
  683.7 3.2 fusion.13
  687.1 2.6 fusion.14
  690.4 37.4 %collective-permute-done.34 = bf16[2,2,144,1728]{3,2,1,0:T(8,128)(2,1)S(1)} collective-permute-done((bf16[2,2,144,1728]{3,2,1,0:T(8,128)(2,1)S(1)}, bf16[2,2,144,1728]{3,2,1,0:T(8,128)(2,1)S(1)}, u32[]{:S(2)}, u32[]{:S(2)}) %collective-permute-start.34) | collective-permute-done | bytes 1990688 | tf_op jit(solution)/shard_map/ppermute | solution.py:664
  729.0 25.8 %collective-permute-done.45 = bf16[2,144,2304]{2,1,0:T(8,128)(2,1)S(1)} collective-permute-done((bf16[2,144,2304]{2,1,0:T(8,128)(2,1)S(1)}, bf16[2,144,2304]{2,1,0:T(8,128)(2,1)S(1)}, u32[]{:S(2)}, u32[]{:S(2)}) %collective-permute-start.45) | collective-permute-done | bytes 1327136 | tf_op jit(solution)/shard_map/ppermute | solution.py:664
  755.3 10.7 %collective-permute-done.51 = bf16[144,2304]{1,0:T(8,128)(2,1)S(1)} collective-permute-done((bf16[144,2304]{1,0:T(8,128)(2,1)S(1)}, bf16[144,2304]{1,0:T(8,128)(2,1)S(1)}, u32[]{:S(2)}, u32[]{:S(2)}) %collective-permute-start.51) | collective-permute-done | bytes 663584 | tf_op jit(solution)/shard_map/ppermute | solution.py:664
  767.8 23.1 %collective-permute-done.46 = bf16[144,2304]{1,0:T(8,128)(2,1)S(1)} collective-permute-done((bf16[144,2304]{1,0:T(8,128)(2,1)S(1)}, bf16[144,2304]{1,0:T(8,128)(2,1)S(1)}, u32[]{:S(2)}, u32[]{:S(2)}) %collective-permute-start.46) | collective-permute-done | bytes 663584 | tf_op jit(solution)/shard_map/ppermute | solution.py:664
  793.3 7.6 collective-permute-done.47
  801.2 17.3 %collective-permute-done.36 = bf16[144,1728]{1,0:T(8,128)(2,1)S(1)} collective-permute-done((bf16[144,1728]{1,0:T(8,128)(2,1)S(1)}, bf16[144,1728]{1,0:T(8,128)(2,1)S(1)}, u32[]{:S(2)}, u32[]{:S(2)}) %collective-permute-start.36) | collective-permute-done | bytes 497696 | tf_op jit(solution)/shard_map/ppermute | solution.py:664
  820.3 5.5 collective-permute-done.37
  (334 shorter events, 130.8 us)
Async XLA Ops:
  0.6 30.4 %copy-start = (bf16[1,576,1152]{2,1,0:T(8,128)(2,1)S(1)}, bf16[1,576,1152]{2,1,0:T(8,128)(2,1)}, u32[]{:S(2)}) copy-start(bf16[1,576,1152]{2,1,0:T(8,128)(2,1)} %param.20) | copy-start | bytes 3981316
  5.2 59.6 %collective-permute-start.2 = (bf16[288,1728]{1,0:T(8,128)(2,1)}, bf16[288,1728]{1,0:T(8,128)(2,1)S(1)}, u32[]{:S(2)}, u32[]{:S(2)}) collective-permute-start(bf16[288,1728]{1,0:T(8,128)(2,1)} %copy.64), channel_id=1, source_target_pairs={{0,1},{1,0},{2,3},{3,2},{4,5},{5,4},{6,7},{7,6},{8,9},{9,8},{10,11... | collective-permute-start | bytes 2985992 | tf_op jit(solution)/shard_map/ppermute | solution.py:664
  11.0 166.3 %copy-start.3 = (bf16[512,1152]{1,0:T(8,128)(2,1)}, bf16[512,1152]{1,0:T(8,128)(2,1)S(1)}, u32[]{:S(2)}) copy-start(bf16[512,1152]{1,0:T(8,128)(2,1)S(1)} %get-tuple-element.167) | copy-start | bytes 3538948
  11.0 60.2 %collective-permute-start = (bf16[512,1152]{1,0:T(8,128)(2,1)}, bf16[512,1152]{1,0:T(8,128)(2,1)}, u32[]{:S(2)}, u32[]{:S(2)}) collective-permute-start(bf16[512,1152]{1,0:T(8,128)(2,1)} %get-tuple-element.168), channel_id=1, source_target_pairs={{0,1},{1,0},{2,3},{3,2},{4,5},{5,4},{6,7},{7,6},{8,9},{9,8},{10,11... | collective-permute-start | bytes 3538952 | tf_op jit(solution)/shard_map/ppermute | solution.py:664
  18.0 45.2 %collective-permute-start.1 = (f32[6,576]{1,0:T(8,128)}, f32[6,576]{1,0:T(8,128)}, u32[]{:S(2)}, u32[]{:S(2)}) collective-permute-start(f32[6,576]{1,0:T(8,128)} %bitcast.199), channel_id=1, source_target_pairs={{0,1},{1,0},{2,3},{3,2},{4,5},{5,4},{6,7},{7,6},{8,9},{9,8},{10,11... | collective-permute-start | bytes 41480 | tf_op jit(solution)/shard_map/ppermute | solution.py:664
  23.9 33.3 %collective-permute-start.6 = (bf16[3456]{0:T(1024)(128)(2,1)}, bf16[3456]{0:T(1024)(128)(2,1)}, u32[]{:S(2)}, u32[]{:S(2)}) collective-permute-start(bf16[3456]{0:T(1024)(128)(2,1)} %pad_maximum_fusion.2), channel_id=1, source_target_pairs={{0,1},{1,0},{2,3},{3,2},{4,5},{5,4},{6,7},{7,6},{8,9},{9,8},{10,11... | collective-permute-start | bytes 20744 | tf_op jit(solution)/shard_map/ppermute | solution.py:664
  64.8 60.4 %collective-permute-start.12 = (bf16[288,2304]{1,0:T(8,128)(2,1)}, bf16[288,2304]{1,0:T(8,128)(2,1)}, u32[]{:S(2)}, u32[]{:S(2)}) collective-permute-start(bf16[288,2304]{1,0:T(8,128)(2,1)} %dynamic-slice_bitcast_fusion.17), channel_id=1, source_target_pairs={{0,1},{1,0},{2,3},{3,2},{4,5},{5,4},{6,7},{7,6},{8,9},{9,8},{10,11... | collective-permute-start | bytes 3981320 | tf_op jit(solution)/shard_map/ppermute | solution.py:664
  66.5 52.8 %collective-permute-start.3 = (bf16[288,1728]{1,0:T(8,128)(2,1)S(1)}, bf16[288,1728]{1,0:T(8,128)(2,1)}, u32[]{:S(2)}, u32[]{:S(2)}) collective-permute-start(bf16[288,1728]{1,0:T(8,128)(2,1)S(1)} %collective-permute-done.2), channel_id=1, source_target_pairs={{0,8},{2,10},{4,12},{6,14},{8,0},{10,2},{12,4},{14,6},{16,24},{18,... | collective-permute-start | bytes 2985992 | tf_op jit(solution)/shard_map/ppermute | solution.py:664
  68.0 54.2 %collective-permute-start.4 = (bf16[288,1728]{1,0:T(8,128)(2,1)S(1)}, bf16[288,1728]{1,0:T(8,128)(2,1)}, u32[]{:S(2)}, u32[]{:S(2)}) collective-permute-start(bf16[288,1728]{1,0:T(8,128)(2,1)S(1)} %collective-permute-done.2), channel_id=1, source_target_pairs={{0,2},{2,0},{4,6},{6,4},{8,10},{10,8},{12,14},{14,12},{16,18},{18,... | collective-permute-start | bytes 2985992 | tf_op jit(solution)/shard_map/ppermute | solution.py:664
  75.1 31.0 %collective-permute-start.7 = (bf16[144,1152]{1,0:T(8,128)(2,1)S(1)}, bf16[144,1152]{1,0:T(8,128)(2,1)}, u32[]{:S(2)}, u32[]{:S(2)}) collective-permute-start(bf16[144,1152]{1,0:T(8,128)(2,1)S(1)} %copy-done.26), channel_id=1, source_target_pairs={{0,1},{1,0},{2,3},{3,2},{4,5},{5,4},{6,7},{7,6},{8,9},{9,8},{10,11... | collective-permute-start | bytes 995336 | tf_op jit(solution)/shard_map/ppermute | solution.py:664
  106.1 10.2 %collective-permute-start.8 = (bf16[144,1152]{1,0:T(8,128)(2,1)}, bf16[144,1152]{1,0:T(8,128)(2,1)S(1)}, u32[]{:S(2)}, u32[]{:S(2)}) collective-permute-start(bf16[144,1152]{1,0:T(8,128)(2,1)} %collective-permute-done.7), channel_id=1, source_target_pairs={{0,8},{2,10},{4,12},{6,14},{8,0},{10,2},{12,4},{14,6},{16,24},{18,... | collective-permute-start | bytes 995336 | tf_op jit(solution)/shard_map/ppermute | solution.py:664
  112.2 6.4 collective-permute-start.9
  116.3 28.9 %collective-permute-start.11 = (bf16[512,1152]{1,0:T(8,128)(2,1)S(1)}, bf16[512,1152]{1,0:T(8,128)(2,1)S(1)}, u32[]{:S(2)}, u32[]{:S(2)}) collective-permute-start(bf16[512,1152]{1,0:T(8,128)(2,1)S(1)} %copy-done.24), channel_id=1, source_target_pairs={{0,1},{1,0},{2,3},{3,2},{4,5},{5,4},{6,7},{7,6},{8,9},{9,8},{10,11... | collective-permute-start | bytes 3538952 | tf_op jit(solution)/shard_map/ppermute | solution.py:664
  118.6 5.8 collective-permute-start.10
  119.4 28.1 %collective-permute-start.5 = (bf16[288,1728]{1,0:T(8,128)(2,1)}, bf16[288,1728]{1,0:T(8,128)(2,1)}, u32[]{:S(2)}, u32[]{:S(2)}) collective-permute-start(bf16[288,1728]{1,0:T(8,128)(2,1)} %collective-permute-done.3), channel_id=1, source_target_pairs={{0,2},{2,0},{4,6},{6,4},{8,10},{10,8},{12,14},{14,12},{16,18},{18,... | collective-permute-start | bytes 2985992 | tf_op jit(solution)/shard_map/ppermute | solution.py:664
  125.2 107.6 %collective-permute-start.16 = (bf16[576,1152]{1,0:T(8,128)(2,1)}, bf16[576,1152]{1,0:T(8,128)(2,1)}, u32[]{:S(2)}, u32[]{:S(2)}) collective-permute-start(bf16[576,1152]{1,0:T(8,128)(2,1)} %dynamic-slice_bitcast_fusion.16), channel_id=1, source_target_pairs={{0,1},{1,0},{2,3},{3,2},{4,5},{5,4},{6,7},{7,6},{8,9},{9,8},{10,11... | collective-permute-start | bytes 3981320 | tf_op jit(solution)/shard_map/ppermute | solution.py:664
  125.7 115.2 %collective-permute-start.13 = (bf16[288,2304]{1,0:T(8,128)(2,1)}, bf16[288,2304]{1,0:T(8,128)(2,1)}, u32[]{:S(2)}, u32[]{:S(2)}) collective-permute-start(bf16[288,2304]{1,0:T(8,128)(2,1)} %collective-permute-done.12), channel_id=1, source_target_pairs={{0,8},{2,10},{4,12},{6,14},{8,0},{10,2},{12,4},{14,6},{16,24},{18,... | collective-permute-start | bytes 3981320 | tf_op jit(solution)/shard_map/ppermute | solution.py:664
  126.2 122.8 %collective-permute-start.14 = (bf16[288,2304]{1,0:T(8,128)(2,1)}, bf16[288,2304]{1,0:T(8,128)(2,1)}, u32[]{:S(2)}, u32[]{:S(2)}) collective-permute-start(bf16[288,2304]{1,0:T(8,128)(2,1)} %collective-permute-done.12), channel_id=1, source_target_pairs={{0,2},{2,0},{4,6},{6,4},{8,10},{10,8},{12,14},{14,12},{16,18},{18,... | collective-permute-start | bytes 3981320 | tf_op jit(solution)/shard_map/ppermute | solution.py:664
  188.1 205.8 %collective-permute-start.24 = (bf16[1024,1152]{1,0:T(8,128)(2,1)}, bf16[1024,1152]{1,0:T(8,128)(2,1)}, u32[]{:S(2)}, u32[]{:S(2)}) collective-permute-start(bf16[1024,1152]{1,0:T(8,128)(2,1)} %add_convert_fusion.3.normed_ref), channel_id=1, source_target_pairs={{0,2},{2,0},{4,6},{6,4},{8,10},{10,8},{12,14},{14,12},{16,18},{18,... | collective-permute-start | bytes 7077896 | tf_op jit(solution)/shard_map/ppermute | solution.py:664
  232.8 31.7 %collective-permute-start.17 = (bf16[576,1152]{1,0:T(8,128)(2,1)}, bf16[576,1152]{1,0:T(8,128)(2,1)S(1)}, u32[]{:S(2)}, u32[]{:S(2)}) collective-permute-start(bf16[576,1152]{1,0:T(8,128)(2,1)} %collective-permute-done.16), channel_id=1, source_target_pairs={{0,8},{2,10},{4,12},{6,14},{8,0},{10,2},{12,4},{14,6},{16,24},{18,... | collective-permute-start | bytes 3981320 | tf_op jit(solution)/shard_map/ppermute | solution.py:664
  240.7 27.6 %collective-permute-start.18 = (bf16[576,1152]{1,0:T(8,128)(2,1)}, bf16[576,1152]{1,0:T(8,128)(2,1)S(1)}, u32[]{:S(2)}, u32[]{:S(2)}) collective-permute-start(bf16[576,1152]{1,0:T(8,128)(2,1)} %collective-permute-done.16), channel_id=1, source_target_pairs={{0,2},{2,0},{4,6},{6,4},{8,10},{10,8},{12,14},{14,12},{16,18},{18,... | collective-permute-start | bytes 3981320 | tf_op jit(solution)/shard_map/ppermute | solution.py:664
  240.9 28.6 %collective-permute-start.15 = (bf16[288,2304]{1,0:T(8,128)(2,1)}, bf16[288,2304]{1,0:T(8,128)(2,1)S(1)}, u32[]{:S(2)}, u32[]{:S(2)}) collective-permute-start(bf16[288,2304]{1,0:T(8,128)(2,1)} %collective-permute-done.13), channel_id=1, source_target_pairs={{0,2},{2,0},{4,6},{6,4},{8,10},{10,8},{12,14},{14,12},{16,18},{18,... | collective-permute-start | bytes 3981320 | tf_op jit(solution)/shard_map/ppermute | solution.py:664
  249.0 138.8 %collective-permute-start.25 = (bf16[1024,1152]{1,0:T(8,128)(2,1)}, bf16[1024,1152]{1,0:T(8,128)(2,1)}, u32[]{:S(2)}, u32[]{:S(2)}) collective-permute-start(bf16[1024,1152]{1,0:T(8,128)(2,1)} %get-tuple-element.151), channel_id=1, source_target_pairs={{0,2},{2,0},{4,6},{6,4},{8,10},{10,8},{12,14},{14,12},{16,18},{18,... | collective-permute-start | bytes 7077896 | tf_op jit(solution)/shard_map/ppermute | solution.py:664
  264.6 6.1 collective-permute-start.19
  338.4 23.2 %collective-permute-start.27 = (bf16[8,72,1152]{2,1,0:T(8,128)(2,1)S(1)}, bf16[8,72,1152]{2,1,0:T(8,128)(2,1)}, u32[]{:S(2)}, u32[]{:S(2)}) collective-permute-start(bf16[8,72,1152]{2,1,0:T(8,128)(2,1)S(1)} %dynamic-slice_bitcast_fusion.15), channel_id=1, source_target_pairs={{0,2},{2,0},{4,6},{6,4},{8,10},{10,8},{12,14},{14,12},{16,18},{18,... | collective-permute-start | bytes 3981320 | tf_op jit(solution)/shard_map/ppermute | solution.py:664
  341.4 53.0 %collective-permute-start.26 = (bf16[1024,1152]{1,0:T(8,128)(2,1)}, bf16[1024,1152]{1,0:T(8,128)(2,1)}, u32[]{:S(2)}, u32[]{:S(2)}) collective-permute-start(bf16[1024,1152]{1,0:T(8,128)(2,1)} %get-tuple-element.153), channel_id=1, source_target_pairs={{0,2},{2,0},{4,6},{6,4},{8,10},{10,8},{12,14},{14,12},{16,18},{18,... | collective-permute-start | bytes 7077896 | tf_op jit(solution)/shard_map/ppermute | solution.py:664
  347.7 35.1 %collective-permute-start.20 = (bf16[512,1152]{1,0:T(8,128)(2,1)}, bf16[512,1152]{1,0:T(8,128)(2,1)}, u32[]{:S(2)}, u32[]{:S(2)}) collective-permute-start(bf16[512,1152]{1,0:T(8,128)(2,1)} %get-tuple-element.164), channel_id=1, source_target_pairs={{0,1},{1,0},{2,3},{3,2},{4,5},{5,4},{6,7},{7,6},{8,9},{9,8},{10,11... | collective-permute-start | bytes 3538952 | tf_op jit(solution)/shard_map/ppermute | solution.py:664
  363.7 17.7 %collective-permute-start.40 = (bf16[2,2,72,1152]{3,2,1,0:T(8,128)(2,1)S(1)}, bf16[2,2,72,1152]{3,2,1,0:T(8,128)(2,1)}, u32[]{:S(2)}, u32[]{:S(2)}) collective-permute-start(bf16[2,2,72,1152]{3,2,1,0:T(8,128)(2,1)S(1)} %dynamic-slice_bitcast_fusion.25), channel_id=1, source_target_pairs={{0,8},{2,10},{4,12},{6,14},{8,0},{10,2},{12,4},{14,6},{16,24},{18,... | collective-permute-start | bytes 1990664 | tf_op jit(solution)/shard_map/ppermute | solution.py:664
  381.4 29.7 %collective-permute-start.21 = (bf16[1024,1152]{1,0:T(8,128)(2,1)S(1)}, bf16[1024,1152]{1,0:T(8,128)(2,1)S(1)}, u32[]{:S(2)}, u32[]{:S(2)}) collective-permute-start(bf16[1024,1152]{1,0:T(8,128)(2,1)S(1)} %copy-done.20), channel_id=1, source_target_pairs={{0,2},{2,0},{4,6},{6,4},{8,10},{10,8},{12,14},{14,12},{16,18},{18,... | collective-permute-start | bytes 7077896 | tf_op jit(solution)/shard_map/ppermute | solution.py:664
  382.8 10.3 %collective-permute-start.41 = (bf16[2,72,1152]{2,1,0:T(8,128)(2,1)S(1)}, bf16[2,72,1152]{2,1,0:T(8,128)(2,1)S(1)}, u32[]{:S(2)}, u32[]{:S(2)}) collective-permute-start(bf16[2,72,1152]{2,1,0:T(8,128)(2,1)S(1)} %dynamic-slice_bitcast_fusion.27), channel_id=1, source_target_pairs={{0,4},{2,6},{4,0},{6,2},{8,12},{10,14},{12,8},{14,10},{16,20},{18,... | collective-permute-start | bytes 995336 | tf_op jit(solution)/shard_map/ppermute | solution.py:664
  387.8 23.4 %collective-permute-start.22 = (bf16[1024,1152]{1,0:T(8,128)(2,1)S(1)}, bf16[1024,1152]{1,0:T(8,128)(2,1)S(1)}, u32[]{:S(2)}, u32[]{:S(2)}) collective-permute-start(bf16[1024,1152]{1,0:T(8,128)(2,1)S(1)} %copy-done.15), channel_id=1, source_target_pairs={{0,2},{2,0},{4,6},{6,4},{8,10},{10,8},{12,14},{14,12},{16,18},{18,... | collective-permute-start | bytes 7077896 | tf_op jit(solution)/shard_map/ppermute | solution.py:664
  393.1 18.1 %collective-permute-start.23 = (bf16[1024,1152]{1,0:T(8,128)(2,1)S(1)}, bf16[1024,1152]{1,0:T(8,128)(2,1)}, u32[]{:S(2)}, u32[]{:S(2)}) collective-permute-start(bf16[1024,1152]{1,0:T(8,128)(2,1)S(1)} %copy-done.17), channel_id=1, source_target_pairs={{0,2},{2,0},{4,6},{6,4},{8,10},{10,8},{12,14},{14,12},{16,18},{18,... | collective-permute-start | bytes 7077896 | tf_op jit(solution)/shard_map/ppermute | solution.py:664
  393.9 236.7 %collective-permute-start.31 = (bf16[1024,1152]{1,0:T(8,128)(2,1)}, bf16[1024,1152]{1,0:T(8,128)(2,1)}, u32[]{:S(2)}, u32[]{:S(2)}) collective-permute-start(bf16[1024,1152]{1,0:T(8,128)(2,1)} %fusion.16), channel_id=1, source_target_pairs={{0,2},{2,0},{4,6},{6,4},{8,10},{10,8},{12,14},{14,12},{16,18},{18,... | collective-permute-start | bytes 7077896 | tf_op jit(solution)/shard_map/ppermute | solution.py:664
  394.4 222.4 %collective-permute-start.42 = (bf16[72,1152]{1,0:T(8,128)(2,1)}, bf16[72,1152]{1,0:T(8,128)(2,1)}, u32[]{:S(2)}, u32[]{:S(2)}) collective-permute-start(bf16[72,1152]{1,0:T(8,128)(2,1)} %dynamic-slice_bitcast_fusion.33), channel_id=1, source_target_pairs={{0,16},{2,18},{4,20},{6,22},{8,24},{10,26},{12,28},{14,30},{16,0},... | collective-permute-start | bytes 497672 | tf_op jit(solution)/shard_map/ppermute | solution.py:664
  463.4 33.0 %copy-start.4 = (bf16[512,1152]{1,0:T(8,128)(2,1)S(1)}, bf16[512,1152]{1,0:T(8,128)(2,1)}, u32[]{:S(2)}) copy-start(bf16[512,1152]{1,0:T(8,128)(2,1)} %copy-done.3) | copy-start | bytes 3538948
  463.4 33.0 %copy-start.29 = (f32[1152]{0:T(1024)S(1)}, f32[1152]{0:T(1024)}, u32[]{:S(2)}) copy-start(f32[1152]{0:T(1024)} %copy-done.28) | copy-start | bytes 13828
  463.4 33.0 %copy-start.31 = (f32[1024]{0:T(1024)S(1)}, f32[1024]{0:T(1024)}, u32[]{:S(2)}) copy-start(f32[1024]{0:T(1024)} %copy-done.30) | copy-start | bytes 12292
  463.4 33.0 %copy-start.34 = (f32[1024]{0:T(1024)S(1)}, f32[1024]{0:T(1024)}, u32[]{:S(2)}) copy-start(f32[1024]{0:T(1024)} %copy-done.33) | copy-start | bytes 12292
  515.2 33.2 %collective-permute-start.29 = (bf16[6,576]{1,0:T(8,128)(2,1)S(1)}, bf16[6,576]{1,0:T(8,128)(2,1)S(1)}, u32[]{:S(2)}, u32[]{:S(2)}) collective-permute-start(bf16[6,576]{1,0:T(8,128)(2,1)S(1)} %bitcast.233), channel_id=1, source_target_pairs={{0,1},{1,0},{2,3},{3,2},{4,5},{5,4},{6,7},{7,6},{8,9},{9,8},{10,11... | collective-permute-start | bytes 20744 | tf_op jit(solution)/shard_map/ppermute | solution.py:664
  522.8 73.8 %collective-permute-start.39 = (f32[4608]{0:T(1024)S(1)}, f32[4608]{0:T(1024)S(1)}, u32[]{:S(2)}, u32[]{:S(2)}) collective-permute-start(f32[4608]{0:T(1024)S(1)} %concatenate.159), channel_id=1, source_target_pairs={{0,1},{1,0},{2,3},{3,2},{4,5},{5,4},{6,7},{7,6},{8,9},{9,8},{10,11... | collective-permute-start | bytes 55304 | tf_op jit(solution)/shard_map/ppermute | solution.py:664
  534.4 96.2 %collective-permute-start.32 = (bf16[1024,864]{0,1:T(8,128)(2,1)}, bf16[1024,864]{0,1:T(8,128)(2,1)}, u32[]{:S(2)}, u32[]{:S(2)}) collective-permute-start(bf16[1024,864]{0,1:T(8,128)(2,1)} %bitcast.220), channel_id=1, source_target_pairs={{0,2},{2,0},{4,6},{6,4},{8,10},{10,8},{12,14},{14,12},{16,18},{18,... | collective-permute-start | bytes 5308424 | tf_op jit(solution)/shard_map/ppermute | solution.py:664
  568.0 28.6 %copy-start.22 = (bf16[1,1024,864]{1,2,0:T(8,128)(2,1)S(1)}, bf16[1,1024,864]{1,2,0:T(8,128)(2,1)}, u32[]{:S(2)}) copy-start(bf16[1,1024,864]{1,2,0:T(8,128)(2,1)} %copy.71) | copy-start | bytes 5308420
  572.5 3.7 collective-permute-start.30
  576.2 47.9 %collective-permute-start.28 = (bf16[512,1152]{1,0:T(8,128)(2,1)}, bf16[512,1152]{1,0:T(8,128)(2,1)}, u32[]{:S(2)}, u32[]{:S(2)}) collective-permute-start(bf16[512,1152]{1,0:T(8,128)(2,1)} %slice.149), channel_id=1, source_target_pairs={{0,1},{1,0},{2,3},{3,2},{4,5},{5,4},{6,7},{7,6},{8,9},{9,8},{10,11... | collective-permute-start | bytes 3538952 | tf_op jit(solution)/shard_map/ppermute | solution.py:664
  596.6 34.0 %collective-permute-start.33 = (bf16[1024,864]{0,1:T(8,128)(2,1)S(1)}, bf16[1024,864]{0,1:T(8,128)(2,1)}, u32[]{:S(2)}, u32[]{:S(2)}) collective-permute-start(bf16[1024,864]{0,1:T(8,128)(2,1)S(1)} %bitcast.221), channel_id=1, source_target_pairs={{0,2},{2,0},{4,6},{6,4},{8,10},{10,8},{12,14},{14,12},{16,18},{18,... | collective-permute-start | bytes 5308424 | tf_op jit(solution)/shard_map/ppermute | solution.py:664
  617.9 5.0 collective-permute-start.43
  622.9 60.8 %collective-permute-start.49 = (bf16[2,2,144,2304]{3,2,1,0:T(8,128)(2,1)}, bf16[2,2,144,2304]{3,2,1,0:T(8,128)(2,1)}, u32[]{:S(2)}, u32[]{:S(2)}) collective-permute-start(bf16[2,2,144,2304]{3,2,1,0:T(8,128)(2,1)} %dynamic-slice_bitcast_fusion), channel_id=1, source_target_pairs={{0,4},{2,6},{4,0},{6,2},{8,12},{10,14},{12,8},{14,10},{16,20},{18,... | collective-permute-start | bytes 7962632 | tf_op jit(solution)/shard_map/ppermute | solution.py:664
  624.1 62.9 %collective-permute-start.44 = (bf16[2,2,144,2304]{3,2,1,0:T(8,128)(2,1)}, bf16[2,2,144,2304]{3,2,1,0:T(8,128)(2,1)}, u32[]{:S(2)}, u32[]{:S(2)}) collective-permute-start(bf16[2,2,144,2304]{3,2,1,0:T(8,128)(2,1)} %dynamic-slice_bitcast_fusion.1), channel_id=1, source_target_pairs={{0,8},{2,10},{4,12},{6,14},{8,0},{10,2},{12,4},{14,6},{16,24},{18,... | collective-permute-start | bytes 7962632 | tf_op jit(solution)/shard_map/ppermute | solution.py:664
  649.0 38.0 %slice-start = ((s8[5308416]{0:T(1024)(128)(4,1)}), s8[4194304]{0:T(1024)(128)(4,1)S(1)}, s32[]{:S(2)}) async-start(s8[5308416]{0:T(1024)(128)(4,1)} %bitcast.207), calls=%async_computation | async-start | bytes 8388608
  650.9 36.2 %slice-start.1 = ((s8[5308416]{0:T(1024)(128)(4,1)}), s8[1114112]{0:T(1024)(128)(4,1)S(1)}, s32[]{:S(2)}) async-start(s8[5308416]{0:T(1024)(128)(4,1)} %bitcast.207), calls=%async_computation.1 | async-start | bytes 2228224
  650.9 76.9 %collective-permute-start.34 = (bf16[2,2,144,1728]{3,2,1,0:T(8,128)(2,1)S(1)}, bf16[2,2,144,1728]{3,2,1,0:T(8,128)(2,1)S(1)}, u32[]{:S(2)}, u32[]{:S(2)}) collective-permute-start(bf16[2,2,144,1728]{3,2,1,0:T(8,128)(2,1)S(1)} %dynamic-slice_bitcast_fusion.10), channel_id=1, source_target_pairs={{0,4},{2,6},{4,0},{6,2},{8,12},{10,14},{12,8},{14,10},{16,20},{18,... | collective-permute-start | bytes 5971976 | tf_op jit(solution)/shard_map/ppermute | solution.py:664
  686.9 40.9 %copy-start.6 = (bf16[1152,1728]{1,0:T(8,128)(2,1)S(1)}, bf16[1152,1728]{1,0:T(8,128)(2,1)}, u32[]{:S(2)}) copy-start(bf16[1152,1728]{1,0:T(8,128)(2,1)} %copy.72) | copy-start | bytes 11943940
  687.0 41.5 %collective-permute-start.50 = (bf16[2,144,2304]{2,1,0:T(8,128)(2,1)S(1)}, bf16[2,144,2304]{2,1,0:T(8,128)(2,1)S(1)}, u32[]{:S(2)}, u32[]{:S(2)}) collective-permute-start(bf16[2,144,2304]{2,1,0:T(8,128)(2,1)S(1)} %dynamic-slice_bitcast_fusion.13), channel_id=1, source_target_pairs={{0,8},{2,10},{4,12},{6,14},{8,0},{10,2},{12,4},{14,6},{16,24},{18,... | collective-permute-start | bytes 3981320 | tf_op jit(solution)/shard_map/ppermute | solution.py:664
  689.8 65.0 %collective-permute-start.45 = (bf16[2,144,2304]{2,1,0:T(8,128)(2,1)S(1)}, bf16[2,144,2304]{2,1,0:T(8,128)(2,1)S(1)}, u32[]{:S(2)}, u32[]{:S(2)}) collective-permute-start(bf16[2,144,2304]{2,1,0:T(8,128)(2,1)S(1)} %dynamic-slice_bitcast_fusion.14), channel_id=1, source_target_pairs={{0,4},{2,6},{4,0},{6,2},{8,12},{10,14},{12,8},{14,10},{16,20},{18,... | collective-permute-start | bytes 3981320 | tf_op jit(solution)/shard_map/ppermute | solution.py:664
  728.4 64.3 %collective-permute-start.35 = (bf16[2,144,1728]{2,1,0:T(8,128)(2,1)S(1)}, bf16[2,144,1728]{2,1,0:T(8,128)(2,1)S(1)}, u32[]{:S(2)}, u32[]{:S(2)}) collective-permute-start(bf16[2,144,1728]{2,1,0:T(8,128)(2,1)S(1)} %dynamic-slice_bitcast_fusion.22), channel_id=1, source_target_pairs={{0,8},{2,10},{4,12},{6,14},{8,0},{10,2},{12,4},{14,6},{16,24},{18,... | collective-permute-start | bytes 2985992 | tf_op jit(solution)/shard_map/ppermute | solution.py:664
  728.9 37.1 %collective-permute-start.51 = (bf16[144,2304]{1,0:T(8,128)(2,1)S(1)}, bf16[144,2304]{1,0:T(8,128)(2,1)S(1)}, u32[]{:S(2)}, u32[]{:S(2)}) collective-permute-start(bf16[144,2304]{1,0:T(8,128)(2,1)S(1)} %dynamic-slice_bitcast_fusion.23), channel_id=1, source_target_pairs={{0,16},{2,18},{4,20},{6,22},{8,24},{10,26},{12,28},{14,30},{16,0},... | collective-permute-start | bytes 1990664 | tf_op jit(solution)/shard_map/ppermute | solution.py:664
  755.2 35.8 %collective-permute-start.46 = (bf16[144,2304]{1,0:T(8,128)(2,1)S(1)}, bf16[144,2304]{1,0:T(8,128)(2,1)S(1)}, u32[]{:S(2)}, u32[]{:S(2)}) collective-permute-start(bf16[144,2304]{1,0:T(8,128)(2,1)S(1)} %dynamic-slice_bitcast_fusion.24), channel_id=1, source_target_pairs={{0,16},{2,18},{4,20},{6,22},{8,24},{10,26},{12,28},{14,30},{16,0},... | collective-permute-start | bytes 1990664 | tf_op jit(solution)/shard_map/ppermute | solution.py:664
  766.2 26.9 %collective-permute-start.52 = (bf16[144,1152]{1,0:T(8,128)(2,1)S(1)}, bf16[144,1152]{1,0:T(8,128)(2,1)S(1)}, u32[]{:S(2)}, u32[]{:S(2)}) collective-permute-start(bf16[144,1152]{1,0:T(8,128)(2,1)S(1)} %slice.133), channel_id=1, source_target_pairs={{0,1},{1,0},{2,3},{3,2},{4,5},{5,4},{6,7},{7,6},{8,9},{9,8},{10,11... | collective-permute-start | bytes 995336 | tf_op jit(solution)/shard_map/ppermute | solution.py:664
  791.1 9.8 %collective-permute-start.47 = (bf16[144,1152]{1,0:T(8,128)(2,1)S(1)}, bf16[144,1152]{1,0:T(8,128)(2,1)S(1)}, u32[]{:S(2)}, u32[]{:S(2)}) collective-permute-start(bf16[144,1152]{1,0:T(8,128)(2,1)S(1)} %slice.130), channel_id=1, source_target_pairs={{0,1},{1,0},{2,3},{3,2},{4,5},{5,4},{6,7},{7,6},{8,9},{9,8},{10,11... | collective-permute-start | bytes 995336 | tf_op jit(solution)/shard_map/ppermute | solution.py:664
  793.0 25.4 %collective-permute-start.36 = (bf16[144,1728]{1,0:T(8,128)(2,1)S(1)}, bf16[144,1728]{1,0:T(8,128)(2,1)S(1)}, u32[]{:S(2)}, u32[]{:S(2)}) collective-permute-start(bf16[144,1728]{1,0:T(8,128)(2,1)S(1)} %dynamic-slice_bitcast_fusion.26), channel_id=1, source_target_pairs={{0,16},{2,18},{4,20},{6,22},{8,24},{10,26},{12,28},{14,30},{16,0},... | collective-permute-start | bytes 1493000 | tf_op jit(solution)/shard_map/ppermute | solution.py:664
  793.2 33.1 %collective-permute-start.53 = (bf16[72,1152]{1,0:T(8,128)(2,1)S(1)}, bf16[72,1152]{1,0:T(8,128)(2,1)S(1)}, u32[]{:S(2)}, u32[]{:S(2)}) collective-permute-start(bf16[72,1152]{1,0:T(8,128)(2,1)S(1)} %get-tuple-element.172), channel_id=1, source_target_pairs={{0,2},{2,0},{4,6},{6,4},{8,10},{10,8},{12,14},{14,12},{16,18},{18,... | collective-permute-start | bytes 497672 | tf_op jit(solution)/shard_map/ppermute | solution.py:664
  801.1 18.2 %collective-permute-start.48 = (bf16[72,1152]{1,0:T(8,128)(2,1)S(1)}, bf16[72,1152]{1,0:T(8,128)(2,1)S(1)}, u32[]{:S(2)}, u32[]{:S(2)}) collective-permute-start(bf16[72,1152]{1,0:T(8,128)(2,1)S(1)} %get-tuple-element.174), channel_id=1, source_target_pairs={{0,2},{2,0},{4,6},{6,4},{8,10},{10,8},{12,14},{14,12},{16,18},{18,... | collective-permute-start | bytes 497672 | tf_op jit(solution)/shard_map/ppermute | solution.py:664
  818.7 7.0 collective-permute-start.37
  826.3 1.5 collective-permute-start.38
  (41 other events, 321.5 us)

commit v2 on v1

--- a/solution.py
+++ b/solution.py
@@ -452,6 +452,10 @@
 VMEM_BYTES = 60 * 2**20
 
 
+def cost(weight):
+    return pl.CostEstimate(flops=weight * 50 * 10**8, bytes_accessed=10**5, transcendentals=0)
+
+
 def dot_dims(left, right, left_dim, right_dim):
     return lax.dot_general(
         left, right, (((left_dim,), (right_dim,)), ((), ())), preferred_element_type=F32
@@ -493,20 +497,16 @@
             jax.ShapeDtypeStruct((heads, tokens), F32),
         ],
         compiler_params=pltpu.CompilerParams(vmem_limit_bytes=VMEM_BYTES),
-        cost_estimate=pl.CostEstimate(
-            flops=4 * heads * tokens * tokens * 256, bytes_accessed=8 * tokens * width,
-            transcendentals=heads * tokens * tokens,
-        ),
+        cost_estimate=cost(18),
     )(qkv)
 
 
 def attend_back_kernel(
-    heads, key_rows, steps,
-    qkv_ref, out_ref, grad_ref, logsum_ref, grads_ref, pairs_ref, dot_ref, query_ref,
+    heads, key_rows, steps, core_ref,
+    qkv_ref, out_ref, grad_ref, logsum_ref, grads_ref, sent_ref, kept_ref, dot_ref, query_ref,
 ):
     step = pl.program_id(0)
     width = heads * HEAD_DIM
-    half = heads // 2
     rows = pl.ds(pl.multiple_of(step * key_rows, key_rows), key_rows)
 
     @pl.when(step == 0)
@@ -522,7 +522,6 @@
 
     def store(part, head, rows, value):
         grads_ref[rows, head_slice(part, head, width)] = value
-        pairs_ref[head // half, rows, head_slice(part, head % half, half * HEAD_DIM)] = value
 
     for head in range(heads):
         queries = qkv_ref[:, head_slice(0, head, width)]
@@ -542,35 +541,50 @@
     def _():
         for head in range(heads):
             store(0, head, slice(None), (query_ref[head] * SCORE_SCALE).T.astype(BF16))
-
-
-def attend_back(qkv, attended, grad_attended, logsum, key_rows=512):
+        half = width // 2
+        for first in range(2):
+
+            @pl.when(core_ref[0] == first)
+            def _():
+                for part in range(3):
+                    here, there = (part * width + side * half for side in (first, 1 - first))
+                    to = slice(part * half, (part + 1) * half)
+                    kept_ref[:, to] = grads_ref[:, here : here + half]
+                    sent_ref[:, to] = grads_ref[:, there : there + half]
+                rest = slice(3 * half, kept_ref.shape[1])
+                kept_ref[:, rest] = jnp.zeros_like(kept_ref[:, rest])
+                sent_ref[:, rest] = jnp.zeros_like(sent_ref[:, rest])
+
+
+def attend_back(core, qkv, attended, grad_attended, logsum, key_rows=512):
     tokens, width = attended.shape
     heads = width // HEAD_DIM
     steps = tokens // key_rows
-    whole = lambda *shape: pl.BlockSpec(shape, lambda i: (0,) * len(shape))
+    whole = lambda *shape: pl.BlockSpec(shape, lambda i, core_ref: (0,) * len(shape))
+    half = (tokens, -(-3 * width // 256) * 128)
     return pl.pallas_call(
         functools.partial(attend_back_kernel, heads, key_rows, steps),
-        grid=(steps,),
-        in_specs=[
-            whole(tokens, 3 * width), whole(tokens, width), whole(tokens, width),
-            whole(heads, tokens),
-        ],
-        out_specs=[whole(tokens, 3 * width), whole(2, tokens, 3 * width // 2)],
+        grid_spec=pltpu.PrefetchScalarGridSpec(
+            num_scalar_prefetch=1,
+            grid=(steps,),
+            in_specs=[
+                whole(tokens, 3 * width), whole(tokens, width), whole(tokens, width),
+                whole(heads, tokens),
+            ],
+            out_specs=[whole(tokens, 3 * width), whole(*half), whole(*half)],
+            scratch_shapes=[
+                pltpu.VMEM((heads, tokens), F32),
+                pltpu.VMEM((heads, HEAD_DIM, tokens), F32),
+            ],
+        ),
         out_shape=[
             jax.ShapeDtypeStruct((tokens, 3 * width), BF16),
-            jax.ShapeDtypeStruct((2, tokens, 3 * width // 2), BF16),
-        ],
-        scratch_shapes=[
-            pltpu.VMEM((heads, tokens), F32),
-            pltpu.VMEM((heads, HEAD_DIM, tokens), F32),
+            jax.ShapeDtypeStruct(half, BF16),
+            jax.ShapeDtypeStruct(half, BF16),
         ],
         compiler_params=pltpu.CompilerParams(vmem_limit_bytes=VMEM_BYTES),
-        cost_estimate=pl.CostEstimate(
-            flops=10 * heads * tokens * tokens * 256, bytes_accessed=22 * tokens * width,
-            transcendentals=heads * tokens * tokens,
-        ),
-    )(qkv, attended, grad_attended, logsum)
+        cost_estimate=cost(32),
+    )(core, qkv, attended, grad_attended, logsum)
 
 
 GELU_OUTER = math.sqrt(2 / math.pi)
@@ -586,16 +600,16 @@
 
 
 def feed_kernel(
-    token_rows, carried, normed_ref, grad_ref, up_ref, bias_ref, down_ref, *refs
+    token_rows, carried, core_ref, normed_ref, grad_ref, up_ref, bias_ref, down_ref, *refs
 ):
     if carried:
         branch_in, normed_in = refs[:2]
         refs = refs[2:]
-    branch_ref, back_ref, hidden_ref, pre_ref, bias_grad_ref = refs
+    branch_ref, back_ref, hidden_sent, hidden_kept, pre_sent, pre_kept, bias_grad_ref = refs
     chunk = pl.program_id(0)
     bias_grad_ref[...] = jnp.zeros_like(bias_grad_ref)
 
-    def block(index, _):
+    def block(hidden_ref, pre_ref, index, _):
         rows = pl.ds(pl.multiple_of(index * token_rows, token_rows), token_rows)
         pre = jnp.dot(normed_ref[rows, :], up_ref[...], preferred_element_type=F32)
         grad_hidden = dot_dims(grad_ref[rows, :], down_ref[...], 1, 1)
@@ -603,57 +617,353 @@
         hidden = hidden.astype(BF16)
         grad_pre = (grad_hidden * slope).astype(BF16)
         bias_grad_ref[...] += jnp.sum(grad_pre.astype(F32), 0, keepdims=True)
-        hidden_ref[0, rows, :] = hidden
-        pre_ref[0, rows, :] = grad_pre
+        hidden_ref[rows, :] = hidden
+        pre_ref[rows, :] = grad_pre
         branch = jnp.dot(hidden, down_ref[...], preferred_element_type=F32)
         back = dot_dims(grad_pre, up_ref[...], 1, 1)
-
-        @pl.when(chunk == 0)
-        def _():
+        if hidden_ref is hidden_kept:
+            branch_ref[rows, :] += branch
+            back_ref[rows, :] += back
+        else:
             branch_ref[rows, :] = branch + branch_in[rows, :] if carried else branch
             back_ref[rows, :] = back + normed_in[rows, :] if carried else back
-
-        @pl.when(chunk > 0)
+        return 0
+
+    for step, refs_here in enumerate(((hidden_sent, pre_sent), (hidden_kept, pre_kept))):
+
+        @pl.when(chunk == step)
         def _():
-            branch_ref[rows, :] += branch
-            back_ref[rows, :] += back
-
-        return 0
-
-    lax.fori_loop(0, normed_ref.shape[0] // token_rows, block, 0)
-
-
-def feed(normed, grad, up, bias, down, carried=(), token_rows=256):
+            lax.fori_loop(
+                0, normed_ref.shape[0] // token_rows, functools.partial(block, *refs_here), 0
+            )
+
+
+def feed(core, normed, grad, up, bias, down, carried=(), token_rows=256):
     tokens, model_width = normed.shape
     hidden_here = up.shape[1]
     width = hidden_here // 2
-    whole = lambda: pl.BlockSpec((tokens, model_width), lambda j: (0, 0))
-    pair = lambda: pl.BlockSpec((1, tokens, width), lambda j: (j, 0, 0))
+    chunk = lambda j, core_ref: lax.rem(j + 1 + core_ref[0], 2)
+    single = pl.Buffered(1)
+    whole = lambda: pl.BlockSpec((tokens, model_width), lambda j, c: (0, 0), pipeline_mode=single)
+    part = lambda: pl.BlockSpec((tokens, width), lambda j, c: (0, 0), pipeline_mode=single)
     return pl.pallas_call(
         functools.partial(feed_kernel, token_rows, len(carried) > 0),
-        grid=(2,),
+        grid_spec=pltpu.PrefetchScalarGridSpec(
+            num_scalar_prefetch=1,
+            grid=(2,),
+            in_specs=[
+                whole(), whole(),
+                pl.BlockSpec((model_width, width), lambda j, c: (0, chunk(j, c))),
+                pl.BlockSpec((1, width), lambda j, c: (0, chunk(j, c))),
+                pl.BlockSpec((width, model_width), lambda j, c: (chunk(j, c), 0)),
+            ] + [whole() for _ in carried],
+            out_specs=[
+                whole(), whole(), part(), part(), part(), part(),
+                pl.BlockSpec((1, width), lambda j, c: (0, chunk(j, c))),
+            ],
+        ),
+        out_shape=[jax.ShapeDtypeStruct((tokens, model_width), F32)] * 2
+        + [jax.ShapeDtypeStruct((tokens, width), BF16)] * 4
+        + [jax.ShapeDtypeStruct((1, hidden_here), F32)],
+        compiler_params=pltpu.CompilerParams(vmem_limit_bytes=VMEM_BYTES),
+        cost_estimate=cost(44),
+    )(core, normed, grad, up, bias, down, *carried)
+
+
+def weight_grad_kernel(chunks, blocks, where_ref, left_mine, left_peer, *refs):
+    rights, outs, left_ref = refs[: 2 * chunks], refs[2 * chunks : -1], refs[-1]
+    tokens, model_width = left_mine.shape
+    rows = model_width // blocks
+    for first, left in ((0, left_mine), (tokens, left_peer)):
+        turned = left[...].T
+        for block in range(blocks):
+            to = pl.ds(pl.multiple_of(where_ref[block] * rows, rows), rows)
+            left_ref[to, first : first + tokens] = turned[block * rows : (block + 1) * rows]
+    for chunk in range(chunks):
+        for part in range(2):
+            half = slice(part * model_width // 2, (part + 1) * model_width // 2)
+            mine, peer = rights[2 * chunk : 2 * chunk + 2]
+            total = jnp.dot(left_ref[half, :tokens], mine[...], preferred_element_type=F32)
+            total += jnp.dot(left_ref[half, tokens:], peer[...], preferred_element_type=F32)
+            total = total.astype(BF16)
+            for block in range(blocks // 2):
+                outs[2 * chunk + part][block] = total[block * rows : (block + 1) * rows]
+
+
+def weight_grad(where, left_mine, left_peer, *rights):
+    tokens, model_width = left_mine.shape
+    blocks = where.shape[0]
+    chunks = len(rights) // 2
+    width = rights[0].shape[1]
+    out = jax.ShapeDtypeStruct((blocks // 2, model_width // blocks, width), BF16)
+    whole = lambda value: pl.BlockSpec(value.shape, lambda j, w: (0,) * len(value.shape))
+    return pl.pallas_call(
+        functools.partial(weight_grad_kernel, chunks, blocks),
+        grid_spec=pltpu.PrefetchScalarGridSpec(
+            num_scalar_prefetch=1,
+            grid=(1,),
+            in_specs=[whole(value) for value in (left_mine, left_peer) + rights],
+            out_specs=[whole(out)] * (2 * chunks),
+            scratch_shapes=[pltpu.VMEM((model_width, 2 * tokens), BF16)],
+        ),
+        out_shape=[out] * (2 * chunks),
+        compiler_params=pltpu.CompilerParams(vmem_limit_bytes=VMEM_BYTES),
+        cost_estimate=cost(13),
+    )(where, left_mine, left_peer, *rights)
+
+
+def add_split_kernel(base_ref, kept_ref, received_ref, *out_refs):
+    for place, out_ref in enumerate(out_refs):
+        block = lax.bitwise_xor(base_ref[0], place)
+        total = kept_ref[block].astype(F32) + received_ref[block].astype(F32)
+        out_ref[...] = total.astype(BF16)
+
+
+def add_split(base, kept, received):
+    blocks, rows, width = kept.shape
+    out = jax.ShapeDtypeStruct((rows, width), BF16)
+    whole = lambda *shape: pl.BlockSpec(shape, lambda j, b: (0,) * len(shape))
+    return pl.pallas_call(
+        add_split_kernel,
+        grid_spec=pltpu.PrefetchScalarGridSpec(
+            num_scalar_prefetch=1, grid=(1,),
+            in_specs=[whole(*kept.shape)] * 2, out_specs=[whole(rows, width)] * blocks,
+        ),
+        out_shape=[out] * blocks,
+        compiler_params=pltpu.CompilerParams(vmem_limit_bytes=VMEM_BYTES),
+        cost_estimate=cost(2),
+    )(base, kept, received)
+
+
+def project_kernel(with_norm, *refs):
+    refs = refs[2:] if with_norm > 1 else refs
+    if with_norm:
+        tokens_ref, rows_ref, weight_ref, offset_ref, normed_ref, out_ref = refs
+        norm, _ = normalize(tokens_ref[...].astype(F32))
+        normed = (norm * (1.0 + rows_ref[1:2]) + rows_ref[0:1]).astype(BF16)
+        normed_ref[...] = normed
+    else:
+        tokens_ref, weight_ref, offset_ref, out_ref = refs
+        normed = tokens_ref[...]
+    out = jnp.dot(normed, weight_ref[...], preferred_element_type=F32) + offset_ref[...]
+    out_ref[...] = out.astype(BF16)
+
+
+def constant_block(shape):
+    return pl.BlockSpec(shape, lambda i: (0,) * len(shape), pipeline_mode=pl.Buffered(1))
+
+
+def row_blocks(rows, width, first=0):
+    return pl.BlockSpec((rows, width), lambda i: (i + first, 0))
+
+
+def project(normed, weight, offset, rows=256):
+    tokens, model_width = normed.shape
+    width = weight.shape[1]
+    return pl.pallas_call(
+        functools.partial(project_kernel, 0),
+        grid=(tokens // rows,),
         in_specs=[
-            whole(), whole(),
-            pl.BlockSpec((model_width, width), lambda j: (0, j)),
-            pl.BlockSpec((1, width), lambda j: (0, j)),
-            pl.BlockSpec((width, model_width), lambda j: (j, 0)),
-        ] + [whole() for _ in carried],
+            row_blocks(rows, model_width), constant_block(weight.shape), constant_block((1, width)),
+        ],
+        out_specs=row_blocks(rows, width),
+        out_shape=jax.ShapeDtypeStruct((tokens, width), BF16),
+        compiler_params=pltpu.CompilerParams(vmem_limit_bytes=VMEM_BYTES),
+        cost_estimate=cost(9),
+    )(normed, weight, offset)
+
+
+def normed_project(half, shifts, weight, offset, filled=None, rows=256):
+    half_tokens, model_width = half.shape
+    width = weight.shape[1]
+    first = 0 if filled is None else half_tokens // rows
+    held = [] if filled is None else list(filled)
+    return pl.pallas_call(
+        functools.partial(project_kernel, 1 if filled is None else 2),
+        grid=(half_tokens // rows,),
+        in_specs=[pl.BlockSpec(memory_space=pl.ANY)] * len(held)
+        + [
+            row_blocks(rows, model_width), constant_block(shifts.shape),
+            constant_block(weight.shape), constant_block((1, width)),
+        ],
+        out_specs=[row_blocks(rows, model_width, first), row_blocks(rows, width, first)],
+        out_shape=[
+            jax.ShapeDtypeStruct((2 * half_tokens, model_width), BF16),
+            jax.ShapeDtypeStruct((2 * half_tokens, width), BF16),
+        ],
+        input_output_aliases={0: 0, 1: 1} if held else {},
+        compiler_params=pltpu.CompilerParams(vmem_limit_bytes=VMEM_BYTES),
+        cost_estimate=cost(7),
+    )(*held, half, shifts, weight, offset)
+
+
+def halves(rows, width, blocks):
+    half = blocks // 2
+    return [
+        pl.BlockSpec((rows, width), lambda i: (jnp.minimum(i, half - 1), 0)),
+        pl.BlockSpec((rows, width), lambda i: (jnp.maximum(i - half, 0), 0)),
+    ]
+
+
+def merge_kernel(
+    blocks, own_ref, other_ref, weight_own, weight_other, first_ref, second_ref, grad_ref, rows_ref,
+    branch_ref, mid_ref, normed_ref, grad_b2_ref,
+):
+    gate1, bias, shift2, scale2, gate2 = (rows_ref[row : row + 1] for row in range(5))
+    stream = jnp.where(pl.program_id(0) < blocks // 2, first_ref[...], second_ref[...])
+    branch = jnp.dot(own_ref[...], weight_own[...], preferred_element_type=F32)
+    branch += jnp.dot(other_ref[...], weight_other[...], preferred_element_type=F32)
+    branch += bias
+    branch_ref[...] = branch.astype(BF16)
+    mid = stream.astype(F32) + gate1 * branch
+    mid_ref[...] = mid
+    norm, _ = normalize(mid)
+    normed_ref[...] = (norm * (1.0 + scale2) + shift2).astype(BF16)
+    grad_b2_ref[...] = (gate2 * grad_ref[...].astype(F32)).astype(BF16)
+
+
+def merge(own, other, weight_own, weight_other, first, second, grad, vectors, rows=256):
+    tokens, width = own.shape
+    model_width = weight_own.shape[1]
+    blocks = tokens // rows
+    part = lambda: row_blocks(rows, width)
+    full = lambda: row_blocks(rows, model_width)
+    shape = lambda kind: jax.ShapeDtypeStruct((tokens, model_width), kind)
+    return pl.pallas_call(
+        functools.partial(merge_kernel, blocks),
+        grid=(blocks,),
+        in_specs=[
+            part(), part(), constant_block(weight_own.shape), constant_block(weight_other.shape),
+            *halves(rows, model_width, blocks), full(), constant_block(vectors.shape),
+        ],
+        out_specs=[full(), full(), full(), full()],
+        out_shape=[shape(BF16), shape(F32), shape(BF16), shape(BF16)],
+        compiler_params=pltpu.CompilerParams(vmem_limit_bytes=VMEM_BYTES),
+        cost_estimate=cost(11),
+    )(own, other, weight_own, weight_other, first, second, grad, vectors)
+
+
+def add_row_sums(sums_ref, *values):
+    @pl.when(pl.program_id(0) == 0)
+    def _():
+        sums_ref[...] = jnp.zeros_like(sums_ref)
+
+    for row, value in enumerate(values):
+        sums_ref[row : row + 1] += jnp.sum(value, 0, keepdims=True)
+
+
+def middle_back_kernel(
+    blocks, branch2_ref, back_ref, mid_ref, branch1_ref, grad_ref, grad_b2_ref, weight_own, weight_other,
+    rows_ref, kept_ref, sent_ref, grad_mid_ref, grad_b1_ref, att_own_ref, att_other_ref, sums_ref,
+):
+    gate1, bias, scale2, gate2 = (rows_ref[row : row + 1] for row in range(4))
+    block = pl.program_id(0)
+    grad = grad_ref[...].astype(F32)
+    mid = mid_ref[...]
+    branch2 = branch2_ref[...] + bias
+    output = (mid + gate2 * branch2).astype(BF16)
+
+    @pl.when(block < blocks // 2)
+    def _():
+        kept_ref[...] = output
+
+    @pl.when(block >= blocks // 2)
+    def _():
+        sent_ref[...] = output
+
+    norm, inverse = normalize(mid)
+    back = back_ref[...]
+    grad_mid = grad + normalize_back(back * (1.0 + scale2), norm, inverse)
+    grad_mid_ref[...] = grad_mid
+    grad_b1 = (gate1 * grad_mid).astype(BF16)
+    grad_b1_ref[...] = grad_b1
+    att_own_ref[...] = dot_dims(grad_b1, weight_own[...], 1, 1).astype(BF16)
+    att_other_ref[...] = dot_dims(grad_b1, weight_other[...], 1, 1).astype(BF16)
+    add_row_sums(
+        sums_ref, grad * branch2, grad_b2_ref[...].astype(F32), back, back * norm,
+        grad_mid * branch1_ref[...].astype(F32), grad_b1.astype(F32),
+    )
+
+
+def middle_back(
+    branch2, back, mid, branch1, grad, grad_b2, weight_own, weight_other, vectors, rows=256
+):
+    tokens, model_width = mid.shape
+    width = weight_own.shape[0]
+    blocks = tokens // rows
+    full = lambda: row_blocks(rows, model_width)
+    shape = lambda count, columns, kind: jax.ShapeDtypeStruct((count, columns), kind)
+    return pl.pallas_call(
+        functools.partial(middle_back_kernel, blocks),
+        grid=(blocks,),
+        in_specs=[full()] * 6
+        + [
+            constant_block(weight_own.shape), constant_block(weight_other.shape),
+            constant_block(vectors.shape),
+        ],
         out_specs=[
-            whole(), whole(), pair(), pair(), pl.BlockSpec((1, width), lambda j: (0, j)),
+            *halves(rows, model_width, blocks), full(), full(), row_blocks(rows, width),
+            row_blocks(rows, width), constant_block((8, model_width)),
         ],
         out_shape=[
-            jax.ShapeDtypeStruct((tokens, model_width), F32),
-            jax.ShapeDtypeStruct((tokens, model_width), F32),
-            jax.ShapeDtypeStruct((2, tokens, width), BF16),
-            jax.ShapeDtypeStruct((2, tokens, width), BF16),
-            jax.ShapeDtypeStruct((1, hidden_here), F32),
+            shape(tokens // 2, model_width, BF16), shape(tokens // 2, model_width, BF16),
+            shape(tokens, model_width, F32), shape(tokens, model_width, BF16),
+            shape(tokens, width, BF16), shape(tokens, width, BF16), shape(8, model_width, F32),
         ],
         compiler_params=pltpu.CompilerParams(vmem_limit_bytes=VMEM_BYTES),
-        cost_estimate=pl.CostEstimate(
-            flops=8 * tokens * model_width * hidden_here,
-            bytes_accessed=30 * tokens * model_width, transcendentals=tokens * hidden_here,
-        ),
-    )(normed, grad, up, bias, down, *carried)
+        cost_estimate=cost(17),
+    )(branch2, back, mid, branch1, grad, grad_b2, weight_own, weight_other, vectors)
+
+
+def first_back_kernel(
+    blocks, own_ref, other_ref, weight_own, weight_other, first_ref, second_ref, grad_mid_ref, rows_ref,
+    kept_ref, sent_ref, sums_ref, own_sums_ref, other_sums_ref,
+):
+    block = pl.program_id(0)
+    stream = jnp.where(block < blocks // 2, first_ref[...], second_ref[...])
+    own, other = own_ref[...], other_ref[...]
+    grad = dot_dims(own, weight_own[...], 1, 1) + dot_dims(other, weight_other[...], 1, 1)
+    norm, inverse = normalize(stream.astype(F32))
+    total = grad_mid_ref[...] + normalize_back(grad * (1.0 + rows_ref[0:1]), norm, inverse)
+
+    @pl.when(block < blocks // 2)
+    def _():
+        kept_ref[...] = total
+
+    @pl.when(block >= blocks // 2)
+    def _():
+        sent_ref[...] = total.astype(BF16)
+
+    add_row_sums(sums_ref, grad, grad * norm)
+    add_row_sums(own_sums_ref, own.astype(F32))
+    add_row_sums(other_sums_ref, other.astype(F32))
+
+
+def first_back(own, other, weight_own, weight_other, first, second, grad_mid, vectors, rows=256):
+    tokens, model_width = grad_mid.shape
+    width = own.shape[1]
+    blocks = tokens // rows
+    full = lambda: row_blocks(rows, model_width)
+    part = lambda: row_blocks(rows, width)
+    shape = jax.ShapeDtypeStruct
+    return pl.pallas_call(
+        functools.partial(first_back_kernel, blocks),
+        grid=(blocks,),
+        in_specs=[
+            part(), part(), constant_block(weight_own.shape), constant_block(weight_other.shape),
+            *halves(rows, model_width, blocks), full(), constant_block(vectors.shape),
+        ],
+        out_specs=[
+            *halves(rows, model_width, blocks), constant_block((8, model_width)),
+            constant_block((8, width)), constant_block((8, width)),
+        ],
+        out_shape=[
+            shape((tokens // 2, model_width), F32), shape((tokens // 2, model_width), BF16),
+            shape((8, model_width), F32), shape((8, width), F32), shape((8, width), F32),
+        ],
+        compiler_params=pltpu.CompilerParams(vmem_limit_bytes=VMEM_BYTES),
+        cost_estimate=cost(21),
+    )(own, other, weight_own, weight_other, first, second, grad_mid, vectors)
 
 
 def bit_pairs(size, bit):
@@ -669,7 +979,7 @@
 
 
 def after(values, *others):
-    return lax.optimization_barrier((values,) + others)[0]
+    return lax.optimization_barrier((values, others))[0]
 
 
 def place(first, second, index, axis=0):
@@ -680,35 +990,92 @@
     )
 
 
-def fetch_other(weight, place_bits, behind=()):
-    near, core = place_bits
-    pieces = weight.shape[0] // 4
-    first = lax.dynamic_slice_in_dim(weight, (2 * near + core) * pieces, pieces, 0)
-    got = swap(after(first, *behind), "tensor", 1)
-    got_near = swap(got, "dp", 4)
-    got_core = swap(got, "dp", 1)
-    got_both = swap(got_near, "dp", 1)
-    whole = jnp.zeros(weight.shape, weight.dtype)
-    for piece, near_here, core_here in (
-        (got, near, core), (got_near, 1 - near, core),
-        (got_core, near, 1 - core), (got_both, 1 - near, 1 - core),
-    ):
-        whole = lax.dynamic_update_slice_in_dim(
-            whole, piece, (2 * near_here + core_here) * pieces, 0
+def cut_kernel(sizes, starts_ref, *refs):
+    count = len(sizes)
+    semaphores = refs[-1]
+    copies = []
+    for index, size in enumerate(sizes):
+        rows = pl.ds(pl.multiple_of(starts_ref[index] * size, size), size)
+        copies.append(
+            pltpu.make_async_copy(
+                refs[index].at[rows], refs[count + index], semaphores.at[index]
+            )
         )
-    return whole, got
-
-
-def scatter_rows(values, bits, order):
-    steps = {"far": (bits[0], 8), "near": (bits[1], 4), "x": (bits[2], 2)}
-    axes = ["far", "near", "x"]
-    for name in order:
-        index, mask = steps[name]
-        axis = axes.index(name)
-        axes.remove(name)
-        sent = swap(pick(values, 1 - index, axis), "dp", mask)
-        kept = pick(values, index, axis)
-        values = (kept.astype(F32) + sent.astype(F32)).astype(BF16)
+    for copy in copies:
+        copy.start()
+    for copy in copies:
+        copy.wait()
+
+
+def cut(values, places, sizes):
+    return pl.pallas_call(
+        functools.partial(cut_kernel, sizes),
+        grid_spec=pltpu.PrefetchScalarGridSpec(
+            num_scalar_prefetch=1,
+            grid=(1,),
+            in_specs=[pl.BlockSpec(memory_space=pl.ANY)] * len(sizes),
+            out_specs=[pl.BlockSpec(memory_space=pltpu.VMEM)] * len(sizes),
+            scratch_shapes=[pltpu.SemaphoreType.DMA((len(sizes),))],
+        ),
+        out_shape=[
+            jax.ShapeDtypeStruct((size,) + value.shape[1:], value.dtype)
+            for value, size in zip(values, sizes)
+        ],
+        compiler_params=pltpu.CompilerParams(vmem_limit_bytes=VMEM_BYTES),
+        cost_estimate=cost(5),
+    )(jnp.stack(places).astype(jnp.int32), *values)
+
+
+def joined_kernel(count, places_ref, *refs):
+    out_ref, semaphores = refs[count:]
+    rows = refs[0].shape[0]
+    copies = [
+        pltpu.make_async_copy(
+            refs[index],
+            out_ref.at[pl.ds(pl.multiple_of(places_ref[index] * rows, rows), rows)],
+            semaphores.at[index],
+        )
+        for index in range(count)
+    ]
+    for copy in copies:
+        copy.start()
+    for copy in copies:
+        copy.wait()
+
+
+def joined(pieces, places):
+    count = len(pieces)
+    rows, width = pieces[0].shape
+    return pl.pallas_call(
+        functools.partial(joined_kernel, count),
+        grid_spec=pltpu.PrefetchScalarGridSpec(
+            num_scalar_prefetch=1,
+            grid=(1,),
+            in_specs=[pl.BlockSpec(memory_space=pltpu.VMEM)] * count,
+            out_specs=pl.BlockSpec(memory_space=pl.ANY),
+            scratch_shapes=[pltpu.SemaphoreType.DMA((count,))],
+        ),
+        out_shape=jax.ShapeDtypeStruct((count * rows, width), pieces[0].dtype),
+        compiler_params=pltpu.CompilerParams(vmem_limit_bytes=VMEM_BYTES),
+        cost_estimate=cost(5),
+    )(places, *pieces)
+
+
+def gather_dp(values):
+    size = lax.axis_size("dp")
+    here = lax.axis_index("dp")
+    step = 1
+    while step < size:
+        values = place(values, swap(values, "dp", step), lax.rem(here // step, 2))
+        step *= 2
+    return values
+
+
+def sum_dp(values):
+    step = 1
+    while step < lax.axis_size("dp"):
+        values = values + swap(values, "dp", step)
+        step *= 2
     return values
 
 
@@ -736,132 +1103,209 @@
     columns = heads_weight.shape[3]
     features = modulate_weight.shape[3]
     hidden_here = up_weight.shape[2]
+    merge_own, up_own, down_own = merge_weight[0], up_weight[0], down_weight[0]
+    padded_rows = lambda *rows: jnp.pad(jnp.stack(rows), ((0, 8 - len(rows)), (0, 0)))
+    bit_value = lambda value: jnp.reshape(value, (1,)).astype(jnp.int32)
+    core_value = bit_value(core)
+    quarter = 2 * near + core
+    places = 2 * jnp.stack([near, 1 - near, near, 1 - near]) + jnp.stack(
+        [core, core, 1 - core, 1 - core]
+    )
+    places = places.astype(jnp.int32)
+
+    def fetch(values, *behind):
+        return swap(after(values, *behind), "tensor", 1)
+
+    def pass_first(got, *behind):
+        got = after(got, *behind)
+        return got, swap(got, "dp", 4), swap(got, "dp", 1)
+
+    def pass_second(passed, *behind):
+        got, from_near, from_core = passed
+        from_near = after(from_near, *behind)
+        return got, from_near, from_core, swap(from_near, "dp", 1)
+
     heads_own = heads_weight[0].reshape(model_width, 3 * columns)
-    merge_own, up_own, down_own = merge_weight[0], up_weight[0], down_weight[0]
-
-    latent_own = pick(latents, side, 0)
-    latent_other = swap(pick(latents, 1 - side, 0), "tensor", 1)
+    (heads_quarter,) = cut((heads_own,), (quarter,), (model_width // 4,))
+    heads_got = swap(heads_quarter, "tensor", 1)
+    sizes = tuple(value.shape[0] // 4 for value in (merge_own, up_own, down_own))
+    latent_own, latent_sent, cotangent_own, cotangent_sent, merge_quarter, up_quarter, down_quarter = cut(
+        (after(latents, heads_quarter), latents, cotangent, cotangent, merge_own, up_own, down_own),
+        (side, 1 - side, side, 1 - side, quarter, quarter, quarter),
+        (1, 1, 1, 1) + sizes,
+    )
+    condition = after(condition, latent_sent)
     silu_cond = jax.nn.silu(condition.astype(F32)).astype(BF16)
     local_mod = jnp.einsum(
         "sd,dkc->skc", silu_cond, modulate_weight[0], preferred_element_type=F32
     ) + modulate_bias[0].astype(F32)
     mod_other = swap(pick(local_mod, 1 - side, 0), "tensor", 1)
+    bias_pack = swap(jnp.concatenate([heads_bias.reshape(-1), up_bias.reshape(-1)]), "tensor", 1)
     shift1, scale1, gate1, shift2, scale2, gate2 = place(
         pick(local_mod, side, 0), mod_other, side, 1
     )
-    silu_all = lax.all_gather(silu_cond, "dp", axis=0, tiled=True)
-    bias_pack = swap(jnp.concatenate([heads_bias.reshape(-1), up_bias.reshape(-1)]), "tensor", 1)
 
     def heads_offset(pair):
-        return jnp.concatenate([pair[0], jnp.zeros_like(pair[0]), pair[1]]).astype(F32)
+        return jnp.concatenate([pair[0], jnp.zeros_like(pair[0]), pair[1]]).astype(F32)[None]
 
     offset_own = heads_offset(heads_bias[0])
     offset_other = heads_offset(bias_pack[: 2 * columns].reshape(2, columns))
     up_bias_own = up_bias.astype(F32)
     up_bias_other = bias_pack[2 * columns :].reshape(1, hidden_here).astype(F32)
-    cotangent_sent = pick(cotangent, 1 - side, 0)
-    fetch_bits = (near, core)
-    heads_other, heads_piece = fetch_other(heads_own, fetch_bits)
-    merge_other, merge_piece = fetch_other(merge_own, fetch_bits, (latent_other,))
-    up_other, up_piece = fetch_other(up_own, fetch_bits, (heads_piece,))
-    cotangent_other = swap(after(cotangent_sent, merge_piece), "tensor", 1)
-    down_other, _ = fetch_other(down_own, fetch_bits, (up_piece,))
-    live_flag = (side < group_counts[0]).astype(F32)
-
-    stream = jnp.concatenate([latent_own, latent_other], 0).astype(F32)
-    norm1, inverse1 = normalize(stream)
-    normed1 = (norm1 * (1.0 + scale1) + shift1).astype(BF16)
-    normed1_peer = swap(normed1, "dp", 1)
-    qkv_own = (jnp.dot(normed1, heads_own, preferred_element_type=F32) + offset_own).astype(BF16)
-    attended_own, logsum_own = attend(qkv_own)
-    qkv_other = (
-        jnp.dot(normed1, heads_other, preferred_element_type=F32) + offset_other
-    ).astype(BF16)
-    attended_other, logsum_other = attend(qkv_other)
-    branch1 = (
-        jnp.dot(attended_own, merge_own, preferred_element_type=F32)
-        + jnp.dot(attended_other, merge_other, preferred_element_type=F32)
-        + merge_bias[0].astype(F32)
-    )
-    mid = stream + gate1 * branch1
-    norm2, inverse2 = normalize(mid)
-    normed2 = (norm2 * (1.0 + scale2) + shift2).astype(BF16)
-
-    grad = jnp.concatenate([pick(cotangent, side, 0), cotangent_other], 0).astype(F32) * live_flag
-    grad_b2 = (gate2 * grad).astype(BF16)
-    branch2, back2, hidden_own, pre_own, up_sums_own = feed(
-        normed2, grad_b2, up_own, up_bias_own, down_own
-    )
-    branch2, back2, hidden_other, pre_other, up_sums_other = feed(
-        normed2, grad_b2, up_other, up_bias_other, down_other, (branch2, back2)
-    )
-    branch2 = branch2 + down_bias[0].astype(F32)
-    output = (mid + gate2 * branch2).astype(BF16)
-    output_other = swap(output[half:], "tensor", 1)
-    block_output = place(output[None, :half], output_other[None], side)
-
+    shifts1 = padded_rows(shift1, scale1)
+
+    heads_passed = pass_first(heads_got, shifts1)
+    latent_other = fetch(latent_sent[0], heads_passed[0])
+    filled = normed_project(
+        after(latent_own[0], heads_passed[0]), shifts1, heads_own, offset_own
+    )
+    heads_passed = pass_second(heads_passed, filled[0])
+    merge_got = fetch(merge_quarter, latent_other)
+    cotangent_other = fetch(cotangent_sent[0], latent_other)
+    normed1, qkv_own = normed_project(
+        after(latent_other, heads_passed[1]), shifts1, heads_own, offset_own, filled
+    )
+    heads_other = joined((after(heads_passed[0], normed1),) + heads_passed[1:], places)
+    qkv_other = project(normed1, heads_other, offset_other)
+    attended_own, logsum_own = attend(after(qkv_own, qkv_other))
+    merge_passed = pass_first(merge_got, attended_own)
+    cotangent_other = after(cotangent_other, attended_own)
+    up_got = fetch(up_quarter, cotangent_other)
+    attended_other, logsum_other = attend(after(qkv_other, merge_passed[0], cotangent_other))
+    merge_passed = pass_second(merge_passed, attended_other)
+    merge_other = joined((after(merge_passed[0], attended_other),) + merge_passed[1:], places)
+    grad = jnp.concatenate([cotangent_own[0], cotangent_other], 0)
+    grad = jnp.where(side < group_counts[0], grad, jnp.zeros_like(grad))
+    branch1, mid, normed2, grad_b2 = merge(
+        attended_own, attended_other, merge_own, merge_other, latent_own[0], latent_other, grad,
+        padded_rows(gate1, merge_bias[0].astype(F32), shift2, scale2, gate2),
+    )
+    up_passed = pass_first(up_got, normed2)
+    down_got = fetch(down_quarter, up_passed[0])
+    normed1_peer = swap(after(normed1, normed2), "dp", 1)
     normed2_peer = swap(normed2, "dp", 1)
     grad_b2_peer = swap(grad_b2, "dp", 1)
-
-    def feature_grad(rows, rows_peer, own, other):
-        mine = jnp.concatenate([pick(own, core, 0), pick(other, core, 0)], 1)
-        peer = jnp.concatenate(
-            [swap(pick(own, 1 - core, 0), "dp", 1), swap(pick(other, 1 - core, 0), "dp", 1)], 1
-        )
-        return (dot_dims(rows, mine, 0, 0) + dot_dims(rows_peer, peer, 0, 0)).astype(BF16)
-
-    def reduce_blocks(total, order):
-        width = total.shape[1] // 2
-        total = scatter_rows(total.reshape(2, 2, 2, -1, 2 * width), bits, order)
-        sent = swap(total[:, width:], "tensor", 1)
-        return total[:, :width].astype(F32) + sent.astype(F32)
-
-    def join_cores(total):
+    branch2, back2, *hidden_own, up_sums_own = feed(
+        core_value, after(normed2, up_passed[0]), grad_b2, up_own, up_bias_own, down_own
+    )
+    hidden_sent_own, hidden_own, pre_sent_own, pre_own = hidden_own
+    hidden_peer_own, pre_peer_own = swap(hidden_sent_own, "dp", 1), swap(pre_sent_own, "dp", 1)
+    up_passed = pass_second(up_passed, hidden_own)
+    down_passed = pass_first(down_got, hidden_own)
+
+    far_of, near_of, x_of = (
+        jnp.arange(8, dtype=jnp.int32) // step % 2 for step in (4, 2, 1)
+    )
+    where_x = 4 * (x_of == x_bit) + 2 * far_of + near_of
+    where_near = 4 * (near_of == near) + 2 * far_of + x_of
+    x_first = (bit_value(2 * far + near), (4, 8, 12))
+    near_first = (bit_value(2 * far + x_bit), (2, 8, 10))
+
+    def spread(kept, received, order, *behind):
+        base, masks = order
+        kept, *sent = add_split(base, after(kept, *behind), received)
+        return kept, [swap(part, "dp", mask) for part, mask in zip(sent, masks)]
+
+    def block_total(kept, received, *behind):
+        received = after(received, *behind)
+        return sum((part.astype(F32) for part in received), kept.astype(F32))
+
+    def pair_total(own, other, first, second):
+        other = block_total(*other, first).astype(BF16)
+        return block_total(*own, first) + after(swap(other, "tensor", 1), second).astype(F32)
+
+    def join_cores(total, *behind):
         total = total.astype(BF16).reshape((2, -1) + total.shape[1:])
-        sent = swap(pick(total, 1 - core, 0), "dp", 1)
+        sent = after(swap(pick(total, 1 - core, 0), "dp", 1), *behind)
         return place(pick(total, core, 0), sent, core, total.ndim - 2).astype(F32)
 
-    down_total = feature_grad(grad_b2, grad_b2_peer, hidden_own, hidden_other)
-    up_total = feature_grad(normed2, normed2_peer, pre_own, pre_other)
-    down_grad = join_cores(reduce_blocks(down_total, ("x", "near", "far")))
-    up_grad = join_cores(reduce_blocks(up_total, ("near", "x", "far")))
-
-    grad_gate2 = jnp.sum(grad * branch2, 0)
-    down_bias_sum = column_sums(grad_b2)
-    grad_shift2 = jnp.sum(back2, 0)
-    grad_scale2 = jnp.sum(back2 * norm2, 0)
-    grad_mid = grad + normalize_back(back2 * (1.0 + scale2), norm2, inverse2)
-    grad_b1 = (gate1 * grad_mid).astype(BF16)
-    grad_gate1 = jnp.sum(grad_mid * branch1, 0)
-    merge_bias_sum = column_sums(grad_b1)
-    grad_att_own = times_transposed(grad_b1, merge_own).astype(BF16)
-    grad_att_other = times_transposed(grad_b1, merge_other).astype(BF16)
+    up_other = joined((after(up_passed[0], hidden_own),) + up_passed[1:], places)
+    down_parts_own = weight_grad(
+        where_x, grad_b2, after(grad_b2_peer, up_other), hidden_own, hidden_peer_own
+    )
+    down_first_own = swap(down_parts_own[0], "dp", 2)
+    up_parts_own = weight_grad(
+        where_near, after(normed2, down_parts_own[0]), normed2_peer, pre_own, pre_peer_own
+    )
+    up_first_own = swap(up_parts_own[0], "dp", 4)
+    down_passed = pass_second(down_passed, up_parts_own[0])
+    down_other = joined((after(down_passed[0], up_parts_own[0]),) + down_passed[1:], places)
+    branch2, back2, *hidden_other, up_sums_other = feed(
+        core_value, normed2, grad_b2, up_other, up_bias_other, down_other, (branch2, back2)
+    )
+    hidden_sent_other, hidden_other, pre_sent_other, pre_other = hidden_other
+    hidden_peer_other = swap(hidden_sent_other, "dp", 1)
+    pre_peer_other = swap(pre_sent_other, "dp", 1)
+    down_spread_own = spread(down_parts_own[1], down_first_own, x_first, hidden_other)
+    up_spread_own = spread(up_parts_own[1], up_first_own, near_first, hidden_other)
+    output_own, output_sent, grad_mid, grad_b1, grad_att_own, grad_att_other, middle_sums = middle_back(
+        after(branch2, down_spread_own[0], up_spread_own[0]), back2, mid, branch1, grad, grad_b2,
+        merge_own, merge_other, padded_rows(gate1, down_bias[0].astype(F32), scale2, gate2),
+    )
+    grad_gate2, down_bias_sum, grad_shift2, grad_scale2, grad_gate1, merge_bias_sum = middle_sums[:6]
+    down_parts_other = weight_grad(
+        where_x, grad_b2, after(grad_b2_peer, grad_att_own, grad_att_other),
+        hidden_other, hidden_peer_other,
+    )
+    down_first_other = swap(down_parts_other[0], "dp", 2)
+    up_parts_other = weight_grad(
+        where_near, after(normed2, down_parts_other[0]), normed2_peer, pre_other, pre_peer_other
+    )
+    up_first_other = swap(up_parts_other[0], "dp", 4)
+    output_other = swap(after(output_sent, up_parts_other[0]), "tensor", 1)
+    grads_own, sent_own, kept_own = attend_back(
+        core_value, qkv_own, attended_own, after(grad_att_own, up_parts_other[0]), logsum_own
+    )
+    heads_peer_own = swap(sent_own, "dp", 1)
+    down_spread_other = spread(down_parts_other[1], down_first_other, x_first, grads_own)
+    up_spread_other = spread(up_parts_other[1], up_first_other, near_first, grads_own)
     merge_total = outer_rows(
-        grad_b1, jnp.concatenate([attended_own, attended_other], 1)
+        after(grad_b1, down_spread_other[0], up_spread_other[0]),
+        jnp.concatenate([attended_own, attended_other], 1),
     ).astype(BF16).reshape(8, 2, -1, 2 * columns)
     merge_sent = swap(pick(merge_total, 1 - core, 1), "dp", 1)
-    merge_total = (pick(merge_total, core, 1).astype(F32) + merge_sent.astype(F32)).astype(BF16)
-    merge_grad = reduce_blocks(merge_total.reshape(-1, 2 * columns), ("near", "x", "far"))
-    grad_att_own = after(grad_att_own, down_total, up_total, merge_total)
-
-    grads_own, pairs_own = attend_back(qkv_own, attended_own, grad_att_own, logsum_own)
-    grad_att_other = after(grad_att_other, grads_own)
-    grads_other, pairs_other = attend_back(qkv_other, attended_other, grad_att_other, logsum_other)
-    heads_grad = reduce_blocks(
-        feature_grad(normed1, normed1_peer, pairs_own, pairs_other), ("x", "near", "far")
-    )
+    heads_parts_own = weight_grad(
+        where_x, normed1, after(normed1_peer, merge_total), kept_own, heads_peer_own
+    )
+    heads_first_own = swap(heads_parts_own[0], "dp", 2)
+    output_other = after(output_other, heads_parts_own[0])
+    block_output = place(output_own[None], output_other[None], side)
+    grads_other, sent_other, kept_other = attend_back(
+        core_value, qkv_other, attended_other, after(grad_att_other, heads_parts_own[0]), logsum_other
+    )
+    heads_peer_other = swap(sent_other, "dp", 1)
+    heads_spread_own = spread(heads_parts_own[1], heads_first_own, x_first, grads_other)
+    heads_parts_other = weight_grad(
+        where_near, normed1, after(normed1_peer, heads_spread_own[0]), kept_other, heads_peer_other
+    )
+    heads_first_other = swap(heads_parts_other[0], "dp", 4)
+    merge_sent = after(merge_sent, heads_parts_own[0])
+    merge_total = pick(merge_total, core, 1).astype(F32) + merge_sent.astype(F32)
+    merge_total = merge_total.astype(BF16).reshape((2, 2, 2) + merge_total.shape[1:])
+    merge_first = swap(pick(after(merge_total, grads_other), 1 - x_bit, 2), "dp", 2)
+    merge_kept = pick(merge_total, x_bit, 2).reshape((4,) + merge_total.shape[3:])
+    merge_first = merge_first.reshape(merge_kept.shape)
+    down_grad = pair_total(down_spread_own, down_spread_other, grads_other, heads_parts_other[0])
+    up_grad = pair_total(up_spread_own, up_spread_other, grads_other, heads_parts_other[0])
+    grad_latent, latent_sent, first_sums, heads_sums_own, heads_sums_other = first_back(
+        grads_own, after(grads_other, heads_parts_other[0], down_grad, up_grad), heads_own, heads_other,
+        latent_own[0], latent_other, grad_mid, padded_rows(scale1),
+    )
+    heads_spread_other = spread(heads_parts_other[1], heads_first_other, near_first, grad_latent)
+    latent_sent = swap(after(latent_sent, heads_spread_other[0]), "tensor", 1).astype(F32)
+    down_grad = join_cores(down_grad, grad_latent)
+    up_grad = join_cores(up_grad, grad_latent)
+    grad_shift1, grad_scale1 = first_sums[0], first_sums[1]
+    merge_spread = spread(merge_kept, merge_first, x_first, heads_spread_other[0])
+    heads_grad = pair_total(heads_spread_own, heads_spread_other, grad_latent, grad_latent)
+    heads_grad = heads_grad[:, : 3 * columns // 2]
     heads_grad = join_cores(heads_grad.reshape(heads_grad.shape[0], 3, columns // 2))
-    grad_n1 = times_transposed(grads_own, heads_own) + times_transposed(grads_other, heads_other)
-    grad_shift1 = jnp.sum(grad_n1, 0)
-    grad_scale1 = jnp.sum(grad_n1 * norm1, 0)
-    grad_latent = grad_mid + normalize_back(grad_n1 * (1.0 + scale1), norm1, inverse1)
-    latent_sent = swap(grad_latent[half:].astype(BF16), "tensor", 1).astype(F32)
-    latent_grad = place(grad_latent[None, :half], latent_sent[None], side)
-
-    def query_value_sums(grads):
-        return jnp.concatenate(
-            [column_sums(grads[:, :columns]), column_sums(grads[:, 2 * columns :])]
-        )
+    merge_total = block_total(*merge_spread)
+    merge_sent = swap(merge_total[:, columns:].astype(BF16), "tensor", 1)
+    merge_grad = merge_total[:, :columns] + merge_sent.astype(F32)
+
+    def query_value_sums(sums):
+        return jnp.concatenate([sums[0, :columns], sums[0, 2 * columns :]])
 
     def by_side(rows):
         rows = rows.reshape(rows.shape[:-1] + (2, features))
@@ -877,14 +1321,18 @@
     merge_own_sum, merge_other_sum = by_side(merge_bias_sum)
     down_own_sum, down_other_sum = by_side(down_bias_sum)
     bias_own = jnp.concatenate(
-        [query_value_sums(grads_own), merge_own_sum, up_sums_own[0], down_own_sum]
+        [query_value_sums(heads_sums_own), merge_own_sum, up_sums_own[0], down_own_sum]
     )
     bias_other = jnp.concatenate(
-        [query_value_sums(grads_other), merge_other_sum, up_sums_other[0], down_other_sum]
+        [query_value_sums(heads_sums_other), merge_other_sum, up_sums_other[0], down_other_sum]
     )
     bias_total = bias_own + swap(bias_other, "tensor", 1)
-    bias_total = jnp.sum(lax.all_gather(bias_total, "dp", axis=0), 0)
-    grad_mod_all = lax.all_gather(grad_mod_slots, "dp", axis=0, tiled=True)
+    bias_total = sum_dp(bias_total)
+    slots_here = silu_cond.shape[0]
+    tail = jnp.concatenate([silu_cond, grad_mod_slots.reshape(slots_here, -1)], 1)
+    tail_all = gather_dp(tail)
+    silu_all = tail_all[:, :model_width]
+    grad_mod_all = tail_all[:, model_width:].reshape((-1,) + grad_mod_slots.shape[1:])
     rows_here = model_width // lax.axis_size("dp")
     silu_rows = lax.dynamic_slice_in_dim(silu_all, place_dp * rows_here, rows_here, 1)
     modulate_grad = jnp.einsum("sd,skc->dkc", silu_rows, grad_mod_all, preferred_element_type=F32)
@@ -894,6 +1342,7 @@
     )
     cond_total = cond_partial + swap(cond_partial, "tensor", 1)
     condition_grad = jax.vjp(jax.nn.silu, condition.astype(F32))[1](cond_total)[0]
+    latent_grad = place(grad_latent[None], latent_sent[None], side)
     edges = (0, 2 * columns, 2 * columns + features, 2 * columns + features + hidden_here, None)
     heads_bias_grad, merge_bias_grad, up_bias_grad, down_bias_grad = (
         bias_total[first:last] for first, last in zip(edges, edges[1:])

time: 837 us -> 703 us (0.84)
  Pallas kernels: 187 us -> 382 us
  matrix products: 146 us -> 17.3 us
  local copies, waits for them, and re-layouts: 116 us -> 31.4 us
  waiting for transfers between devices: 216 us -> 149 us
  blocking collectives: 56.9 us -> 0 us
  starting transfers between devices: 33.5 us -> 87.6 us
  other arithmetic: 71.4 us -> 27 us
    pallas_call x0 -> x25, Pallas kernels: none -> 194 us  [the longest x6 75.3 us: weight_grad(): pl.pallas_call(functools.partial(weight_grad_kernel, chunks, blocks), gri...]
    dot_general x14 -> x0, matrix products: 131 us -> none  [the longest x6 70.1 us: dot_dims(): lax.dot_general(left, right, (((left_dim,), (right_dim,)), ((), ())), pre...]
    ppermute x54 -> x78, waiting for transfers between devices: 216 us -> 149 us  [swap(): return lax.ppermute(values, axis, bit_pairs(lax.axis_size(axis), bit))]
    all_gather x3 -> x0, blocking collectives: 56.9 us -> none  [the longest x1 19.7 us: slot_device(): bias_total = jnp.sum(lax.all_gather(bias_total, 'dp', axis=0), 0)]
    ppermute x54 -> x78, starting transfers between devices: 33.5 us -> 87.6 us  [swap(): return lax.ppermute(values, axis, bit_pairs(lax.axis_size(axis), bit))]
    reduce_sum x10 -> x0, other arithmetic: 28.6 us -> none  [the longest x1 8.84 us: slot_device(): grad_gate2 = jnp.sum(grad * branch2, 0)]
    squeeze x20 -> x3, local copies, waits for them, and re-layouts: 28.9 us -> 2.09 us  [pick(): return lax.dynamic_index_in_dim(values, index, axis, keepdims=False)]
    dynamic_update_slice x16 -> x0, local copies, waits for them, and re-layouts: 26.7 us -> none  [fetch_other(): lax.dynamic_update_slice_in_dim(whole, piece, (2 * near_here + core_here)...]
  transfers between devices with their start and end apart: 54 -> 78, of which waited for: 17 -> 23; matrix products, arithmetic and copies ran while one was open for 39% -> 9% of each run, Pallas kernels for 23% -> 54%
where the time goes in v2:
time: 703 us; the launch traced here: 696 us
  Pallas kernels  382 us (54%)
  waiting for transfers between devices  149 us (21%)
  starting transfers between devices  87.6 us (12%)
  local copies, waits for them, and re-layouts  31.4 us (4%)
  other arithmetic  27 us (4%)
  matrix products  17.3 us (2%)
    ppermute x78, waiting for transfers between devices, swap(): return lax.ppermute(values, axis, bit_pairs(lax.axis_size(axis), bit))  149 us
    pallas_call x2, Pallas kernels, feed(): pl.pallas_call(functools.partial(feed_kernel, token_rows, len(carried) >...  88.1 us
    ppermute x78, starting transfers between devices, swap(): return lax.ppermute(values, axis, bit_pairs(lax.axis_size(axis), bit))  87.6 us
    pallas_call x6, Pallas kernels, weight_grad(): pl.pallas_call(functools.partial(weight_grad_kernel, chunks, blocks), gri...  75.3 us
    pallas_call x2, Pallas kernels, attend_back(): pl.pallas_call(functools.partial(attend_back_kernel, heads, key_rows, ste...  63.7 us
    pallas_call x2, Pallas kernels, attend(): pl.pallas_call(functools.partial(attend_kernel, heads), grid=(tokens // q...  36 us
    pallas_call x1, Pallas kernels, first_back(): pl.pallas_call(functools.partial(first_back_kernel, blocks), grid=(blocks...  20.7 us
    pallas_call x4, Pallas kernels, joined(): pl.pallas_call(functools.partial(joined_kernel, count), grid_spec=pltpu.P...  18.9 us
  transfers between devices with their start and end apart: 78, of which 23 were waited for; matrix products, arithmetic and copies ran while one was open for 9% of the time, Pallas kernels for 54%

profile of v2, /device:TPU:0, one launch (start us, length us, event | category | flops | bytes accessed | tf_op | source)
XLA Modules:
  0.0 696.5 jit_solution(7385959145871757204)
XLA Ops:
  0.7 6.4 copy.32.refs_0_.refs_2_.refs_4_.weight_own
  7.1 2.2 shard_map.237
  9.3 3.0 collective-permute-start
  12.9 7.3 %shard_map.238 = (bf16[1,512,1152]{2,1,0:T(8,128)(2,1)}, bf16[1,512,1152]{2,1,0:T(8,128)(2,1)}, bf16[1,512,1152]{2,1,0:T(8,128)(2,1)}, bf16[1,512,1152]{2,1,0:T(...) custom-call(s32[7]{0:T(128)} %stack.65.starts_ref, ...), custom_call_target="tpu_custom_call" | custom-call | flops 24999999488 | bytes 100000 | tf_op jit(solution)/shard_map/pallas_call | solution.py:1011
  20.3 5.7 fusion.11
  26.9 2.1 collective-permute-start.6
  32.2 3.7 collective-permute-done.6
  39.3 1.8 collective-permute-start.3
  42.6 6.6 shard_map.239
  49.2 14.2 %collective-permute-done.3.refs_1_ = bf16[288,1728]{1,0:T(8,128)(2,1)} collective-permute-done((bf16[288,1728]{1,0:T(8,128)(2,1)S(1)}, bf16[288,1728]{1,0:T(8,128)(2,1)}, u32[]{:S(2)}, u32[]{:S(2)}) %collective-permute-start.3) | collective-permute-done | bytes 995360 | tf_op jit(solution)/shard_map/ppermute | solution.py:974
  63.4 6.1 collective-permute-done.2.refs_2_.second_ref
  70.5 6.6 shard_map.240
  79.1 4.8 shard_map.241.refs_1_.weight_other
  83.9 8.8 %shard_map.242.qkv_ref = bf16[1024,1728]{1,0:T(8,128)(2,1)} custom-call(bf16[1024,1152]{1,0:T(8,128)(2,1)} %get-tuple-element.253.refs_0_.left_mine, bf16[1152,1728]{1,0:T(8,128)(2,1)} %shard_map.241.refs_1_.weight_other, f32[1,1728]{1,0:T(1,128)} %convert_element_type.218.refs_2_), custom_call_target="tpu_custom_call" | custom-call | flops 44999999488 | bytes 100000 | tf_op jit(solution)/shard_map/pallas_call | solution.py:763
  92.7 17.9 %shard_map.243 = (bf16[1024,576]{1,0:T(8,128)(2,1)}, f32[8,1024]{1,0:T(8,128)}) custom-call(bf16[1024,1728]{1,0:T(8,128)(2,1)} %get-tuple-element.193.qkv_ref), custom_call_target="tpu_custom_call" | custom-call | flops 89999998976 | bytes 100000 | tf_op jit(solution)/shard_map/pallas_call | solution.py:487
  112.4 18.2 %shard_map.244 = (bf16[1024,576]{1,0:T(8,128)(2,1)}, f32[8,1024]{1,0:T(8,128)}) custom-call(bf16[1024,1728]{1,0:T(8,128)(2,1)} %shard_map.242.qkv_ref), custom_call_target="tpu_custom_call" | custom-call | flops 89999998976 | bytes 100000 | tf_op jit(solution)/shard_map/pallas_call | solution.py:487
  133.4 3.1 maximum_select_fusion.1.grad_ref
  137.9 3.1 shard_map.245.weight_other
  141.0 10.9 %shard_map.246 = (bf16[1024,1152]{1,0:T(8,128)(2,1)}, f32[1024,1152]{1,0:T(8,128)}, bf16[1024,1152]{1,0:T(8,128)(2,1)}, bf16[1024,1152]{1,0:T(8,128)(2,1)}) custom-call(bf16[1024,576]{1,0:T(8,128)(2,1)} %get-tuple-element.194.own_ref.out_ref, bf16[1024,576]{1,0:T(8,128)(2,1)} %get-tuple-element.202.other_ref.out_ref, bf16[576,1152]{1,0:T(8,128)(2,1)} %bitcast.119, ...), custom_call_target="tpu_custom_call" | custom-call | flops 54999998464 | bytes 100000 | tf_op jit(solution)/shard_map/pallas_call | solution.py:832
  151.9 11.1 %collective-permute-done.12.refs_0_ = bf16[288,2304]{1,0:T(8,128)(2,1)} collective-permute-done((bf16[288,2304]{1,0:T(8,128)(2,1)S(1)}, bf16[288,2304]{1,0:T(8,128)(2,1)}, u32[]{:S(2)}, u32[]{:S(2)}) %collective-permute-start.12) | collective-permute-done | bytes 1327136 | tf_op jit(solution)/shard_map/ppermute | solution.py:974
  166.2 43.4 %shard_map.247 = (f32[1024,1152]{1,0:T(8,128)}, f32[1024,1152]{1,0:T(8,128)}, bf16[1024,1152]{1,0:T(8,128)(2,1)}, bf16[1024,1152]{1,0:T(8,128)(2,1)}, bf16[1024,...) custom-call(s32[1]{0:T(128)} %bitcast.core_ref, ...), custom_call_target="tpu_custom_call" | custom-call | flops 219999993856 | bytes 100000 | tf_op jit(solution)/shard_map/pallas_call | solution.py:649
  213.5 5.5 shard_map.248.up_ref
  220.0 3.1 collective-permute-done.18.refs_1_
  223.2 13.1 %shard_map.249 = (bf16[4,144,1152]{2,1,0:T(8,128)(2,1)}, bf16[4,144,1152]{2,1,0:T(8,128)(2,1)}) custom-call(s32[8]{0:T(128)} %fusion.41.where_ref, bf16[1024,1152]{1,0:T(8,128)(2,1)} %get-tuple-element.207.grad_ref.left_mine.grad_b2_ref, bf16[1024,1152]{1,0:T(8,128)(2,1)} %collective-permute-done.17.left_peer, ...), custom_call_target="tpu_custom_call" | custom-call | flops 65000001536 | bytes 100000 | tf_op jit(solution)/shard_map/pallas_call | solution.py:700
  236.3 13.2 %shard_map.250 = (bf16[4,144,1152]{2,1,0:T(8,128)(2,1)}, bf16[4,144,1152]{2,1,0:T(8,128)(2,1)}) custom-call(s32[8]{0:T(128)} %fusion.38.where_ref, bf16[1024,1152]{1,0:T(8,128)(2,1)} %get-tuple-element.248.normed_ref.left_mine, bf16[1024,1152]{1,0:T(8,128)(2,1)} %collective-permute-done.19.left_peer, bf16[1024,1152]{1,0:T(8,128)(2,1)} %get-tuple-element.222.refs_0_, ...), custom_call_target="tpu_custom_call" | custom-call | flops 65000001536 | bytes 100000 | tf_op jit(solution)/shard_map/pallas_call | solution.py:700
  254.9 5.5 shard_map.251.down_ref
  260.4 44.7 %shard_map.252 = (f32[1024,1152]{1,0:T(8,128)}, f32[1024,1152]{1,0:T(8,128)}, bf16[1024,1152]{1,0:T(8,128)(2,1)}, bf16[1024,1152]{1,0:T(8,128)(2,1)}, bf16[1024,...) custom-call(s32[1]{0:T(128)} %bitcast.core_ref, ...), custom_call_target="tpu_custom_call" | custom-call | flops 219999993856 | bytes 100000 | tf_op jit(solution)/shard_map/pallas_call | solution.py:649
  305.1 2.9 shard_map.254
  308.0 2.9 shard_map.253
  310.9 17.7 %shard_map.255 = (bf16[512,1152]{1,0:T(8,128)(2,1)}, bf16[512,1152]{1,0:T(8,128)(2,1)}, f32[1024,1152]{1,0:T(8,128)}, bf16[1024,1152]{1,0:T(8,128)(2,1)}, bf16[1...) custom-call(f32[1024,1152]{1,0:T(8,128)} %get-tuple-element.237.branch2_ref, ...), custom_call_target="tpu_custom_call" | custom-call | flops 85000003584 | bytes 100000 | tf_op jit(solution)/shard_map/pallas_call | solution.py:896
  330.8 2.6 collective-permute-start.36
  338.5 13.1 %shard_map.256 = (bf16[4,144,1152]{2,1,0:T(8,128)(2,1)}, bf16[4,144,1152]{2,1,0:T(8,128)(2,1)}) custom-call(s32[8]{0:T(128)} %fusion.41.where_ref, bf16[1024,1152]{1,0:T(8,128)(2,1)} %get-tuple-element.207.grad_ref.left_mine.grad_b2_ref, bf16[1024,1152]{1,0:T(8,128)(2,1)} %collective-permute-done.17.left_peer, ...), custom_call_target="tpu_custom_call" | custom-call | flops 65000001536 | bytes 100000 | tf_op jit(solution)/shard_map/pallas_call | solution.py:700
  351.6 13.0 %shard_map.257 = (bf16[4,144,1152]{2,1,0:T(8,128)(2,1)}, bf16[4,144,1152]{2,1,0:T(8,128)(2,1)}) custom-call(s32[8]{0:T(128)} %fusion.38.where_ref, bf16[1024,1152]{1,0:T(8,128)(2,1)} %get-tuple-element.248.normed_ref.left_mine, bf16[1024,1152]{1,0:T(8,128)(2,1)} %collective-permute-done.19.left_peer, bf16[1024,1152]{1,0:T(8,128)(2,1)} %get-tuple-element.249.refs_0_, ...), custom_call_target="tpu_custom_call" | custom-call | flops 65000001536 | bytes 100000 | tf_op jit(solution)/shard_map/pallas_call | solution.py:700
  365.6 31.9 %shard_map.258 = (bf16[1024,1728]{1,0:T(8,128)(2,1)}, bf16[1024,896]{1,0:T(8,128)(2,1)}, bf16[1024,896]{1,0:T(8,128)(2,1)}) custom-call(s32[1]{0:T(128)} %bitcast.core_ref, bf16[1024,1728]{1,0:T(8,128)(2,1)} %get-tuple-element.193.qkv_ref, bf16[1024,576]{1,0:T(8,128)(2,1)} %get-tuple-element.194.own_ref.out_ref, ...), custom_call_target="tpu_custom_call" | custom-call | flops 160000000000 | bytes 100000 | tf_op jit(solution)/shard_map/pallas_call | solution.py:565
  399.0 2.9 shard_map.260
  402.0 2.9 shard_map.259
  404.8 5.8 convolution_convert_fusion
  415.0 11.4 %shard_map.261 = (bf16[4,144,896]{2,1,0:T(8,128)(2,1)}, bf16[4,144,896]{2,1,0:T(8,128)(2,1)}) custom-call(s32[8]{0:T(128)} %fusion.41.where_ref, bf16[1024,1152]{1,0:T(8,128)(2,1)} %get-tuple-element.253.refs_0_.left_mine, bf16[1024,1152]{1,0:T(8,128)(2,1)} %collective-permute-done.29.left_peer, bf16[1024,896]{1,0:T(8,128)(2,1)} %get-tuple-element.266.refs_0_, ...), custom_call_target="tpu_custom_call" | custom-call | flops 65000001536 | bytes 100000 | tf_op jit(solution)/shard_map/pallas_call | solution.py:700
  431.6 20.6 %collective-permute-start.40 = (bf16[144,1152]{1,0:T(8,128)(2,1)}, bf16[144,1152]{1,0:T(8,128)(2,1)}, u32[]{:S(2)}, u32[]{:S(2)}) collective-permute-start(bf16[144,1152]{1,0:T(8,128)(2,1)} %get-tuple-element.288), channel_id=1, source_target_pairs={{0,24},{2,26},{4,28},{6,30},{8,16},{10,18},{12,20},{14,22},{16,8},... | collective-permute-start | bytes 995336 | tf_op jit(solution)/shard_map/ppermute | solution.py:974
  452.2 31.8 %shard_map.262 = (bf16[1024,1728]{1,0:T(8,128)(2,1)}, bf16[1024,896]{1,0:T(8,128)(2,1)}, bf16[1024,896]{1,0:T(8,128)(2,1)}) custom-call(s32[1]{0:T(128)} %bitcast.core_ref, bf16[1024,1728]{1,0:T(8,128)(2,1)} %shard_map.242.qkv_ref, bf16[1024,576]{1,0:T(8,128)(2,1)} %get-tuple-element.202.other_ref.out_ref, bf16[1024,576]{1,0:T(8,128)(2,1)} %get-tuple-element.270.grad_ref, ...), custom_call_target="tpu_custom_call" | custom-call | flops 160000000000 | bytes 100000 | tf_op jit(solution)/shard_map/pallas_call | solution.py:565
  484.3 4.3 collective-permute-start.47
  491.5 12.8 %collective-permute-done.46 = bf16[144,1152]{1,0:T(8,128)(2,1)S(1)} collective-permute-done((bf16[144,1152]{1,0:T(8,128)(2,1)}, bf16[144,1152]{1,0:T(8,128)(2,1)S(1)}, u32[]{:S(2)}, u32[]{:S(2)}) %collective-permute-start.46) | collective-permute-done | bytes 331808 | tf_op jit(solution)/shard_map/ppermute | solution.py:974
  504.8 6.4 collective-permute-done.47
  512.0 3.6 maximum_select_fusion.2
  517.7 4.5 collective-permute-done.33.received_ref
  522.2 2.5 shard_map.263
  526.0 3.1 collective-permute-start.55
  529.2 11.5 %shard_map.264 = (bf16[4,144,896]{2,1,0:T(8,128)(2,1)}, bf16[4,144,896]{2,1,0:T(8,128)(2,1)}) custom-call(s32[8]{0:T(128)} %fusion.38.where_ref, bf16[1024,1152]{1,0:T(8,128)(2,1)} %get-tuple-element.253.refs_0_.left_mine, bf16[1024,1152]{1,0:T(8,128)(2,1)} %collective-permute-done.29.left_peer, bf16[1024,896]{1,0:T(8,128)(2,1)} %get-tuple-element.277.refs_0_, ...), custom_call_target="tpu_custom_call" | custom-call | flops 65000001536 | bytes 100000 | tf_op jit(solution)/shard_map/pallas_call | solution.py:700
  540.8 1.8 convert_add_fusion.1
  542.7 20.7 %shard_map.265 = (f32[512,1152]{1,0:T(8,128)}, bf16[512,1152]{1,0:T(8,128)(2,1)}, f32[8,1152]{1,0:T(8,128)}, f32[8,1728]{1,0:T(8,128)}, f32[8,1728]{1,0:T(8,128)}) custom-call(bf16[1024,1728]{1,0:T(8,128)(2,1)} %get-tuple-element.258.own_ref, bf16[1024,1728]{1,0:T(8,128)(2,1)} %get-tuple-element.306.other_ref, ...), custom_call_target="tpu_custom_call" | custom-call | flops 105000001536 | bytes 100000 | tf_op jit(solution)/shard_map/pallas_call | solution.py:949
  568.4 4.5 fusion.8
  573.7 3.0 collective-permute-done.52
  579.2 1.8 collective-permute-start.75
  583.1 2.0 collective-permute-start.49
  586.8 20.2 %collective-permute-done.65 = f32[4608]{0:T(1024)S(1)} collective-permute-done((f32[4608]{0:T(1024)S(1)}, f32[4608]{0:T(1024)S(1)}, u32[]{:S(2)}, u32[]{:S(2)}) %collective-permute-start.65) | collective-permute-done | bytes 18464 | tf_op jit(solution)/shard_map/ppermute | solution.py:974
  611.4 4.2 collective-permute-start.77
  617.5 2.6 shard_map.266
  620.1 2.2 shard_map.267
  624.1 2.7 collective-permute-start.58
  627.1 2.3 collective-permute-done.68
  629.4 1.8 collective-permute-start.70
  633.7 23.5 %collective-permute-done.69 = bf16[72,1152]{1,0:T(8,128)(2,1)S(1)} collective-permute-done((bf16[72,1152]{1,0:T(8,128)(2,1)}, bf16[72,1152]{1,0:T(8,128)(2,1)S(1)}, u32[]{:S(2)}, u32[]{:S(2)}) %collective-permute-start.69) | collective-permute-done | bytes 165920 | tf_op jit(solution)/shard_map/ppermute | solution.py:974
  661.2 26.6 %collective-permute-done.59 = bf16[144,896]{1,0:T(8,128)(2,1)S(1)} collective-permute-done((bf16[144,896]{1,0:T(8,128)(2,1)S(1)}, bf16[144,896]{1,0:T(8,128)(2,1)S(1)}, u32[]{:S(2)}, u32[]{:S(2)}) %collective-permute-start.59) | collective-permute-done | bytes 258080 | tf_op jit(solution)/shard_map/ppermute | solution.py:974
  693.6 2.5 maximum_select_fusion
  (360 shorter events, 90.9 us)
Async XLA Ops:
  9.3 30.0 %collective-permute-start = (bf16[288,1728]{1,0:T(8,128)(2,1)}, bf16[288,1728]{1,0:T(8,128)(2,1)S(1)}, u32[]{:S(2)}, u32[]{:S(2)}) collective-permute-start(bf16[288,1728]{1,0:T(8,128)(2,1)} %shard_map.237), channel_id=1, source_target_pairs={{0,1},{1,0},{2,3},{3,2},{4,5},{5,4},{6,7},{7,6},{8,9},{9,8},{10,11... | collective-permute-start | bytes 2985992 | tf_op jit(solution)/shard_map/ppermute | solution.py:974
  26.0 10.7 %collective-permute-start.1 = (f32[6,576]{1,0:T(8,128)S(1)}, f32[6,576]{1,0:T(8,128)S(1)}, u32[]{:S(2)}, u32[]{:S(2)}) collective-permute-start(f32[6,576]{1,0:T(8,128)S(1)} %bitcast.113), channel_id=1, source_target_pairs={{0,1},{1,0},{2,3},{3,2},{4,5},{5,4},{6,7},{7,6},{8,9},{9,8},{10,11... | collective-permute-start | bytes 41480 | tf_op jit(solution)/shard_map/ppermute | solution.py:974
  26.9 9.1 %collective-permute-start.6 = (bf16[3456]{0:T(1024)(128)(2,1)S(1)}, bf16[3456]{0:T(1024)(128)(2,1)S(1)}, u32[]{:S(2)}, u32[]{:S(2)}) collective-permute-start(bf16[3456]{0:T(1024)(128)(2,1)S(1)} %pad_maximum_fusion.2), channel_id=1, source_target_pairs={{0,1},{1,0},{2,3},{3,2},{4,5},{5,4},{6,7},{7,6},{8,9},{9,8},{10,11... | collective-permute-start | bytes 20744 | tf_op jit(solution)/shard_map/ppermute | solution.py:974
  39.3 24.1 %collective-permute-start.3 = (bf16[288,1728]{1,0:T(8,128)(2,1)S(1)}, bf16[288,1728]{1,0:T(8,128)(2,1)}, u32[]{:S(2)}, u32[]{:S(2)}) collective-permute-start(bf16[288,1728]{1,0:T(8,128)(2,1)S(1)} %collective-permute-done.refs_0_), channel_id=1, source_target_pairs={{0,8},{2,10},{4,12},{6,14},{8,0},{10,2},{12,4},{14,6},{16,24},{18,... | collective-permute-start | bytes 2985992 | tf_op jit(solution)/shard_map/ppermute | solution.py:974
  41.1 38.0 %collective-permute-start.4 = (bf16[288,1728]{1,0:T(8,128)(2,1)S(1)}, bf16[288,1728]{1,0:T(8,128)(2,1)}, u32[]{:S(2)}, u32[]{:S(2)}) collective-permute-start(bf16[288,1728]{1,0:T(8,128)(2,1)S(1)} %collective-permute-done.refs_0_), channel_id=1, source_target_pairs={{0,2},{2,0},{4,6},{6,4},{8,10},{10,8},{12,14},{14,12},{16,18},{18,... | collective-permute-start | bytes 2985992 | tf_op jit(solution)/shard_map/ppermute | solution.py:974
  41.1 28.4 %collective-permute-start.2 = (bf16[512,1152]{1,0:T(8,128)(2,1)S(1)}, bf16[512,1152]{1,0:T(8,128)(2,1)S(1)}, u32[]{:S(2)}, u32[]{:S(2)}) collective-permute-start(bf16[512,1152]{1,0:T(8,128)(2,1)S(1)} %bitcast.121), channel_id=1, source_target_pairs={{0,1},{1,0},{2,3},{3,2},{4,5},{5,4},{6,7},{7,6},{8,9},{9,8},{10,11... | collective-permute-start | bytes 3538952 | tf_op jit(solution)/shard_map/ppermute | solution.py:974
  63.4 15.7 %collective-permute-start.5 = (bf16[288,1728]{1,0:T(8,128)(2,1)}, bf16[288,1728]{1,0:T(8,128)(2,1)}, u32[]{:S(2)}, u32[]{:S(2)}) collective-permute-start(bf16[288,1728]{1,0:T(8,128)(2,1)} %collective-permute-done.3.refs_1_), channel_id=1, source_target_pairs={{0,2},{2,0},{4,6},{6,4},{8,10},{10,8},{12,14},{14,12},{16,18},{18,... | collective-permute-start | bytes 2985992 | tf_op jit(solution)/shard_map/ppermute | solution.py:974
  77.1 35.4 %collective-permute-start.8 = (bf16[512,1152]{1,0:T(8,128)(2,1)}, bf16[512,1152]{1,0:T(8,128)(2,1)}, u32[]{:S(2)}, u32[]{:S(2)}) collective-permute-start(bf16[512,1152]{1,0:T(8,128)(2,1)} %bitcast.18), channel_id=1, source_target_pairs={{0,1},{1,0},{2,3},{3,2},{4,5},{5,4},{6,7},{7,6},{8,9},{9,8},{10,11... | collective-permute-start | bytes 3538952 | tf_op jit(solution)/shard_map/ppermute | solution.py:974
  78.6 33.5 %collective-permute-start.7 = (bf16[144,1152]{1,0:T(8,128)(2,1)}, bf16[144,1152]{1,0:T(8,128)(2,1)}, u32[]{:S(2)}, u32[]{:S(2)}) collective-permute-start(bf16[144,1152]{1,0:T(8,128)(2,1)} %get-tuple-element.196), channel_id=1, source_target_pairs={{0,1},{1,0},{2,3},{3,2},{4,5},{5,4},{6,7},{7,6},{8,9},{9,8},{10,11... | collective-permute-start | bytes 995336 | tf_op jit(solution)/shard_map/ppermute | solution.py:974
  112.1 18.5 %collective-permute-start.9 = (bf16[144,1152]{1,0:T(8,128)(2,1)}, bf16[144,1152]{1,0:T(8,128)(2,1)S(1)}, u32[]{:S(2)}, u32[]{:S(2)}) collective-permute-start(bf16[144,1152]{1,0:T(8,128)(2,1)} %collective-permute-done.7.refs_0_), channel_id=1, source_target_pairs={{0,8},{2,10},{4,12},{6,14},{8,0},{10,2},{12,4},{14,6},{16,24},{18,... | collective-permute-start | bytes 995336 | tf_op jit(solution)/shard_map/ppermute | solution.py:974
  112.4 24.0 %collective-permute-start.10 = (bf16[144,1152]{1,0:T(8,128)(2,1)}, bf16[144,1152]{1,0:T(8,128)(2,1)S(1)}, u32[]{:S(2)}, u32[]{:S(2)}) collective-permute-start(bf16[144,1152]{1,0:T(8,128)(2,1)} %collective-permute-done.7.refs_0_), channel_id=1, source_target_pairs={{0,2},{2,0},{4,6},{6,4},{8,10},{10,8},{12,14},{14,12},{16,18},{18,... | collective-permute-start | bytes 995336 | tf_op jit(solution)/shard_map/ppermute | solution.py:974
  131.6 31.4 %collective-permute-start.12 = (bf16[288,2304]{1,0:T(8,128)(2,1)S(1)}, bf16[288,2304]{1,0:T(8,128)(2,1)}, u32[]{:S(2)}, u32[]{:S(2)}) collective-permute-start(bf16[288,2304]{1,0:T(8,128)(2,1)S(1)} %copy-done.49), channel_id=1, source_target_pairs={{0,1},{1,0},{2,3},{3,2},{4,5},{5,4},{6,7},{7,6},{8,9},{9,8},{10,11... | collective-permute-start | bytes 3981320 | tf_op jit(solution)/shard_map/ppermute | solution.py:974
  163.0 46.6 %collective-permute-start.13 = (bf16[288,2304]{1,0:T(8,128)(2,1)}, bf16[288,2304]{1,0:T(8,128)(2,1)}, u32[]{:S(2)}, u32[]{:S(2)}) collective-permute-start(bf16[288,2304]{1,0:T(8,128)(2,1)} %collective-permute-done.12.refs_0_), channel_id=1, source_target_pairs={{0,8},{2,10},{4,12},{6,14},{8,0},{10,2},{12,4},{14,6},{16,24},{18,... | collective-permute-start | bytes 3981320 | tf_op jit(solution)/shard_map/ppermute | solution.py:974
  164.6 47.1 %collective-permute-start.14 = (bf16[288,2304]{1,0:T(8,128)(2,1)}, bf16[288,2304]{1,0:T(8,128)(2,1)}, u32[]{:S(2)}, u32[]{:S(2)}) collective-permute-start(bf16[288,2304]{1,0:T(8,128)(2,1)} %collective-permute-done.12.refs_0_), channel_id=1, source_target_pairs={{0,2},{2,0},{4,6},{6,4},{8,10},{10,8},{12,14},{14,12},{16,18},{18,... | collective-permute-start | bytes 3981320 | tf_op jit(solution)/shard_map/ppermute | solution.py:974
  164.6 46.8 %collective-permute-start.16 = (bf16[576,1152]{1,0:T(8,128)(2,1)}, bf16[576,1152]{1,0:T(8,128)(2,1)}, u32[]{:S(2)}, u32[]{:S(2)}) collective-permute-start(bf16[576,1152]{1,0:T(8,128)(2,1)} %get-tuple-element.216), channel_id=1, source_target_pairs={{0,1},{1,0},{2,3},{3,2},{4,5},{5,4},{6,7},{7,6},{8,9},{9,8},{10,11... | collective-permute-start | bytes 3981320 | tf_op jit(solution)/shard_map/ppermute | solution.py:974
  210.4 9.4 %collective-permute-start.17 = (bf16[1024,1152]{1,0:T(8,128)(2,1)}, bf16[1024,1152]{1,0:T(8,128)(2,1)}, u32[]{:S(2)}, u32[]{:S(2)}) collective-permute-start(bf16[1024,1152]{1,0:T(8,128)(2,1)} %get-tuple-element.207.grad_ref.left_mine.grad_b2_ref), channel_id=1, source_target_pairs={{0,2},{2,0},{4,6},{6,4},{8,10},{10,8},{12,14},{14,12},{16,18},{18,... | collective-permute-start | bytes 7077896 | tf_op jit(solution)/shard_map/ppermute | solution.py:974
  210.7 12.5 %collective-permute-start.18 = (bf16[1024,1152]{1,0:T(8,128)(2,1)}, bf16[1024,1152]{1,0:T(8,128)(2,1)}, u32[]{:S(2)}, u32[]{:S(2)}) collective-permute-start(bf16[1024,1152]{1,0:T(8,128)(2,1)} %get-tuple-element.219), channel_id=1, source_target_pairs={{0,2},{2,0},{4,6},{6,4},{8,10},{10,8},{12,14},{14,12},{16,18},{18,... | collective-permute-start | bytes 7077896 | tf_op jit(solution)/shard_map/ppermute | solution.py:974
  211.4 24.8 %collective-permute-start.19 = (bf16[1024,1152]{1,0:T(8,128)(2,1)S(1)}, bf16[1024,1152]{1,0:T(8,128)(2,1)}, u32[]{:S(2)}, u32[]{:S(2)}) collective-permute-start(bf16[1024,1152]{1,0:T(8,128)(2,1)S(1)} %copy-done.46), channel_id=1, source_target_pairs={{0,2},{2,0},{4,6},{6,4},{8,10},{10,8},{12,14},{14,12},{16,18},{18,... | collective-permute-start | bytes 7077896 | tf_op jit(solution)/shard_map/ppermute | solution.py:974
  211.7 24.6 %collective-permute-start.20 = (bf16[1024,1152]{1,0:T(8,128)(2,1)}, bf16[1024,1152]{1,0:T(8,128)(2,1)}, u32[]{:S(2)}, u32[]{:S(2)}) collective-permute-start(bf16[1024,1152]{1,0:T(8,128)(2,1)} %get-tuple-element.223), channel_id=1, source_target_pairs={{0,2},{2,0},{4,6},{6,4},{8,10},{10,8},{12,14},{14,12},{16,18},{18,... | collective-permute-start | bytes 7077896 | tf_op jit(solution)/shard_map/ppermute | solution.py:974
  213.1 36.4 %collective-permute-start.21 = (bf16[576,1152]{1,0:T(8,128)(2,1)}, bf16[576,1152]{1,0:T(8,128)(2,1)}, u32[]{:S(2)}, u32[]{:S(2)}) collective-permute-start(bf16[576,1152]{1,0:T(8,128)(2,1)} %collective-permute-done.16.refs_0_), channel_id=1, source_target_pairs={{0,8},{2,10},{4,12},{6,14},{8,0},{10,2},{12,4},{14,6},{16,24},{18,... | collective-permute-start | bytes 3981320 | tf_op jit(solution)/shard_map/ppermute | solution.py:974
  219.8 34.0 %collective-permute-start.22 = (bf16[576,1152]{1,0:T(8,128)(2,1)}, bf16[576,1152]{1,0:T(8,128)(2,1)}, u32[]{:S(2)}, u32[]{:S(2)}) collective-permute-start(bf16[576,1152]{1,0:T(8,128)(2,1)} %collective-permute-done.16.refs_0_), channel_id=1, source_target_pairs={{0,2},{2,0},{4,6},{6,4},{8,10},{10,8},{12,14},{14,12},{16,18},{18,... | collective-permute-start | bytes 3981320 | tf_op jit(solution)/shard_map/ppermute | solution.py:974
  251.0 159.7 %collective-permute-start.29 = (bf16[1024,1152]{1,0:T(8,128)(2,1)}, bf16[1024,1152]{1,0:T(8,128)(2,1)}, u32[]{:S(2)}, u32[]{:S(2)}) collective-permute-start(bf16[1024,1152]{1,0:T(8,128)(2,1)} %get-tuple-element.253.refs_0_.left_mine), channel_id=1, source_target_pairs={{0,2},{2,0},{4,6},{6,4},{8,10},{10,8},{12,14},{14,12},{16,18},{18,... | collective-permute-start | bytes 7077896 | tf_op jit(solution)/shard_map/ppermute | solution.py:974
  251.9 53.2 %collective-permute-start.25 = (bf16[4,144,1152]{2,1,0:T(8,128)(2,1)}, bf16[4,144,1152]{2,1,0:T(8,128)(2,1)}, u32[]{:S(2)}, u32[]{:S(2)}) collective-permute-start(bf16[4,144,1152]{2,1,0:T(8,128)(2,1)} %get-tuple-element.224), channel_id=1, source_target_pairs={{0,8},{2,10},{4,12},{6,14},{8,0},{10,2},{12,4},{14,6},{16,24},{18,... | collective-permute-start | bytes 3981320 | tf_op jit(solution)/shard_map/ppermute | solution.py:974
  252.3 55.7 %collective-permute-start.24 = (bf16[4,144,1152]{2,1,0:T(8,128)(2,1)}, bf16[4,144,1152]{2,1,0:T(8,128)(2,1)}, u32[]{:S(2)}, u32[]{:S(2)}) collective-permute-start(bf16[4,144,1152]{2,1,0:T(8,128)(2,1)} %get-tuple-element.220), channel_id=1, source_target_pairs={{0,4},{2,6},{4,0},{6,2},{8,12},{10,14},{12,8},{14,10},{16,20},{18,... | collective-permute-start | bytes 3981320 | tf_op jit(solution)/shard_map/ppermute | solution.py:974
  310.9 27.7 %collective-permute-start.26 = (bf16[1024,1152]{1,0:T(8,128)(2,1)}, bf16[1024,1152]{1,0:T(8,128)(2,1)}, u32[]{:S(2)}, u32[]{:S(2)}) collective-permute-start(bf16[1024,1152]{1,0:T(8,128)(2,1)} %get-tuple-element.246), channel_id=1, source_target_pairs={{0,2},{2,0},{4,6},{6,4},{8,10},{10,8},{12,14},{14,12},{16,18},{18,... | collective-permute-start | bytes 7077896 | tf_op jit(solution)/shard_map/ppermute | solution.py:974
  328.6 23.0 %collective-permute-start.27 = (bf16[1024,1152]{1,0:T(8,128)(2,1)S(1)}, bf16[1024,1152]{1,0:T(8,128)(2,1)}, u32[]{:S(2)}, u32[]{:S(2)}) collective-permute-start(bf16[1024,1152]{1,0:T(8,128)(2,1)S(1)} %copy-done.47), channel_id=1, source_target_pairs={{0,2},{2,0},{4,6},{6,4},{8,10},{10,8},{12,14},{14,12},{16,18},{18,... | collective-permute-start | bytes 7077896 | tf_op jit(solution)/shard_map/ppermute | solution.py:974
  329.1 97.3 %collective-permute-start.35 = (bf16[144,1152]{1,0:T(8,128)(2,1)}, bf16[144,1152]{1,0:T(8,128)(2,1)}, u32[]{:S(2)}, u32[]{:S(2)}) collective-permute-start(bf16[144,1152]{1,0:T(8,128)(2,1)} %get-tuple-element.280), channel_id=1, source_target_pairs={{0,8},{2,10},{4,12},{6,14},{8,0},{10,2},{12,4},{14,6},{16,24},{18,... | collective-permute-start | bytes 995336 | tf_op jit(solution)/shard_map/ppermute | solution.py:974
  330.8 97.1 %collective-permute-start.36 = (bf16[144,1152]{1,0:T(8,128)(2,1)}, bf16[144,1152]{1,0:T(8,128)(2,1)}, u32[]{:S(2)}, u32[]{:S(2)}) collective-permute-start(bf16[144,1152]{1,0:T(8,128)(2,1)} %get-tuple-element.281), channel_id=1, source_target_pairs={{0,16},{2,18},{4,20},{6,22},{8,24},{10,26},{12,28},{14,30},{16,0},... | collective-permute-start | bytes 995336 | tf_op jit(solution)/shard_map/ppermute | solution.py:974
  364.6 32.9 %collective-permute-start.31 = (bf16[4,144,1152]{2,1,0:T(8,128)(2,1)}, bf16[4,144,1152]{2,1,0:T(8,128)(2,1)}, u32[]{:S(2)}, u32[]{:S(2)}) collective-permute-start(bf16[4,144,1152]{2,1,0:T(8,128)(2,1)} %get-tuple-element.251), channel_id=1, source_target_pairs={{0,8},{2,10},{4,12},{6,14},{8,0},{10,2},{12,4},{14,6},{16,24},{18,... | collective-permute-start | bytes 3981320 | tf_op jit(solution)/shard_map/ppermute | solution.py:974
  365.0 36.9 %collective-permute-start.30 = (bf16[4,144,1152]{2,1,0:T(8,128)(2,1)}, bf16[4,144,1152]{2,1,0:T(8,128)(2,1)}, u32[]{:S(2)}, u32[]{:S(2)}) collective-permute-start(bf16[4,144,1152]{2,1,0:T(8,128)(2,1)} %get-tuple-element.247), channel_id=1, source_target_pairs={{0,4},{2,6},{4,0},{6,2},{8,12},{10,14},{12,8},{14,10},{16,20},{18,... | collective-permute-start | bytes 3981320 | tf_op jit(solution)/shard_map/ppermute | solution.py:974
  397.5 31.6 %collective-permute-start.37 = (bf16[144,1152]{1,0:T(8,128)(2,1)S(1)}, bf16[144,1152]{1,0:T(8,128)(2,1)S(1)}, u32[]{:S(2)}, u32[]{:S(2)}) collective-permute-start(bf16[144,1152]{1,0:T(8,128)(2,1)S(1)} %copy-done.56), channel_id=1, source_target_pairs={{0,24},{2,26},{4,28},{6,30},{8,16},{10,18},{12,20},{14,22},{16,8},... | collective-permute-start | bytes 995336 | tf_op jit(solution)/shard_map/ppermute | solution.py:974
  401.9 11.5 %collective-permute-start.32 = (bf16[1024,896]{1,0:T(8,128)(2,1)S(1)}, bf16[1024,896]{1,0:T(8,128)(2,1)}, u32[]{:S(2)}, u32[]{:S(2)}) collective-permute-start(bf16[1024,896]{1,0:T(8,128)(2,1)S(1)} %copy-done.48), channel_id=1, source_target_pairs={{0,2},{2,0},{4,6},{6,4},{8,10},{10,8},{12,14},{14,12},{16,18},{18,... | collective-permute-start | bytes 5505032 | tf_op jit(solution)/shard_map/ppermute | solution.py:974
  410.6 20.2 %collective-permute-start.38 = (bf16[144,1152]{1,0:T(8,128)(2,1)S(1)}, bf16[144,1152]{1,0:T(8,128)(2,1)S(1)}, u32[]{:S(2)}, u32[]{:S(2)}) collective-permute-start(bf16[144,1152]{1,0:T(8,128)(2,1)S(1)} %copy-done.58), channel_id=1, source_target_pairs={{0,8},{2,10},{4,12},{6,14},{8,0},{10,2},{12,4},{14,6},{16,24},{18,... | collective-permute-start | bytes 995336 | tf_op jit(solution)/shard_map/ppermute | solution.py:974
  413.3 18.3 %collective-permute-start.39 = (bf16[144,1152]{1,0:T(8,128)(2,1)S(1)}, bf16[144,1152]{1,0:T(8,128)(2,1)S(1)}, u32[]{:S(2)}, u32[]{:S(2)}) collective-permute-start(bf16[144,1152]{1,0:T(8,128)(2,1)S(1)} %copy-done.57), channel_id=1, source_target_pairs={{0,16},{2,18},{4,20},{6,22},{8,24},{10,26},{12,28},{14,30},{16,0},... | collective-permute-start | bytes 995336 | tf_op jit(solution)/shard_map/ppermute | solution.py:974
  426.4 57.8 %collective-permute-start.42 = (bf16[144,1152]{1,0:T(8,128)(2,1)}, bf16[144,1152]{1,0:T(8,128)(2,1)}, u32[]{:S(2)}, u32[]{:S(2)}) collective-permute-start(bf16[144,1152]{1,0:T(8,128)(2,1)} %get-tuple-element.293), channel_id=1, source_target_pairs={{0,4},{2,6},{4,0},{6,2},{8,12},{10,14},{12,8},{14,10},{16,20},{18,... | collective-permute-start | bytes 995336 | tf_op jit(solution)/shard_map/ppermute | solution.py:974
  427.9 56.4 %collective-permute-start.43 = (bf16[144,1152]{1,0:T(8,128)(2,1)}, bf16[144,1152]{1,0:T(8,128)(2,1)}, u32[]{:S(2)}, u32[]{:S(2)}) collective-permute-start(bf16[144,1152]{1,0:T(8,128)(2,1)} %get-tuple-element.294), channel_id=1, source_target_pairs={{0,16},{2,18},{4,20},{6,22},{8,24},{10,26},{12,28},{14,30},{16,0},... | collective-permute-start | bytes 995336 | tf_op jit(solution)/shard_map/ppermute | solution.py:974
  429.1 59.4 %collective-permute-start.44 = (bf16[144,1152]{1,0:T(8,128)(2,1)}, bf16[144,1152]{1,0:T(8,128)(2,1)}, u32[]{:S(2)}, u32[]{:S(2)}) collective-permute-start(bf16[144,1152]{1,0:T(8,128)(2,1)} %get-tuple-element.295), channel_id=1, source_target_pairs={{0,20},{2,22},{4,16},{6,18},{8,28},{10,30},{12,24},{14,26},{16,4},... | collective-permute-start | bytes 995336 | tf_op jit(solution)/shard_map/ppermute | solution.py:974
  430.8 80.6 %collective-permute-start.28 = (bf16[512,1152]{1,0:T(8,128)(2,1)}, bf16[512,1152]{1,0:T(8,128)(2,1)}, u32[]{:S(2)}, u32[]{:S(2)}) collective-permute-start(bf16[512,1152]{1,0:T(8,128)(2,1)} %get-tuple-element.252), channel_id=1, source_target_pairs={{0,1},{1,0},{2,3},{3,2},{4,5},{5,4},{6,7},{7,6},{8,9},{9,8},{10,11... | collective-permute-start | bytes 3538952 | tf_op jit(solution)/shard_map/ppermute | solution.py:974
  431.6 52.5 %collective-permute-start.40 = (bf16[144,1152]{1,0:T(8,128)(2,1)}, bf16[144,1152]{1,0:T(8,128)(2,1)}, u32[]{:S(2)}, u32[]{:S(2)}) collective-permute-start(bf16[144,1152]{1,0:T(8,128)(2,1)} %get-tuple-element.288), channel_id=1, source_target_pairs={{0,24},{2,26},{4,28},{6,30},{8,16},{10,18},{12,20},{14,22},{16,8},... | collective-permute-start | bytes 995336 | tf_op jit(solution)/shard_map/ppermute | solution.py:974
  484.2 20.1 %collective-permute-start.46 = (bf16[144,1152]{1,0:T(8,128)(2,1)}, bf16[144,1152]{1,0:T(8,128)(2,1)S(1)}, u32[]{:S(2)}, u32[]{:S(2)}) collective-permute-start(bf16[144,1152]{1,0:T(8,128)(2,1)} %get-tuple-element.300), channel_id=1, source_target_pairs={{0,16},{2,18},{4,20},{6,22},{8,24},{10,26},{12,28},{14,30},{16,0},... | collective-permute-start | bytes 995336 | tf_op jit(solution)/shard_map/ppermute | solution.py:974
  484.3 27.0 %collective-permute-start.47 = (bf16[144,1152]{1,0:T(8,128)(2,1)}, bf16[144,1152]{1,0:T(8,128)(2,1)S(1)}, u32[]{:S(2)}, u32[]{:S(2)}) collective-permute-start(bf16[144,1152]{1,0:T(8,128)(2,1)} %get-tuple-element.301), channel_id=1, source_target_pairs={{0,20},{2,22},{4,16},{6,18},{8,28},{10,30},{12,24},{14,26},{16,4},... | collective-permute-start | bytes 995336 | tf_op jit(solution)/shard_map/ppermute | solution.py:974
  488.6 27.1 %collective-permute-start.66 = (bf16[8,72,1152]{2,1,0:T(8,128)(2,1)S(1)}, bf16[8,72,1152]{2,1,0:T(8,128)(2,1)S(1)}, u32[]{:S(2)}, u32[]{:S(2)}) collective-permute-start(bf16[8,72,1152]{2,1,0:T(8,128)(2,1)S(1)} %copy-done.3), channel_id=1, source_target_pairs={{0,2},{2,0},{4,6},{6,4},{8,10},{10,8},{12,14},{14,12},{16,18},{18,... | collective-permute-start | bytes 3981320 | tf_op jit(solution)/shard_map/ppermute | solution.py:974
  491.5 30.8 %collective-permute-start.33 = (bf16[4,144,896]{2,1,0:T(8,128)(2,1)S(1)}, bf16[4,144,896]{2,1,0:T(8,128)(2,1)}, u32[]{:S(2)}, u32[]{:S(2)}) collective-permute-start(bf16[4,144,896]{2,1,0:T(8,128)(2,1)S(1)} %copy-done.55), channel_id=1, source_target_pairs={{0,4},{2,6},{4,0},{6,2},{8,12},{10,14},{12,8},{14,10},{16,20},{18,... | collective-permute-start | bytes 3096584 | tf_op jit(solution)/shard_map/ppermute | solution.py:974
  504.3 36.4 %collective-permute-start.41 = (bf16[144,1152]{1,0:T(8,128)(2,1)S(1)}, bf16[144,1152]{1,0:T(8,128)(2,1)S(1)}, u32[]{:S(2)}, u32[]{:S(2)}) collective-permute-start(bf16[144,1152]{1,0:T(8,128)(2,1)S(1)} %add_convert_fusion.1), channel_id=1, source_target_pairs={{0,1},{1,0},{2,3},{3,2},{4,5},{5,4},{6,7},{7,6},{8,9},{9,8},{10,11... | collective-permute-start | bytes 995336 | tf_op jit(solution)/shard_map/ppermute | solution.py:974
  511.2 14.8 %collective-permute-start.34 = (bf16[1024,896]{1,0:T(8,128)(2,1)}, bf16[1024,896]{1,0:T(8,128)(2,1)}, u32[]{:S(2)}, u32[]{:S(2)}) collective-permute-start(bf16[1024,896]{1,0:T(8,128)(2,1)} %get-tuple-element.278), channel_id=1, source_target_pairs={{0,2},{2,0},{4,6},{6,4},{8,10},{10,8},{12,14},{14,12},{16,18},{18,... | collective-permute-start | bytes 5505032 | tf_op jit(solution)/shard_map/ppermute | solution.py:974
  511.4 29.3 %collective-permute-start.48 = (bf16[144,1152]{1,0:T(8,128)(2,1)S(1)}, bf16[144,1152]{1,0:T(8,128)(2,1)S(1)}, u32[]{:S(2)}, u32[]{:S(2)}) collective-permute-start(bf16[144,1152]{1,0:T(8,128)(2,1)S(1)} %add_convert_fusion), channel_id=1, source_target_pairs={{0,1},{1,0},{2,3},{3,2},{4,5},{5,4},{6,7},{7,6},{8,9},{9,8},{10,11... | collective-permute-start | bytes 995336 | tf_op jit(solution)/shard_map/ppermute | solution.py:974
  524.8 57.9 %collective-permute-start.53 = (bf16[144,896]{1,0:T(8,128)(2,1)}, bf16[144,896]{1,0:T(8,128)(2,1)}, u32[]{:S(2)}, u32[]{:S(2)}) collective-permute-start(bf16[144,896]{1,0:T(8,128)(2,1)} %get-tuple-element.316), channel_id=1, source_target_pairs={{0,8},{2,10},{4,12},{6,14},{8,0},{10,2},{12,4},{14,6},{16,24},{18,... | collective-permute-start | bytes 774152 | tf_op jit(solution)/shard_map/ppermute | solution.py:974
  524.8 58.3 %collective-permute-start.54 = (bf16[144,896]{1,0:T(8,128)(2,1)}, bf16[144,896]{1,0:T(8,128)(2,1)}, u32[]{:S(2)}, u32[]{:S(2)}) collective-permute-start(bf16[144,896]{1,0:T(8,128)(2,1)} %get-tuple-element.317), channel_id=1, source_target_pairs={{0,16},{2,18},{4,20},{6,22},{8,24},{10,26},{12,28},{14,30},{16,0},... | collective-permute-start | bytes 774152 | tf_op jit(solution)/shard_map/ppermute | solution.py:974
  526.0 59.0 %collective-permute-start.55 = (bf16[144,896]{1,0:T(8,128)(2,1)}, bf16[144,896]{1,0:T(8,128)(2,1)}, u32[]{:S(2)}, u32[]{:S(2)}) collective-permute-start(bf16[144,896]{1,0:T(8,128)(2,1)} %get-tuple-element.318), channel_id=1, source_target_pairs={{0,24},{2,26},{4,28},{6,30},{8,16},{10,18},{12,20},{14,22},{16,8},... | collective-permute-start | bytes 774152 | tf_op jit(solution)/shard_map/ppermute | solution.py:974
  565.9 11.5 %collective-permute-start.61 = (f32[4608]{0:T(1024)S(1)}, f32[4608]{0:T(1024)S(1)}, u32[]{:S(2)}, u32[]{:S(2)}) collective-permute-start(f32[4608]{0:T(1024)S(1)} %concatenate.180), channel_id=1, source_target_pairs={{0,1},{1,0},{2,3},{3,2},{4,5},{5,4},{6,7},{7,6},{8,9},{9,8},{10,11... | collective-permute-start | bytes 55304 | tf_op jit(solution)/shard_map/ppermute | solution.py:974
  582.7 37.4 %collective-permute-start.67 = (bf16[2,2,72,1152]{3,2,1,0:T(8,128)(2,1)S(1)}, bf16[2,2,72,1152]{3,2,1,0:T(8,128)(2,1)}, u32[]{:S(2)}, u32[]{:S(2)}) collective-permute-start(bf16[2,2,72,1152]{3,2,1,0:T(8,128)(2,1)S(1)} %copy-done.6), channel_id=1, source_target_pairs={{0,4},{2,6},{4,0},{6,2},{8,12},{10,14},{12,8},{14,10},{16,20},{18,... | collective-permute-start | bytes 1990664 | tf_op jit(solution)/shard_map/ppermute | solution.py:974
  583.1 34.5 %collective-permute-start.49 = (bf16[4,144,896]{2,1,0:T(8,128)(2,1)S(1)}, bf16[4,144,896]{2,1,0:T(8,128)(2,1)}, u32[]{:S(2)}, u32[]{:S(2)}) collective-permute-start(bf16[4,144,896]{2,1,0:T(8,128)(2,1)S(1)} %copy-done.53), channel_id=1, source_target_pairs={{0,8},{2,10},{4,12},{6,14},{8,0},{10,2},{12,4},{14,6},{16,24},{18,... | collective-permute-start | bytes 3096584 | tf_op jit(solution)/shard_map/ppermute | solution.py:974
  585.1 30.5 %collective-permute-start.73 = (bf16[72,1152]{1,0:T(8,128)(2,1)S(1)}, bf16[72,1152]{1,0:T(8,128)(2,1)S(1)}, u32[]{:S(2)}, u32[]{:S(2)}) collective-permute-start(bf16[72,1152]{1,0:T(8,128)(2,1)S(1)} %get-tuple-element.373), channel_id=1, source_target_pairs={{0,2},{2,0},{4,6},{6,4},{8,10},{10,8},{12,14},{14,12},{16,18},{18,... | collective-permute-start | bytes 497672 | tf_op jit(solution)/shard_map/ppermute | solution.py:974
  586.7 28.9 %collective-permute-start.72 = (bf16[72,1152]{1,0:T(8,128)(2,1)S(1)}, bf16[72,1152]{1,0:T(8,128)(2,1)S(1)}, u32[]{:S(2)}, u32[]{:S(2)}) collective-permute-start(bf16[72,1152]{1,0:T(8,128)(2,1)S(1)} %get-tuple-element.375), channel_id=1, source_target_pairs={{0,2},{2,0},{4,6},{6,4},{8,10},{10,8},{12,14},{14,12},{16,18},{18,... | collective-permute-start | bytes 497672 | tf_op jit(solution)/shard_map/ppermute | solution.py:974
  586.7 20.4 %collective-permute-start.65 = (f32[4608]{0:T(1024)S(1)}, f32[4608]{0:T(1024)S(1)}, u32[]{:S(2)}, u32[]{:S(2)}) collective-permute-start(f32[4608]{0:T(1024)S(1)} %add.262), channel_id=1, source_target_pairs={{0,16},{2,18},{4,20},{6,22},{8,24},{10,26},{12,28},{14,30},{16,0},... | collective-permute-start | bytes 55304 | tf_op jit(solution)/shard_map/ppermute | solution.py:974
  611.4 15.3 %collective-permute-start.77 = (bf16[16,4608]{1,0:T(8,128)(2,1)S(1)}, bf16[16,4608]{1,0:T(8,128)(2,1)S(1)}, u32[]{:S(2)}, u32[]{:S(2)}) collective-permute-start(bf16[16,4608]{1,0:T(8,128)(2,1)S(1)} %maximum_select_fusion.7), channel_id=1, source_target_pairs={{0,16},{2,18},{4,20},{6,22},{8,24},{10,26},{12,28},{14,30},{16,0},... | collective-permute-start | bytes 442376 | tf_op jit(solution)/shard_map/ppermute | solution.py:974
  622.3 35.4 %collective-permute-start.56 = (bf16[144,896]{1,0:T(8,128)(2,1)}, bf16[144,896]{1,0:T(8,128)(2,1)S(1)}, u32[]{:S(2)}, u32[]{:S(2)}) collective-permute-start(bf16[144,896]{1,0:T(8,128)(2,1)} %get-tuple-element.322), channel_id=1, source_target_pairs={{0,4},{2,6},{4,0},{6,2},{8,12},{10,14},{12,8},{14,10},{16,20},{18,... | collective-permute-start | bytes 774152 | tf_op jit(solution)/shard_map/ppermute | solution.py:974
  624.0 33.7 %collective-permute-start.57 = (bf16[144,896]{1,0:T(8,128)(2,1)S(1)}, bf16[144,896]{1,0:T(8,128)(2,1)S(1)}, u32[]{:S(2)}, u32[]{:S(2)}) collective-permute-start(bf16[144,896]{1,0:T(8,128)(2,1)S(1)} %copy-done.63), channel_id=1, source_target_pairs={{0,16},{2,18},{4,20},{6,22},{8,24},{10,26},{12,28},{14,30},{16,0},... | collective-permute-start | bytes 774152 | tf_op jit(solution)/shard_map/ppermute | solution.py:974
  624.1 33.7 %collective-permute-start.58 = (bf16[144,896]{1,0:T(8,128)(2,1)S(1)}, bf16[144,896]{1,0:T(8,128)(2,1)S(1)}, u32[]{:S(2)}, u32[]{:S(2)}) collective-permute-start(bf16[144,896]{1,0:T(8,128)(2,1)S(1)} %copy-done.62), channel_id=1, source_target_pairs={{0,20},{2,22},{4,16},{6,18},{8,28},{10,30},{12,24},{14,26},{16,4},... | collective-permute-start | bytes 774152 | tf_op jit(solution)/shard_map/ppermute | solution.py:974
  626.8 30.4 %collective-permute-start.69 = (bf16[72,1152]{1,0:T(8,128)(2,1)}, bf16[72,1152]{1,0:T(8,128)(2,1)S(1)}, u32[]{:S(2)}, u32[]{:S(2)}) collective-permute-start(bf16[72,1152]{1,0:T(8,128)(2,1)} %get-tuple-element.338), channel_id=1, source_target_pairs={{0,16},{2,18},{4,20},{6,22},{8,24},{10,26},{12,28},{14,30},{16,0},... | collective-permute-start | bytes 497672 | tf_op jit(solution)/shard_map/ppermute | solution.py:974
  629.4 28.3 %collective-permute-start.70 = (bf16[72,1152]{1,0:T(8,128)(2,1)}, bf16[72,1152]{1,0:T(8,128)(2,1)}, u32[]{:S(2)}, u32[]{:S(2)}) collective-permute-start(bf16[72,1152]{1,0:T(8,128)(2,1)} %get-tuple-element.339), channel_id=1, source_target_pairs={{0,24},{2,26},{4,28},{6,30},{8,16},{10,18},{12,20},{14,22},{16,8},... | collective-permute-start | bytes 497672 | tf_op jit(solution)/shard_map/ppermute | solution.py:974
  657.2 35.3 %collective-permute-start.50 = (bf16[512,1152]{1,0:T(8,128)(2,1)}, bf16[512,1152]{1,0:T(8,128)(2,1)S(1)}, u32[]{:S(2)}, u32[]{:S(2)}) collective-permute-start(bf16[512,1152]{1,0:T(8,128)(2,1)} %get-tuple-element.313), channel_id=1, source_target_pairs={{0,1},{1,0},{2,3},{3,2},{4,5},{5,4},{6,7},{7,6},{8,9},{9,8},{10,11... | collective-permute-start | bytes 3538952 | tf_op jit(solution)/shard_map/ppermute | solution.py:974
  657.9 29.9 %collective-permute-start.59 = (bf16[144,896]{1,0:T(8,128)(2,1)S(1)}, bf16[144,896]{1,0:T(8,128)(2,1)S(1)}, u32[]{:S(2)}, u32[]{:S(2)}) collective-permute-start(bf16[144,896]{1,0:T(8,128)(2,1)S(1)} %add_convert_fusion.3), channel_id=1, source_target_pairs={{0,1},{1,0},{2,3},{3,2},{4,5},{5,4},{6,7},{7,6},{8,9},{9,8},{10,11... | collective-permute-start | bytes 774152 | tf_op jit(solution)/shard_map/ppermute | solution.py:974
  660.6 29.1 %collective-permute-start.71 = (bf16[72,576]{1,0:T(8,128)(2,1)S(1)}, bf16[72,576]{1,0:T(8,128)(2,1)S(1)}, u32[]{:S(2)}, u32[]{:S(2)}) collective-permute-start(bf16[72,576]{1,0:T(8,128)(2,1)S(1)} %slice.146), channel_id=1, source_target_pairs={{0,1},{1,0},{2,3},{3,2},{4,5},{5,4},{6,7},{7,6},{8,9},{9,8},{10,11... | collective-permute-start | bytes 248840 | tf_op jit(solution)/shard_map/ppermute | solution.py:974
  (78 other events, 1238.7 us)

commit v3 on v2

--- a/solution.py
+++ b/solution.py
@@ -456,6 +456,46 @@
     return pl.CostEstimate(flops=weight * 50 * 10**8, bytes_accessed=10**5, transcendentals=0)
 
 
+class Tied:
+    def __init__(self, value, behind):
+        self.value, self.behind = value, behind
+
+
+def untied(value):
+    return value.value if isinstance(value, Tied) else value
+
+
+def after(value, *behind):
+    return Tied(value, behind)
+
+
+def run(kernel, weight, scalars, inputs, in_specs, grid, out_specs, out_shape, scratch=(), aliases={}):
+    behind = []
+    for value in inputs:
+        if isinstance(value, Tied):
+            behind += [untied(other) for other in value.behind]
+    inputs = [untied(value) for value in inputs]
+    first = len(scalars) + len(inputs)
+
+    def without_ties(*refs):
+        kernel(*refs[:first], *refs[first + len(behind) :])
+
+    return pl.pallas_call(
+        without_ties,
+        grid_spec=pltpu.PrefetchScalarGridSpec(
+            num_scalar_prefetch=len(scalars),
+            grid=grid,
+            in_specs=list(in_specs) + [pl.BlockSpec(memory_space=pl.ANY)] * len(behind),
+            out_specs=out_specs,
+            scratch_shapes=list(scratch),
+        ),
+        out_shape=out_shape,
+        input_output_aliases=aliases,
+        compiler_params=pltpu.CompilerParams(vmem_limit_bytes=VMEM_BYTES),
+        cost_estimate=cost(weight),
+    )(*scalars, *inputs, *behind)
+
+
 def dot_dims(left, right, left_dim, right_dim):
     return lax.dot_general(
         left, right, (((left_dim,), (right_dim,)), ((), ())), preferred_element_type=F32
@@ -482,23 +522,21 @@
 
 
 def attend(qkv, query_rows=512):
-    tokens, width = qkv.shape[0], qkv.shape[1] // 3
+    tokens, width = untied(qkv).shape[0], untied(qkv).shape[1] // 3
     heads = width // HEAD_DIM
-    return pl.pallas_call(
-        functools.partial(attend_kernel, heads),
-        grid=(tokens // query_rows,),
-        in_specs=[pl.BlockSpec((tokens, 3 * width), lambda i: (0, 0))],
-        out_specs=[
+    return run(
+        functools.partial(attend_kernel, heads), 18, (), [qkv],
+        [pl.BlockSpec((tokens, 3 * width), lambda i: (0, 0))],
+        (tokens // query_rows,),
+        [
             pl.BlockSpec((query_rows, width), lambda i: (i, 0)),
             pl.BlockSpec((heads, query_rows), lambda i: (0, i)),
         ],
-        out_shape=[
+        [
             jax.ShapeDtypeStruct((tokens, width), BF16),
             jax.ShapeDtypeStruct((heads, tokens), F32),
         ],
-        compiler_params=pltpu.CompilerParams(vmem_limit_bytes=VMEM_BYTES),
-        cost_estimate=cost(18),
-    )(qkv)
+    )
 
 
 def attend_back_kernel(
@@ -562,29 +600,22 @@
     steps = tokens // key_rows
     whole = lambda *shape: pl.BlockSpec(shape, lambda i, core_ref: (0,) * len(shape))
     half = (tokens, -(-3 * width // 256) * 128)
-    return pl.pallas_call(
-        functools.partial(attend_back_kernel, heads, key_rows, steps),
-        grid_spec=pltpu.PrefetchScalarGridSpec(
-            num_scalar_prefetch=1,
-            grid=(steps,),
-            in_specs=[
-                whole(tokens, 3 * width), whole(tokens, width), whole(tokens, width),
-                whole(heads, tokens),
-            ],
-            out_specs=[whole(tokens, 3 * width), whole(*half), whole(*half)],
-            scratch_shapes=[
-                pltpu.VMEM((heads, tokens), F32),
-                pltpu.VMEM((heads, HEAD_DIM, tokens), F32),
-            ],
-        ),
-        out_shape=[
+    return run(
+        functools.partial(attend_back_kernel, heads, key_rows, steps), 32,
+        [core], [qkv, attended, grad_attended, logsum],
+        [
+            whole(tokens, 3 * width), whole(tokens, width), whole(tokens, width),
+            whole(heads, tokens),
+        ],
+        (steps,),
+        [whole(tokens, 3 * width), whole(*half), whole(*half)],
+        [
             jax.ShapeDtypeStruct((tokens, 3 * width), BF16),
             jax.ShapeDtypeStruct(half, BF16),
             jax.ShapeDtypeStruct(half, BF16),
         ],
-        compiler_params=pltpu.CompilerParams(vmem_limit_bytes=VMEM_BYTES),
-        cost_estimate=cost(32),
-    )(core, qkv, attended, grad_attended, logsum)
+        [pltpu.VMEM((heads, tokens), F32), pltpu.VMEM((heads, HEAD_DIM, tokens), F32)],
+    )
 
 
 GELU_OUTER = math.sqrt(2 / math.pi)
@@ -639,35 +670,31 @@
 
 
 def feed(core, normed, grad, up, bias, down, carried=(), token_rows=256):
-    tokens, model_width = normed.shape
+    tokens, model_width = untied(normed).shape
     hidden_here = up.shape[1]
     width = hidden_here // 2
     chunk = lambda j, core_ref: lax.rem(j + 1 + core_ref[0], 2)
     single = pl.Buffered(1)
     whole = lambda: pl.BlockSpec((tokens, model_width), lambda j, c: (0, 0), pipeline_mode=single)
     part = lambda: pl.BlockSpec((tokens, width), lambda j, c: (0, 0), pipeline_mode=single)
-    return pl.pallas_call(
-        functools.partial(feed_kernel, token_rows, len(carried) > 0),
-        grid_spec=pltpu.PrefetchScalarGridSpec(
-            num_scalar_prefetch=1,
-            grid=(2,),
-            in_specs=[
-                whole(), whole(),
-                pl.BlockSpec((model_width, width), lambda j, c: (0, chunk(j, c))),
-                pl.BlockSpec((1, width), lambda j, c: (0, chunk(j, c))),
-                pl.BlockSpec((width, model_width), lambda j, c: (chunk(j, c), 0)),
-            ] + [whole() for _ in carried],
-            out_specs=[
-                whole(), whole(), part(), part(), part(), part(),
-                pl.BlockSpec((1, width), lambda j, c: (0, chunk(j, c))),
-            ],
-        ),
-        out_shape=[jax.ShapeDtypeStruct((tokens, model_width), F32)] * 2
+    return run(
+        functools.partial(feed_kernel, token_rows, len(carried) > 0), 44,
+        [core], [normed, grad, up, bias, down, *carried],
+        [
+            whole(), whole(),
+            pl.BlockSpec((model_width, width), lambda j, c: (0, chunk(j, c))),
+            pl.BlockSpec((1, width), lambda j, c: (0, chunk(j, c))),
+            pl.BlockSpec((width, model_width), lambda j, c: (chunk(j, c), 0)),
+        ] + [whole() for _ in carried],
+        (2,),
+        [
+            whole(), whole(), part(), part(), part(), part(),
+            pl.BlockSpec((1, width), lambda j, c: (0, chunk(j, c))),
+        ],
+        [jax.ShapeDtypeStruct((tokens, model_width), F32)] * 2
         + [jax.ShapeDtypeStruct((tokens, width), BF16)] * 4
         + [jax.ShapeDtypeStruct((1, hidden_here), F32)],
-        compiler_params=pltpu.CompilerParams(vmem_limit_bytes=VMEM_BYTES),
-        cost_estimate=cost(44),
-    )(core, normed, grad, up, bias, down, *carried)
+    )
 
 
 def weight_grad_kernel(chunks, blocks, where_ref, left_mine, left_peer, *refs):
@@ -690,49 +717,37 @@
                 outs[2 * chunk + part][block] = total[block * rows : (block + 1) * rows]
 
 
-def weight_grad(where, left_mine, left_peer, *rights):
-    tokens, model_width = left_mine.shape
+def weight_grad(where, left_mine, left_peer, *rights, weight=0):
+    tokens, model_width = untied(left_mine).shape
     blocks = where.shape[0]
     chunks = len(rights) // 2
     width = rights[0].shape[1]
     out = jax.ShapeDtypeStruct((blocks // 2, model_width // blocks, width), BF16)
     whole = lambda value: pl.BlockSpec(value.shape, lambda j, w: (0,) * len(value.shape))
-    return pl.pallas_call(
-        functools.partial(weight_grad_kernel, chunks, blocks),
-        grid_spec=pltpu.PrefetchScalarGridSpec(
-            num_scalar_prefetch=1,
-            grid=(1,),
-            in_specs=[whole(value) for value in (left_mine, left_peer) + rights],
-            out_specs=[whole(out)] * (2 * chunks),
-            scratch_shapes=[pltpu.VMEM((model_width, 2 * tokens), BF16)],
-        ),
-        out_shape=[out] * (2 * chunks),
-        compiler_params=pltpu.CompilerParams(vmem_limit_bytes=VMEM_BYTES),
-        cost_estimate=cost(13),
-    )(where, left_mine, left_peer, *rights)
-
-
-def add_split_kernel(base_ref, kept_ref, received_ref, *out_refs):
-    for place, out_ref in enumerate(out_refs):
-        block = lax.bitwise_xor(base_ref[0], place)
-        total = kept_ref[block].astype(F32) + received_ref[block].astype(F32)
-        out_ref[...] = total.astype(BF16)
-
-
-def add_split(base, kept, received):
+    inputs = [left_mine, left_peer, *rights]
+    return run(
+        functools.partial(weight_grad_kernel, chunks, blocks), weight,
+        [where], inputs, [whole(untied(value)) for value in inputs],
+        (1,), [whole(out)] * (2 * chunks), [out] * (2 * chunks),
+        [pltpu.VMEM((model_width, 2 * tokens), BF16)],
+    )
+
+
+def halve_kernel(bit_ref, kept_out, sent_out, kept_in, sent_in, sent_ref, kept_ref):
+    sent_ref[...] = (kept_out[...].astype(F32) + sent_out[...].astype(F32)).astype(BF16)
+    kept_ref[...] = (kept_in[...].astype(F32) + sent_in[...].astype(F32)).astype(BF16)
+
+
+def halve(bit, kept, received):
     blocks, rows, width = kept.shape
-    out = jax.ShapeDtypeStruct((rows, width), BF16)
-    whole = lambda *shape: pl.BlockSpec(shape, lambda j, b: (0,) * len(shape))
-    return pl.pallas_call(
-        add_split_kernel,
-        grid_spec=pltpu.PrefetchScalarGridSpec(
-            num_scalar_prefetch=1, grid=(1,),
-            in_specs=[whole(*kept.shape)] * 2, out_specs=[whole(rows, width)] * blocks,
-        ),
-        out_shape=[out] * blocks,
-        compiler_params=pltpu.CompilerParams(vmem_limit_bytes=VMEM_BYTES),
-        cost_estimate=cost(2),
-    )(base, kept, received)
+    out = jax.ShapeDtypeStruct((blocks // 2, rows, width), BF16)
+    leave = pl.BlockSpec((1, rows, width), lambda j, b: (2 * j + 1 - b[0], 0, 0))
+    stay = pl.BlockSpec((1, rows, width), lambda j, b: (2 * j + b[0], 0, 0))
+    here = pl.BlockSpec((1, rows, width), lambda j, b: (j, 0, 0))
+    return run(
+        halve_kernel, 0, [bit], [kept, received, kept, untied(received)],
+        [leave, leave, stay, stay], (blocks // 2,), [here, here], [out, out],
+    )
 
 
 def project_kernel(with_norm, *refs):
@@ -760,41 +775,34 @@
 def project(normed, weight, offset, rows=256):
     tokens, model_width = normed.shape
     width = weight.shape[1]
-    return pl.pallas_call(
-        functools.partial(project_kernel, 0),
-        grid=(tokens // rows,),
-        in_specs=[
-            row_blocks(rows, model_width), constant_block(weight.shape), constant_block((1, width)),
-        ],
-        out_specs=row_blocks(rows, width),
-        out_shape=jax.ShapeDtypeStruct((tokens, width), BF16),
-        compiler_params=pltpu.CompilerParams(vmem_limit_bytes=VMEM_BYTES),
-        cost_estimate=cost(9),
-    )(normed, weight, offset)
+    return run(
+        functools.partial(project_kernel, 0), 9, (), [normed, weight, offset],
+        [row_blocks(rows, model_width), constant_block(weight.shape), constant_block((1, width))],
+        (tokens // rows,), row_blocks(rows, width), jax.ShapeDtypeStruct((tokens, width), BF16),
+    )
 
 
 def normed_project(half, shifts, weight, offset, filled=None, rows=256):
-    half_tokens, model_width = half.shape
+    half_tokens, model_width = untied(half).shape
     width = weight.shape[1]
     first = 0 if filled is None else half_tokens // rows
     held = [] if filled is None else list(filled)
-    return pl.pallas_call(
-        functools.partial(project_kernel, 1 if filled is None else 2),
-        grid=(half_tokens // rows,),
-        in_specs=[pl.BlockSpec(memory_space=pl.ANY)] * len(held)
+    return run(
+        functools.partial(project_kernel, 1 if filled is None else 2), 7, (),
+        [*held, half, shifts, weight, offset],
+        [pl.BlockSpec(memory_space=pl.ANY)] * len(held)
         + [
             row_blocks(rows, model_width), constant_block(shifts.shape),
             constant_block(weight.shape), constant_block((1, width)),
         ],
-        out_specs=[row_blocks(rows, model_width, first), row_blocks(rows, width, first)],
-        out_shape=[
+        (half_tokens // rows,),
+        [row_blocks(rows, model_width, first), row_blocks(rows, width, first)],
+        [
             jax.ShapeDtypeStruct((2 * half_tokens, model_width), BF16),
             jax.ShapeDtypeStruct((2 * half_tokens, width), BF16),
         ],
-        input_output_aliases={0: 0, 1: 1} if held else {},
-        compiler_params=pltpu.CompilerParams(vmem_limit_bytes=VMEM_BYTES),
-        cost_estimate=cost(7),
-    )(*held, half, shifts, weight, offset)
+        aliases={0: 0, 1: 1} if held else {},
+    )
 
 
 def halves(rows, width, blocks):
@@ -806,11 +814,15 @@
 
 
 def merge_kernel(
-    blocks, own_ref, other_ref, weight_own, weight_other, first_ref, second_ref, grad_ref, rows_ref,
-    branch_ref, mid_ref, normed_ref, grad_b2_ref,
+    blocks, live_ref, own_ref, other_ref, weight_own, weight_other, first_ref, second_ref,
+    grad_first, grad_second, rows_ref, branch_ref, mid_ref, normed_ref, grad_ref, grad_b2_ref,
 ):
     gate1, bias, shift2, scale2, gate2 = (rows_ref[row : row + 1] for row in range(5))
-    stream = jnp.where(pl.program_id(0) < blocks // 2, first_ref[...], second_ref[...])
+    early = pl.program_id(0) < blocks // 2
+    stream = jnp.where(early, first_ref[...], second_ref[...])
+    grad = jnp.where(early, grad_first[...], grad_second[...])
+    grad = jnp.where(live_ref[0] > 0, grad, jnp.zeros_like(grad))
+    grad_ref[...] = grad
     branch = jnp.dot(own_ref[...], weight_own[...], preferred_element_type=F32)
     branch += jnp.dot(other_ref[...], weight_other[...], preferred_element_type=F32)
     branch += bias
@@ -819,28 +831,34 @@
     mid_ref[...] = mid
     norm, _ = normalize(mid)
     normed_ref[...] = (norm * (1.0 + scale2) + shift2).astype(BF16)
-    grad_b2_ref[...] = (gate2 * grad_ref[...].astype(F32)).astype(BF16)
-
-
-def merge(own, other, weight_own, weight_other, first, second, grad, vectors, rows=256):
+    grad_b2_ref[...] = (gate2 * grad.astype(F32)).astype(BF16)
+
+
+def merge(
+    live, own, other, weight_own, weight_other, first, second, grad_first, grad_second, vectors,
+    rows=256,
+):
     tokens, width = own.shape
     model_width = weight_own.shape[1]
     blocks = tokens // rows
-    part = lambda: row_blocks(rows, width)
-    full = lambda: row_blocks(rows, model_width)
+    half = blocks // 2
+    block = lambda columns: pl.BlockSpec((rows, columns), lambda i, v: (i, 0))
+    whole = lambda shape: pl.BlockSpec(shape, lambda i, v: (0,) * len(shape))
+    pair = lambda: [
+        pl.BlockSpec((rows, model_width), lambda i, v: (jnp.minimum(i, half - 1), 0)),
+        pl.BlockSpec((rows, model_width), lambda i, v: (jnp.maximum(i - half, 0), 0)),
+    ]
     shape = lambda kind: jax.ShapeDtypeStruct((tokens, model_width), kind)
-    return pl.pallas_call(
-        functools.partial(merge_kernel, blocks),
-        grid=(blocks,),
-        in_specs=[
-            part(), part(), constant_block(weight_own.shape), constant_block(weight_other.shape),
-            *halves(rows, model_width, blocks), full(), constant_block(vectors.shape),
+    return run(
+        functools.partial(merge_kernel, blocks), 11, [live],
+        [own, other, weight_own, weight_other, first, second, grad_first, grad_second, vectors],
+        [
+            block(width), block(width), whole(weight_own.shape), whole(weight_other.shape),
+            *pair(), *pair(), whole(vectors.shape),
         ],
-        out_specs=[full(), full(), full(), full()],
-        out_shape=[shape(BF16), shape(F32), shape(BF16), shape(BF16)],
-        compiler_params=pltpu.CompilerParams(vmem_limit_bytes=VMEM_BYTES),
-        cost_estimate=cost(11),
-    )(own, other, weight_own, weight_other, first, second, grad, vectors)
+        (blocks,), [block(model_width) for _ in range(5)],
+        [shape(BF16), shape(F32), shape(BF16), shape(BF16), shape(BF16)],
+    )
 
 
 def add_row_sums(sums_ref, *values):
@@ -893,26 +911,25 @@
     blocks = tokens // rows
     full = lambda: row_blocks(rows, model_width)
     shape = lambda count, columns, kind: jax.ShapeDtypeStruct((count, columns), kind)
-    return pl.pallas_call(
-        functools.partial(middle_back_kernel, blocks),
-        grid=(blocks,),
-        in_specs=[full()] * 6
+    return run(
+        functools.partial(middle_back_kernel, blocks), 17, (),
+        [branch2, back, mid, branch1, grad, grad_b2, weight_own, weight_other, vectors],
+        [full() for _ in range(6)]
         + [
             constant_block(weight_own.shape), constant_block(weight_other.shape),
             constant_block(vectors.shape),
         ],
-        out_specs=[
+        (blocks,),
+        [
             *halves(rows, model_width, blocks), full(), full(), row_blocks(rows, width),
             row_blocks(rows, width), constant_block((8, model_width)),
         ],
-        out_shape=[
+        [
             shape(tokens // 2, model_width, BF16), shape(tokens // 2, model_width, BF16),
             shape(tokens, model_width, F32), shape(tokens, model_width, BF16),
             shape(tokens, width, BF16), shape(tokens, width, BF16), shape(8, model_width, F32),
         ],
-        compiler_params=pltpu.CompilerParams(vmem_limit_bytes=VMEM_BYTES),
-        cost_estimate=cost(17),
-    )(branch2, back, mid, branch1, grad, grad_b2, weight_own, weight_other, vectors)
+    )
 
 
 def first_back_kernel(
@@ -941,29 +958,28 @@
 
 def first_back(own, other, weight_own, weight_other, first, second, grad_mid, vectors, rows=256):
     tokens, model_width = grad_mid.shape
-    width = own.shape[1]
+    width = untied(own).shape[1]
     blocks = tokens // rows
     full = lambda: row_blocks(rows, model_width)
     part = lambda: row_blocks(rows, width)
     shape = jax.ShapeDtypeStruct
-    return pl.pallas_call(
-        functools.partial(first_back_kernel, blocks),
-        grid=(blocks,),
-        in_specs=[
+    return run(
+        functools.partial(first_back_kernel, blocks), 21, (),
+        [own, other, weight_own, weight_other, first, second, grad_mid, vectors],
+        [
             part(), part(), constant_block(weight_own.shape), constant_block(weight_other.shape),
             *halves(rows, model_width, blocks), full(), constant_block(vectors.shape),
         ],
-        out_specs=[
+        (blocks,),
+        [
             *halves(rows, model_width, blocks), constant_block((8, model_width)),
             constant_block((8, width)), constant_block((8, width)),
         ],
-        out_shape=[
+        [
             shape((tokens // 2, model_width), F32), shape((tokens // 2, model_width), BF16),
             shape((8, model_width), F32), shape((8, width), F32), shape((8, width), F32),
         ],
-        compiler_params=pltpu.CompilerParams(vmem_limit_bytes=VMEM_BYTES),
-        cost_estimate=cost(21),
-    )(own, other, weight_own, weight_other, first, second, grad_mid, vectors)
+    )
 
 
 def bit_pairs(size, bit):
@@ -976,10 +992,6 @@
 
 def pick(values, index, axis):
     return lax.dynamic_index_in_dim(values, index, axis, keepdims=False)
-
-
-def after(values, *others):
-    return lax.optimization_barrier((values, others))[0]
 
 
 def place(first, second, index, axis=0):
@@ -1008,22 +1020,16 @@
 
 
 def cut(values, places, sizes):
-    return pl.pallas_call(
-        functools.partial(cut_kernel, sizes),
-        grid_spec=pltpu.PrefetchScalarGridSpec(
-            num_scalar_prefetch=1,
-            grid=(1,),
-            in_specs=[pl.BlockSpec(memory_space=pl.ANY)] * len(sizes),
-            out_specs=[pl.BlockSpec(memory_space=pltpu.VMEM)] * len(sizes),
-            scratch_shapes=[pltpu.SemaphoreType.DMA((len(sizes),))],
-        ),
-        out_shape=[
-            jax.ShapeDtypeStruct((size,) + value.shape[1:], value.dtype)
+    return run(
+        functools.partial(cut_kernel, sizes), 0, [jnp.stack(places).astype(jnp.int32)], list(values),
+        [pl.BlockSpec(memory_space=pl.ANY)] * len(sizes), (1,),
+        [pl.BlockSpec(memory_space=pltpu.VMEM)] * len(sizes),
+        [
+            jax.ShapeDtypeStruct((size,) + untied(value).shape[1:], untied(value).dtype)
             for value, size in zip(values, sizes)
         ],
-        compiler_params=pltpu.CompilerParams(vmem_limit_bytes=VMEM_BYTES),
-        cost_estimate=cost(5),
-    )(jnp.stack(places).astype(jnp.int32), *values)
+        [pltpu.SemaphoreType.DMA((len(sizes),))],
+    )
 
 
 def joined_kernel(count, places_ref, *refs):
@@ -1045,20 +1051,33 @@
 
 def joined(pieces, places):
     count = len(pieces)
-    rows, width = pieces[0].shape
-    return pl.pallas_call(
-        functools.partial(joined_kernel, count),
-        grid_spec=pltpu.PrefetchScalarGridSpec(
-            num_scalar_prefetch=1,
-            grid=(1,),
-            in_specs=[pl.BlockSpec(memory_space=pltpu.VMEM)] * count,
-            out_specs=pl.BlockSpec(memory_space=pl.ANY),
-            scratch_shapes=[pltpu.SemaphoreType.DMA((count,))],
-        ),
-        out_shape=jax.ShapeDtypeStruct((count * rows, width), pieces[0].dtype),
-        compiler_params=pltpu.CompilerParams(vmem_limit_bytes=VMEM_BYTES),
-        cost_estimate=cost(5),
-    )(places, *pieces)
+    rows, width = untied(pieces[0]).shape
+    return run(
+        functools.partial(joined_kernel, count), 0, [places], list(pieces),
+        [pl.BlockSpec(memory_space=pltpu.VMEM)] * count, (1,), pl.BlockSpec(memory_space=pl.ANY),
+        jax.ShapeDtypeStruct((count * rows, width), BF16),
+        [pltpu.SemaphoreType.DMA((count,))],
+    )
+
+
+def added_kernel(left_ref, right_ref, out_ref):
+    out_ref[...] = (left_ref[...].astype(F32) + right_ref[...].astype(F32)).astype(BF16)
+
+
+def added(left, right, *behind):
+    whole = pl.BlockSpec(memory_space=pltpu.VMEM)
+    out = jax.ShapeDtypeStruct(left.shape, BF16)
+    return run(added_kernel, 0, (), [after(left, *behind), right], [whole, whole], (), whole, out)
+
+
+def relay_kernel(value_ref, out_ref):
+    out_ref[...] = value_ref[...]
+
+
+def relay(value, *behind):
+    whole = pl.BlockSpec(memory_space=pltpu.VMEM)
+    out = jax.ShapeDtypeStruct(value.shape, value.dtype)
+    return run(relay_kernel, 0, (), [after(value, *behind)], [whole], (), whole, out)
 
 
 def gather_dp(values):
@@ -1113,28 +1132,33 @@
     )
     places = places.astype(jnp.int32)
 
-    def fetch(values, *behind):
-        return swap(after(values, *behind), "tensor", 1)
-
-    def pass_first(got, *behind):
-        got = after(got, *behind)
+    def fetch(values):
+        return swap(values, "tensor", 1)
+
+    def pass_on(got):
         return got, swap(got, "dp", 4), swap(got, "dp", 1)
 
-    def pass_second(passed, *behind):
+    def pass_last(passed, *behind):
         got, from_near, from_core = passed
-        from_near = after(from_near, *behind)
-        return got, from_near, from_core, swap(from_near, "dp", 1)
-
+        to_core = relay(from_near, *behind) if behind else from_near
+        return got, from_near, from_core, swap(to_core, "dp", 1)
+
+    def joined_after(passed, *behind):
+        return joined((after(passed[0], *behind),) + passed[1:], places)
+
+    def quarter_of(weight, *behind):
+        return cut((after(weight, *behind),), (quarter,), (weight.shape[0] // 4,))[0]
+
+    latent_own, latent_sent, cotangent_own = cut(
+        (latents, latents, cotangent), (side, 1 - side, side), (1, 1, 1)
+    )
+    latent_other = fetch(latent_sent[0])
     heads_own = heads_weight[0].reshape(model_width, 3 * columns)
-    (heads_quarter,) = cut((heads_own,), (quarter,), (model_width // 4,))
-    heads_got = swap(heads_quarter, "tensor", 1)
-    sizes = tuple(value.shape[0] // 4 for value in (merge_own, up_own, down_own))
-    latent_own, latent_sent, cotangent_own, cotangent_sent, merge_quarter, up_quarter, down_quarter = cut(
-        (after(latents, heads_quarter), latents, cotangent, cotangent, merge_own, up_own, down_own),
-        (side, 1 - side, side, 1 - side, quarter, quarter, quarter),
-        (1, 1, 1, 1) + sizes,
-    )
-    condition = after(condition, latent_sent)
+    core_places = jnp.stack([core, 1 - core]).astype(jnp.int32)
+
+    def half_of(weight, *behind):
+        return cut((after(weight, *behind),), (core,), (weight.shape[0] // 2,))[0]
+
     silu_cond = jax.nn.silu(condition.astype(F32)).astype(BF16)
     local_mod = jnp.einsum(
         "sd,dkc->skc", silu_cond, modulate_weight[0], preferred_element_type=F32
@@ -1154,92 +1178,96 @@
     up_bias_other = bias_pack[2 * columns :].reshape(1, hidden_here).astype(F32)
     shifts1 = padded_rows(shift1, scale1)
 
-    heads_passed = pass_first(heads_got, shifts1)
-    latent_other = fetch(latent_sent[0], heads_passed[0])
+    heads_half = half_of(heads_own, latent_sent)
+    heads_got = fetch(heads_half)
     filled = normed_project(
-        after(latent_own[0], heads_passed[0]), shifts1, heads_own, offset_own
-    )
-    heads_passed = pass_second(heads_passed, filled[0])
-    merge_got = fetch(merge_quarter, latent_other)
-    cotangent_other = fetch(cotangent_sent[0], latent_other)
-    normed1, qkv_own = normed_project(
-        after(latent_other, heads_passed[1]), shifts1, heads_own, offset_own, filled
-    )
-    heads_other = joined((after(heads_passed[0], normed1),) + heads_passed[1:], places)
+        after(latent_own[0], heads_half), shifts1, heads_own, offset_own
+    )
+    normed1, qkv_own = normed_project(latent_other, shifts1, heads_own, offset_own, filled)
+    attended_own, logsum_own = attend(qkv_own)
+    heads_got = relay(heads_got, attended_own)
+    heads_core = swap(heads_got, "dp", 1)
+    merge_half_own = half_of(merge_own, heads_got)
+    (cotangent_sent,) = cut((after(cotangent, merge_half_own),), (1 - side,), (1,))
+    merge_got = fetch(merge_half_own)
+    cotangent_other = fetch(cotangent_sent[0])
+    heads_other = joined((after(heads_got, cotangent_sent), heads_core), core_places)
     qkv_other = project(normed1, heads_other, offset_other)
-    attended_own, logsum_own = attend(after(qkv_own, qkv_other))
-    merge_passed = pass_first(merge_got, attended_own)
-    cotangent_other = after(cotangent_other, attended_own)
-    up_got = fetch(up_quarter, cotangent_other)
-    attended_other, logsum_other = attend(after(qkv_other, merge_passed[0], cotangent_other))
-    merge_passed = pass_second(merge_passed, attended_other)
-    merge_other = joined((after(merge_passed[0], attended_other),) + merge_passed[1:], places)
-    grad = jnp.concatenate([cotangent_own[0], cotangent_other], 0)
-    grad = jnp.where(side < group_counts[0], grad, jnp.zeros_like(grad))
-    branch1, mid, normed2, grad_b2 = merge(
-        attended_own, attended_other, merge_own, merge_other, latent_own[0], latent_other, grad,
-        padded_rows(gate1, merge_bias[0].astype(F32), shift2, scale2, gate2),
-    )
-    up_passed = pass_first(up_got, normed2)
-    down_got = fetch(down_quarter, up_passed[0])
-    normed1_peer = swap(after(normed1, normed2), "dp", 1)
+    attended_other, logsum_other = attend(qkv_other)
+    up_quarter = quarter_of(up_own, attended_other)
+    up_passed = pass_on(fetch(up_quarter))
+    merge_got = relay(merge_got, up_quarter)
+    merge_other = joined((merge_got, swap(merge_got, "dp", 1)), core_places)
+    live = bit_value(side < group_counts[0])
+    branch1, mid, normed2, grad, grad_b2 = merge(
+        live, attended_own, attended_other, merge_own, merge_other, latent_own[0], latent_other, cotangent_own[0],
+        cotangent_other, padded_rows(gate1, merge_bias[0].astype(F32), shift2, scale2, gate2),
+    )
+    down_half = half_of(down_own, normed2)
+    down_got = fetch(down_half)
+    normed1_peer = swap(normed1, "dp", 1)
     normed2_peer = swap(normed2, "dp", 1)
     grad_b2_peer = swap(grad_b2, "dp", 1)
     branch2, back2, *hidden_own, up_sums_own = feed(
-        core_value, after(normed2, up_passed[0]), grad_b2, up_own, up_bias_own, down_own
+        core_value, after(normed2, down_half), grad_b2, up_own, up_bias_own, down_own
     )
     hidden_sent_own, hidden_own, pre_sent_own, pre_own = hidden_own
     hidden_peer_own, pre_peer_own = swap(hidden_sent_own, "dp", 1), swap(pre_sent_own, "dp", 1)
-    up_passed = pass_second(up_passed, hidden_own)
-    down_passed = pass_first(down_got, hidden_own)
 
     far_of, near_of, x_of = (
         jnp.arange(8, dtype=jnp.int32) // step % 2 for step in (4, 2, 1)
     )
     where_x = 4 * (x_of == x_bit) + 2 * far_of + near_of
     where_near = 4 * (near_of == near) + 2 * far_of + x_of
-    x_first = (bit_value(2 * far + near), (4, 8, 12))
-    near_first = (bit_value(2 * far + x_bit), (2, 8, 10))
-
-    def spread(kept, received, order, *behind):
-        base, masks = order
-        kept, *sent = add_split(base, after(kept, *behind), received)
-        return kept, [swap(part, "dp", mask) for part, mask in zip(sent, masks)]
-
-    def block_total(kept, received, *behind):
-        received = after(received, *behind)
-        return sum((part.astype(F32) for part in received), kept.astype(F32))
-
-    def pair_total(own, other, first, second):
-        other = block_total(*other, first).astype(BF16)
-        return block_total(*own, first) + after(swap(other, "tensor", 1), second).astype(F32)
-
-    def join_cores(total, *behind):
+    near_next = (near, 4)
+    x_next = (x_bit, 2)
+
+    def halved(kept, received, step, *behind):
+        sent, kept = halve(bit_value(step[0]), kept, after(received, *behind))
+        return kept, swap(sent, "dp", step[1])
+
+    def halved_last(pairs, *behind):
+        halves_here = [
+            halve(bit_value(far), kept, after(received, *behind)) for kept, received in pairs
+        ]
+        sent = jnp.concatenate([sent[0] for sent, _ in halves_here], 1)
+        return jnp.concatenate([kept[0] for _, kept in halves_here], 1), swap(sent, "dp", 8)
+
+    def pair_total(own, other, *behind):
+        return own.astype(F32) + swap(other, "tensor", 1).astype(F32)
+
+    def swap_rows(total, *behind):
         total = total.astype(BF16).reshape((2, -1) + total.shape[1:])
-        sent = after(swap(pick(total, 1 - core, 0), "dp", 1), *behind)
-        return place(pick(total, core, 0), sent, core, total.ndim - 2).astype(F32)
-
-    up_other = joined((after(up_passed[0], hidden_own),) + up_passed[1:], places)
+        return pick(total, core, 0), swap(pick(total, 1 - core, 0), "dp", 1)
+
+    def join_columns(mine, others):
+        return place(mine, others, core, mine.ndim - 1).astype(F32)
+
     down_parts_own = weight_grad(
-        where_x, grad_b2, after(grad_b2_peer, up_other), hidden_own, hidden_peer_own
+        where_x, grad_b2, after(grad_b2_peer, normed2), hidden_own, hidden_peer_own
     )
     down_first_own = swap(down_parts_own[0], "dp", 2)
     up_parts_own = weight_grad(
-        where_near, after(normed2, down_parts_own[0]), normed2_peer, pre_own, pre_peer_own
+        where_near, after(normed2, down_parts_own[0]), normed2_peer, pre_own, pre_peer_own,
+        weight=13,
     )
     up_first_own = swap(up_parts_own[0], "dp", 4)
-    down_passed = pass_second(down_passed, up_parts_own[0])
-    down_other = joined((after(down_passed[0], up_parts_own[0]),) + down_passed[1:], places)
+    up_passed = pass_last(up_passed, up_parts_own[0])
+    down_pieces = (down_got, swap(down_got, "dp", 1))
+    up_other = joined_after(up_passed, up_parts_own[0])
+    down_other = joined(
+        (after(down_pieces[0], up_other), down_pieces[1]), core_places
+    )
     branch2, back2, *hidden_other, up_sums_other = feed(
         core_value, normed2, grad_b2, up_other, up_bias_other, down_other, (branch2, back2)
     )
     hidden_sent_other, hidden_other, pre_sent_other, pre_other = hidden_other
     hidden_peer_other = swap(hidden_sent_other, "dp", 1)
     pre_peer_other = swap(pre_sent_other, "dp", 1)
-    down_spread_own = spread(down_parts_own[1], down_first_own, x_first, hidden_other)
-    up_spread_own = spread(up_parts_own[1], up_first_own, near_first, hidden_other)
+    down_half_own = halved(down_parts_own[1], down_first_own, near_next, hidden_other)
+    up_half_own = halved(up_parts_own[1], up_first_own, x_next, hidden_other)
     output_own, output_sent, grad_mid, grad_b1, grad_att_own, grad_att_other, middle_sums = middle_back(
-        after(branch2, down_spread_own[0], up_spread_own[0]), back2, mid, branch1, grad, grad_b2,
+        after(branch2, down_half_own[0], up_half_own[0]), back2, mid, branch1, grad, grad_b2,
         merge_own, merge_other, padded_rows(gate1, down_bias[0].astype(F32), scale2, gate2),
     )
     grad_gate2, down_bias_sum, grad_shift2, grad_scale2, grad_gate1, merge_bias_sum = middle_sums[:6]
@@ -1252,57 +1280,71 @@
         where_near, after(normed2, down_parts_other[0]), normed2_peer, pre_other, pre_peer_other
     )
     up_first_other = swap(up_parts_other[0], "dp", 4)
-    output_other = swap(after(output_sent, up_parts_other[0]), "tensor", 1)
+    output_other = swap(output_sent, "tensor", 1)
     grads_own, sent_own, kept_own = attend_back(
         core_value, qkv_own, attended_own, after(grad_att_own, up_parts_other[0]), logsum_own
     )
     heads_peer_own = swap(sent_own, "dp", 1)
-    down_spread_other = spread(down_parts_other[1], down_first_other, x_first, grads_own)
-    up_spread_other = spread(up_parts_other[1], up_first_other, near_first, grads_own)
     merge_total = outer_rows(
-        after(grad_b1, down_spread_other[0], up_spread_other[0]),
+        grad_b1,
         jnp.concatenate([attended_own, attended_other], 1),
     ).astype(BF16).reshape(8, 2, -1, 2 * columns)
     merge_sent = swap(pick(merge_total, 1 - core, 1), "dp", 1)
-    heads_parts_own = weight_grad(
-        where_x, normed1, after(normed1_peer, merge_total), kept_own, heads_peer_own
-    )
-    heads_first_own = swap(heads_parts_own[0], "dp", 2)
-    output_other = after(output_other, heads_parts_own[0])
+    merge_total = pick(merge_total, core, 1).astype(F32) + merge_sent.astype(F32)
+    merge_total = merge_total.astype(BF16).reshape((2, 2, 2) + merge_total.shape[1:])
+    merge_first = swap(pick(merge_total, 1 - near, 1), "dp", 4)
+    merge_kept = pick(merge_total, near, 1).reshape((4,) + merge_total.shape[3:])
+    merge_first = merge_first.reshape(merge_kept.shape)
+    down_half_other = halved(down_parts_other[1], down_first_other, near_next, grads_own)
+    up_half_other = halved(up_parts_other[1], up_first_other, x_next, grads_own)
+    feed_last_own = halved_last([down_half_own, up_half_own], down_half_other[0], up_half_other[0])
     block_output = place(output_own[None], output_other[None], side)
     grads_other, sent_other, kept_other = attend_back(
-        core_value, qkv_other, attended_other, after(grad_att_other, heads_parts_own[0]), logsum_other
+        core_value, qkv_other, attended_other,
+        after(grad_att_other, feed_last_own[0], down_half_other[0], up_half_other[0]), logsum_other,
     )
     heads_peer_other = swap(sent_other, "dp", 1)
-    heads_spread_own = spread(heads_parts_own[1], heads_first_own, x_first, grads_other)
+    feed_last_other = halved_last([down_half_other, up_half_other], grads_other)
+    heads_parts_own = weight_grad(
+        where_x, normed1, after(normed1_peer, feed_last_other[0], merge_kept),
+        kept_own, heads_peer_own, weight=13,
+    )
+    heads_first_own = swap(heads_parts_own[0], "dp", 2)
     heads_parts_other = weight_grad(
-        where_near, normed1, after(normed1_peer, heads_spread_own[0]), kept_other, heads_peer_other
-    )
-    heads_first_other = swap(heads_parts_other[0], "dp", 4)
-    merge_sent = after(merge_sent, heads_parts_own[0])
-    merge_total = pick(merge_total, core, 1).astype(F32) + merge_sent.astype(F32)
-    merge_total = merge_total.astype(BF16).reshape((2, 2, 2) + merge_total.shape[1:])
-    merge_first = swap(pick(after(merge_total, grads_other), 1 - x_bit, 2), "dp", 2)
-    merge_kept = pick(merge_total, x_bit, 2).reshape((4,) + merge_total.shape[3:])
-    merge_first = merge_first.reshape(merge_kept.shape)
-    down_grad = pair_total(down_spread_own, down_spread_other, grads_other, heads_parts_other[0])
-    up_grad = pair_total(up_spread_own, up_spread_other, grads_other, heads_parts_other[0])
+        where_x, normed1, after(normed1_peer, heads_parts_own[0]), kept_other, heads_peer_other
+    )
+    heads_first_other = swap(heads_parts_other[0], "dp", 2)
+    done = heads_parts_other[0]
+    merge_half = halved(merge_kept, merge_first, x_next, done)
+    feed_own = added(*feed_last_own, done)
     grad_latent, latent_sent, first_sums, heads_sums_own, heads_sums_other = first_back(
-        grads_own, after(grads_other, heads_parts_other[0], down_grad, up_grad), heads_own, heads_other,
+        grads_own, after(grads_other, done, merge_half[0], feed_own), heads_own, heads_other,
         latent_own[0], latent_other, grad_mid, padded_rows(scale1),
     )
-    heads_spread_other = spread(heads_parts_other[1], heads_first_other, near_first, grad_latent)
-    latent_sent = swap(after(latent_sent, heads_spread_other[0]), "tensor", 1).astype(F32)
-    down_grad = join_cores(down_grad, grad_latent)
-    up_grad = join_cores(up_grad, grad_latent)
+    heads_half_own = halved(heads_parts_own[1], heads_first_own, near_next, grad_latent)
+    heads_half_other = halved(
+        heads_parts_other[1], heads_first_other, near_next, heads_half_own[0]
+    )
+    latent_sent = swap(latent_sent, "tensor", 1)
+    feed_other = added(*feed_last_other, heads_half_other[0])
+    feed_total = pair_total(feed_own, feed_other)
+    merge_last = halved_last([merge_half], feed_other)
+    heads_last = halved_last([heads_half_own, heads_half_other], feed_other)
+    feed_mine, feed_others = swap_rows(feed_total)
+    cut_at = feed_mine.shape[1] // 2
+    down_grad = join_columns(feed_mine[:, :cut_at], feed_others[:, :cut_at])
+    up_grad = join_columns(feed_mine[:, cut_at:], feed_others[:, cut_at:])
     grad_shift1, grad_scale1 = first_sums[0], first_sums[1]
-    merge_spread = spread(merge_kept, merge_first, x_first, heads_spread_other[0])
-    heads_grad = pair_total(heads_spread_own, heads_spread_other, grad_latent, grad_latent)
-    heads_grad = heads_grad[:, : 3 * columns // 2]
-    heads_grad = join_cores(heads_grad.reshape(heads_grad.shape[0], 3, columns // 2))
-    merge_total = block_total(*merge_spread)
-    merge_sent = swap(merge_total[:, columns:].astype(BF16), "tensor", 1)
-    merge_grad = merge_total[:, :columns] + merge_sent.astype(F32)
+    merge_total = added(*merge_last, heads_last[0])
+    heads_total = added(*heads_last, merge_total)
+    cut_at = heads_total.shape[1] // 2
+    heads_total = pair_total(heads_total[:, :cut_at], heads_total[:, cut_at:])
+    latent_sent = latent_sent.astype(F32)
+    heads_total = heads_total[:, : 3 * columns // 2]
+    heads_grad = join_columns(
+        *swap_rows(heads_total.reshape(heads_total.shape[0], 3, columns // 2))
+    )
+    merge_grad = pair_total(merge_total[:, :columns], merge_total[:, columns:], latent_sent)
 
     def query_value_sums(sums):
         return jnp.concatenate([sums[0, :columns], sums[0, 2 * columns :]])
@@ -1315,9 +1357,6 @@
         [grad_shift1, grad_scale1, grad_gate1, grad_shift2, grad_scale2, grad_gate2]
     ).astype(BF16)
     grad_mod_own, grad_mod_sent = by_side(grad_mod)
-    grad_mod_slots = place(
-        grad_mod_own[None], swap(grad_mod_sent, "tensor", 1)[None], side
-    )
     merge_own_sum, merge_other_sum = by_side(merge_bias_sum)
     down_own_sum, down_other_sum = by_side(down_bias_sum)
     bias_own = jnp.concatenate(
@@ -1326,8 +1365,13 @@
     bias_other = jnp.concatenate(
         [query_value_sums(heads_sums_other), merge_other_sum, up_sums_other[0], down_other_sum]
     )
-    bias_total = bias_own + swap(bias_other, "tensor", 1)
-    bias_total = sum_dp(bias_total)
+    crossing = jnp.concatenate([bias_other, grad_mod_sent.astype(F32).reshape(-1)])
+    crossing = swap(relay(crossing.reshape(-1, 128), heads_last[0]), "tensor", 1).reshape(-1)
+    bias_total = sum_dp(bias_own + crossing[: bias_own.shape[0]])
+    grad_mod_slots = place(
+        grad_mod_own[None],
+        crossing[bias_own.shape[0] :].astype(BF16).reshape(grad_mod_own[None].shape), side,
+    )
     slots_here = silu_cond.shape[0]
     tail = jnp.concatenate([silu_cond, grad_mod_slots.reshape(slots_here, -1)], 1)
     tail_all = gather_dp(tail)

time: 703 us -> 659 us (0.937)
  waiting for transfers between devices: 149 us -> 85.8 us
  Pallas kernels: 382 us -> 421 us
  starting transfers between devices: 87.6 us -> 50.2 us
    ppermute x78 -> x59, waiting for transfers between devices: 149 us -> 85.8 us  [swap(): return lax.ppermute(values, axis, bit_pairs(lax.axis_size(axis), bit))]
    pallas_call x31 -> x50, Pallas kernels: 382 us -> 421 us  [run(): pl.pallas_call(without_ties, grid_spec=pltpu.PrefetchScalarGridSpec(num_s...]
    ppermute x78 -> x59, starting transfers between devices: 87.6 us -> 50.2 us  [swap(): return lax.ppermute(values, axis, bit_pairs(lax.axis_size(axis), bit))]
    unnamed x131 -> x103, local copies, waits for them, and re-layouts: 6.59 us -> 15 us
    concatenate x0 -> x6, other arithmetic: none -> 8.36 us  [the longest x3 5.49 us: halved_last(): jnp.concatenate([kept[0] for _, kept in halves_here], 1)]
  transfers between devices with their start and end apart: 78 -> 59, of which waited for: 23 -> 15; matrix products, arithmetic and copies ran while one was open for 9% -> 10% of each run, Pallas kernels for 54% -> 64%
where the time goes in v3:
time: 659 us; the launch traced here: 648 us
  Pallas kernels  421 us (64%)
  waiting for transfers between devices  85.8 us (13%)
  starting transfers between devices  50.2 us (8%)
  local copies, waits for them, and re-layouts  37.4 us (6%)
  other arithmetic  34 us (5%)
  matrix products  17.2 us (3%)
    pallas_call x50, Pallas kernels, run(): pl.pallas_call(without_ties, grid_spec=pltpu.PrefetchScalarGridSpec(num_s...  421 us
    ppermute x59, waiting for transfers between devices, swap(): return lax.ppermute(values, axis, bit_pairs(lax.axis_size(axis), bit))  85.8 us
    ppermute x59, starting transfers between devices, swap(): return lax.ppermute(values, axis, bit_pairs(lax.axis_size(axis), bit))  50.2 us
    unnamed x103, local copies, waits for them, and re-layouts  15 us
  transfers between devices with their start and end apart: 59, of which 15 were waited for; matrix products, arithmetic and copies ran while one was open for 10% of the time, Pallas kernels for 64%

profile of v3, /device:TPU:0, one launch (start us, length us, event | category | flops | bytes accessed | tf_op | source)
XLA Modules:
  0.0 648.1 jit_solution(9035989051049326140)
XLA Ops:
  1.4 5.6 fusion.11
  7.0 3.0 collective-permute-start
  10.6 4.4 shard_map.237
  15.1 6.4 copy.48.refs_1_.refs_2_.refs_4_
  21.5 2.9 shard_map.238.refs_4_
  29.2 6.7 %shard_map.239 = (bf16[1024,1152]{1,0:T(8,128)(2,1)}, bf16[1024,1728]{1,0:T(8,128)(2,1)}) custom-call(bf16[512,1152]{1,0:T(8,128)(2,1)} %bitcast.162, f32[8,1152]{1,0:T(8,128)} %pad.16.refs_1_.refs_3_, bf16[1152,1728]{1,0:T(8,128)(2,1)} %copy.48.refs_1_.refs_2_.refs_4_, f32[1,1728]{1,0:T(1,128)} %convert_element_type.161.refs_3_.refs_5_, ...), custom_call_target="tpu_custom_call" | custom-call | flops 35000000512 | bytes 100000 | tf_op jit(solution)/shard_map/pallas_call | solution.py:483
  35.9 8.4 %collective-permute-done.1.refs_2_.refs_6_.refs_5_ = bf16[512,1152]{1,0:T(8,128)(2,1)S(1)} collective-permute-done((bf16[512,1152]{1,0:T(8,128)(2,1)}, bf16[512,1152]{1,0:T(8,128)(2,1)S(1)}, u32[]{:S(2)}, u32[]{:S(2)}) %collective-permute-start.1) | collective-permute-done | bytes 1179680 | tf_op jit(solution)/shard_map/ppermute | solution.py:990
  45.2 6.6 %shard_map.240 = (bf16[1024,1152]{1,0:T(8,128)(2,1)}, bf16[1024,1728]{1,0:T(8,128)(2,1)}) custom-call(bf16[1024,1152]{1,0:T(8,128)(2,1)} %get-tuple-element.103.refs_0_, bf16[1024,1728]{1,0:T(8,128)(2,1)} %get-tuple-element.104.refs_1_, bf16[512,1152]{1,0:T(8,128)(2,1)} %copy-done.48, ...), custom_call_target="tpu_custom_call", output_to_operand_aliasing={{0}: (0, {}), {1}: (1, {})} | custom-call | flops 35000000512 | bytes 100000 | tf_op jit(solution)/shard_map/pallas_call | solution.py:483
  51.9 17.7 %shard_map.241 = (bf16[1024,576]{1,0:T(8,128)(2,1)}, f32[8,1024]{1,0:T(8,128)}) custom-call(bf16[1024,1728]{1,0:T(8,128)(2,1)} %get-tuple-element.105.refs_0_.refs_1_), custom_call_target="tpu_custom_call" | custom-call | flops 89999998976 | bytes 100000 | tf_op jit(solution)/shard_map/pallas_call | solution.py:483
  69.6 17.5 %collective-permute-done.2.refs_0_ = bf16[576,1728]{1,0:T(8,128)(2,1)} collective-permute-done((bf16[576,1728]{1,0:T(8,128)(2,1)}, bf16[576,1728]{1,0:T(8,128)(2,1)}, u32[]{:S(2)}, u32[]{:S(2)}) %collective-permute-start.2) | collective-permute-done | bytes 1990688 | tf_op jit(solution)/shard_map/ppermute | solution.py:990
  87.1 3.1 shard_map.242.refs_2_.refs_1_
  97.9 2.4 shard_map.244.refs_3_
  103.7 4.8 shard_map.245.refs_1_.refs_3_
  108.6 9.0 %shard_map.246.refs_0_.refs_1_ = bf16[1024,1728]{1,0:T(8,128)(2,1)} custom-call(bf16[1024,1152]{1,0:T(8,128)(2,1)} %get-tuple-element.107.refs_0_.refs_1_, bf16[1152,1728]{1,0:T(8,128)(2,1)} %shard_map.245.refs_1_.refs_3_, f32[1,1728]{1,0:T(1,128)} %convert_element_type.162.refs_2_), custom_call_target="tpu_custom_call" | custom-call | flops 44999999488 | bytes 100000 | tf_op jit(solution)/shard_map/pallas_call | solution.py:483
  117.5 17.7 %shard_map.247 = (bf16[1024,576]{1,0:T(8,128)(2,1)}, f32[8,1024]{1,0:T(8,128)}) custom-call(bf16[1024,1728]{1,0:T(8,128)(2,1)} %shard_map.246.refs_0_.refs_1_), custom_call_target="tpu_custom_call" | custom-call | flops 89999998976 | bytes 100000 | tf_op jit(solution)/shard_map/pallas_call | solution.py:483
  135.2 2.4 shard_map.248.refs_1_
  143.6 3.0 shard_map.250.refs_4_.refs_7_
  146.7 11.7 %shard_map.251 = (bf16[1024,1152]{1,0:T(8,128)(2,1)}, f32[1024,1152]{1,0:T(8,128)}, bf16[1024,1152]{1,0:T(8,128)(2,1)}, bf16[1024,1152]{1,0:T(8,128)(2,1)}, bf16[1024,1152]{1,0:T(8,128)(2,1)}) custom-call(s32[1]{0:T(128)} %bitcast.2.refs_0_, bf16[1024,576]{1,0:T(8,128)(2,1)} %get-tuple-element.106.refs_1_.refs_2_, ...), custom_call_target="tpu_custom_call" | custom-call | flops 54999998464 | bytes 100000 | tf_op jit(solution)/shard_map/pallas_call | solution.py:483
  158.3 3.3 shard_map.252.refs_6_
  162.7 43.4 %shard_map.253 = (f32[1024,1152]{1,0:T(8,128)}, f32[1024,1152]{1,0:T(8,128)}, bf16[1024,1152]{1,0:T(8,128)(2,1)}, bf16[1024,1152]{1,0:T(8,128)(2,1)}, bf16[1024,...) custom-call(s32[1]{0:T(128)} %bitcast.refs_0_, ...), custom_call_target="tpu_custom_call" | custom-call | flops 219999993856 | bytes 100000 | tf_op jit(solution)/shard_map/pallas_call | solution.py:483
  208.4 2.7 collective-permute-done.14.refs_4_
  212.7 5.2 collective-permute-done.13.refs_2_
  218.0 13.1 %shard_map.254 = (bf16[4,144,1152]{2,1,0:T(8,128)(2,1)}, bf16[4,144,1152]{2,1,0:T(8,128)(2,1)}) custom-call(s32[8]{0:T(128)} %fusion.41.refs_0_, bf16[1024,1152]{1,0:T(8,128)(2,1)} %get-tuple-element.111.refs_2_.refs_1_.refs_5_, bf16[1024,1152]{1,0:T(8,128)(2,1)} %collective-permute-done.13.refs_2_, bf16[1024,1152]{1,0:T(8,128)(2,1)} %get-tuple-element.114.refs_3_, ...), custom_call_target="tpu_custom_call" | custom-call | bytes 100000 | tf_op jit(solution)/shard_map/pallas_call | solution.py:483
  231.4 13.1 %shard_map.255 = (bf16[4,144,1152]{2,1,0:T(8,128)(2,1)}, bf16[4,144,1152]{2,1,0:T(8,128)(2,1)}) custom-call(s32[8]{0:T(128)} %fusion.38.refs_0_, bf16[1024,1152]{1,0:T(8,128)(2,1)} %get-tuple-element.110.refs_2_.refs_1_.refs_5_, bf16[1024,1152]{1,0:T(8,128)(2,1)} %collective-permute-done.11.refs_2_, bf16[1024,1152]{1,0:T(8,128)(2,1)} %get-tuple-element.112.refs_3_, ...), custom_call_target="tpu_custom_call" | custom-call | flops 65000001536 | bytes 100000 | tf_op jit(solution)/shard_map/pallas_call | solution.py:483
  244.5 2.5 shard_map.256
  252.5 5.6 shard_map.257.refs_3_
  258.2 5.6 shard_map.258.refs_5_
  263.7 44.7 %shard_map.259 = (f32[1024,1152]{1,0:T(8,128)}, f32[1024,1152]{1,0:T(8,128)}, bf16[1024,1152]{1,0:T(8,128)(2,1)}, bf16[1024,1152]{1,0:T(8,128)(2,1)}, bf16[1024,...) custom-call(s32[1]{0:T(128)} %bitcast.refs_0_, ...), custom_call_target="tpu_custom_call" | custom-call | flops 219999993856 | bytes 100000 | tf_op jit(solution)/shard_map/pallas_call | solution.py:483
  309.0 2.6 shard_map.260
  311.7 2.7 shard_map.261
  314.3 17.6 %shard_map.262 = (bf16[512,1152]{1,0:T(8,128)(2,1)}, bf16[512,1152]{1,0:T(8,128)(2,1)}, f32[1024,1152]{1,0:T(8,128)}, bf16[1024,1152]{1,0:T(8,128)(2,1)}, bf16[1...) custom-call(f32[1024,1152]{1,0:T(8,128)} %get-tuple-element.120.refs_0_, ...), custom_call_target="tpu_custom_call" | custom-call | flops 85000003584 | bytes 100000 | tf_op jit(solution)/shard_map/pallas_call | solution.py:483
  331.9 5.8 convolution_convert_fusion
  346.7 13.1 %shard_map.263 = (bf16[4,144,1152]{2,1,0:T(8,128)(2,1)}, bf16[4,144,1152]{2,1,0:T(8,128)(2,1)}) custom-call(s32[8]{0:T(128)} %fusion.41.refs_0_, bf16[1024,1152]{1,0:T(8,128)(2,1)} %get-tuple-element.111.refs_2_.refs_1_.refs_5_, bf16[1024,1152]{1,0:T(8,128)(2,1)} %collective-permute-done.13.refs_2_, bf16[1024,1152]{1,0:T(8,128)(2,1)} %get-tuple-element.126.refs_5_.refs_3_, ...), custom_call_target="tpu_custom_call" | custom-call | bytes 100000 | tf_op jit(solution)/shard_map/pallas_call | solution.py:483
  360.3 13.1 %shard_map.264 = (bf16[4,144,1152]{2,1,0:T(8,128)(2,1)}, bf16[4,144,1152]{2,1,0:T(8,128)(2,1)}) custom-call(s32[8]{0:T(128)} %fusion.38.refs_0_, bf16[1024,1152]{1,0:T(8,128)(2,1)} %get-tuple-element.110.refs_2_.refs_1_.refs_5_, bf16[1024,1152]{1,0:T(8,128)(2,1)} %collective-permute-done.11.refs_2_, bf16[1024,1152]{1,0:T(8,128)(2,1)} %get-tuple-element.134.refs_3_, ...), custom_call_target="tpu_custom_call" | custom-call | bytes 100000 | tf_op jit(solution)/shard_map/pallas_call | solution.py:483
  375.0 31.6 %shard_map.265 = (bf16[1024,1728]{1,0:T(8,128)(2,1)}, bf16[1024,896]{1,0:T(8,128)(2,1)}, bf16[1024,896]{1,0:T(8,128)(2,1)}) custom-call(s32[1]{0:T(128)} %bitcast.refs_0_, bf16[1024,1728]{1,0:T(8,128)(2,1)} %get-tuple-element.105.refs_0_.refs_1_, bf16[1024,576]{1,0:T(8,128)(2,1)} %get-tuple-element.106.refs_1_.refs_2_, ...), custom_call_target="tpu_custom_call" | custom-call | flops 160000000000 | bytes 100000 | tf_op jit(solution)/shard_map/pallas_call | solution.py:483
  407.6 2.6 shard_map.267
  410.3 2.6 shard_map.266
  413.5 2.2 shard_map.268
  417.2 2.2 shard_map.269
  421.2 31.9 %shard_map.270 = (bf16[1024,1728]{1,0:T(8,128)(2,1)}, bf16[1024,896]{1,0:T(8,128)(2,1)}, bf16[1024,896]{1,0:T(8,128)(2,1)}) custom-call(s32[1]{0:T(128)} %bitcast.refs_0_, bf16[1024,1728]{1,0:T(8,128)(2,1)} %shard_map.246.refs_0_.refs_1_, bf16[1024,576]{1,0:T(8,128)(2,1)} %get-tuple-element.108.refs_2_, ...), custom_call_target="tpu_custom_call" | custom-call | flops 160000000000 | bytes 100000 | tf_op jit(solution)/shard_map/pallas_call | solution.py:483
  457.0 2.6 collective-permute-start.34
  463.7 11.4 %shard_map.273 = (bf16[4,144,896]{2,1,0:T(8,128)(2,1)}, bf16[4,144,896]{2,1,0:T(8,128)(2,1)}) custom-call(s32[8]{0:T(128)} %fusion.41.refs_0_, bf16[1024,1152]{1,0:T(8,128)(2,1)} %get-tuple-element.107.refs_0_.refs_1_, bf16[1024,1152]{1,0:T(8,128)(2,1)} %collective-permute-done.27.refs_2_, bf16[1024,896]{1,0:T(8,128)(2,1)} %get-tuple-element.154.refs_3_, ...), custom_call_target="tpu_custom_call" | custom-call | flops 65000001536 | bytes 100000 | tf_op jit(solution)/shard_map/pallas_call | solution.py:483
  477.8 11.4 %shard_map.274 = (bf16[4,144,896]{2,1,0:T(8,128)(2,1)}, bf16[4,144,896]{2,1,0:T(8,128)(2,1)}) custom-call(s32[8]{0:T(128)} %fusion.41.refs_0_, bf16[1024,1152]{1,0:T(8,128)(2,1)} %get-tuple-element.107.refs_0_.refs_1_, bf16[1024,1152]{1,0:T(8,128)(2,1)} %collective-permute-done.27.refs_2_, bf16[1024,896]{1,0:T(8,128)(2,1)} %get-tuple-element.152.refs_3_, ...), custom_call_target="tpu_custom_call" | custom-call | bytes 100000 | tf_op jit(solution)/shard_map/pallas_call | solution.py:483
  492.3 2.4 shard_map.276.refs_10_
  494.7 20.9 %shard_map.277 = (f32[512,1152]{1,0:T(8,128)}, bf16[512,1152]{1,0:T(8,128)(2,1)}, f32[8,1152]{1,0:T(8,128)}, f32[8,1728]{1,0:T(8,128)}, f32[8,1728]{1,0:T(8,128)}) custom-call(bf16[1024,1728]{1,0:T(8,128)(2,1)} %get-tuple-element.140.refs_5_.refs_0_, bf16[1024,1728]{1,0:T(8,128)(2,1)} %get-tuple-element.150.refs_5_.refs_1_, ...), custom_call_target="tpu_custom_call" | custom-call | flops 105000001536 | bytes 100000 | tf_op jit(solution)/shard_map/pallas_call | solution.py:483
  520.9 2.5 shard_map.278
  524.8 4.3 maximum_select_fusion.1
  532.4 10.5 %collective-permute-done.39.refs_2_.refs_4_ = bf16[4,144,896]{2,1,0:T(8,128)(2,1)S(1)} collective-permute-done((bf16[4,144,896]{2,1,0:T(8,128)(2,1)S(1)}, bf16[4,144,896]{2,1,0:T(8,128)(2,1)S(1)}, u32[]{:S(2)}, u32[]{:S(2)}) %collective-permute-start.39) | collective-permute-done | bytes 1032224 | tf_op jit(solution)/shard_map/ppermute | solution.py:990
  543.9 2.5 shard_map.279
  546.8 4.8 collective-permute-done.38.refs_1_
  551.6 2.3 shard_map.280.refs_5_
  558.4 2.2 shard_map.281
  560.6 2.9 bitcast_convert_fusion
  564.3 2.3 shard_map.282
  570.7 4.9 maximum_select_fusion
  580.3 4.5 fusion.8
  585.9 2.6 collective-permute-done.42
  589.3 3.0 collective-permute-start.43
  596.1 2.8 collective-permute-start.50
  599.6 4.8 collective-permute-done.50
  604.4 3.5 collective-permute-start.51
  608.1 8.6 %collective-permute-done.51 = f32[4608]{0:T(1024)S(1)} collective-permute-done((f32[4608]{0:T(1024)S(1)}, f32[4608]{0:T(1024)S(1)}, u32[]{:S(2)}, u32[]{:S(2)}) %collective-permute-start.51) | collective-permute-done | bytes 18464 | tf_op jit(solution)/shard_map/ppermute | solution.py:990
  619.7 10.2 %collective-permute-done.58 = bf16[16,4608]{1,0:T(8,128)(2,1)S(1)} collective-permute-done((bf16[16,4608]{1,0:T(8,128)(2,1)S(1)}, bf16[16,4608]{1,0:T(8,128)(2,1)S(1)}, u32[]{:S(2)}, u32[]{:S(2)}) %collective-permute-start.58) | collective-permute-done | bytes 147488 | tf_op jit(solution)/shard_map/ppermute | solution.py:990
  639.0 5.4 collective-permute-done.46
  (317 shorter events, 112.2 us)
Async XLA Ops:
  7.0 20.3 %collective-permute-start = (f32[6,576]{1,0:T(8,128)S(1)}, f32[6,576]{1,0:T(8,128)S(1)}, u32[]{:S(2)}, u32[]{:S(2)}) collective-permute-start(f32[6,576]{1,0:T(8,128)S(1)} %bitcast.161), channel_id=1, source_target_pairs={{0,1},{1,0},{2,3},{3,2},{4,5},{5,4},{6,7},{7,6},{8,9},{9,8},{10,11... | collective-permute-start | bytes 41480 | tf_op jit(solution)/shard_map/ppermute | solution.py:990
  15.0 29.2 %collective-permute-start.1 = (bf16[512,1152]{1,0:T(8,128)(2,1)}, bf16[512,1152]{1,0:T(8,128)(2,1)S(1)}, u32[]{:S(2)}, u32[]{:S(2)}) collective-permute-start(bf16[512,1152]{1,0:T(8,128)(2,1)} %bitcast.142), channel_id=1, source_target_pairs={{0,1},{1,0},{2,3},{3,2},{4,5},{5,4},{6,7},{7,6},{8,9},{9,8},{10,11... | collective-permute-start | bytes 3538952 | tf_op jit(solution)/shard_map/ppermute | solution.py:990
  24.4 62.6 %collective-permute-start.2 = (bf16[576,1728]{1,0:T(8,128)(2,1)}, bf16[576,1728]{1,0:T(8,128)(2,1)}, u32[]{:S(2)}, u32[]{:S(2)}) collective-permute-start(bf16[576,1728]{1,0:T(8,128)(2,1)} %shard_map.238.refs_4_), channel_id=1, source_target_pairs={{0,1},{1,0},{2,3},{3,2},{4,5},{5,4},{6,7},{7,6},{8,9},{9,8},{10,11... | collective-permute-start | bytes 5971976 | tf_op jit(solution)/shard_map/ppermute | solution.py:990
  90.2 12.3 %collective-permute-start.3 = (bf16[576,1728]{1,0:T(8,128)(2,1)}, bf16[576,1728]{1,0:T(8,128)(2,1)S(1)}, u32[]{:S(2)}, u32[]{:S(2)}) collective-permute-start(bf16[576,1728]{1,0:T(8,128)(2,1)} %shard_map.242.refs_2_.refs_1_), channel_id=1, source_target_pairs={{0,2},{2,0},{4,6},{6,4},{8,10},{10,8},{12,14},{14,12},{16,18},{18,... | collective-permute-start | bytes 5971976 | tf_op jit(solution)/shard_map/ppermute | solution.py:990
  90.9 3.7 collective-permute-start.4
  100.4 37.3 %collective-permute-start.5 = (bf16[288,1152]{1,0:T(8,128)(2,1)S(1)}, bf16[288,1152]{1,0:T(8,128)(2,1)S(1)}, u32[]{:S(2)}, u32[]{:S(2)}) collective-permute-start(bf16[288,1152]{1,0:T(8,128)(2,1)S(1)} %copy-done.5), channel_id=1, source_target_pairs={{0,1},{1,0},{2,3},{3,2},{4,5},{5,4},{6,7},{7,6},{8,9},{9,8},{10,11... | collective-permute-start | bytes 1990664 | tf_op jit(solution)/shard_map/ppermute | solution.py:990
  100.7 46.0 %collective-permute-start.7 = (bf16[512,1152]{1,0:T(8,128)(2,1)}, bf16[512,1152]{1,0:T(8,128)(2,1)}, u32[]{:S(2)}, u32[]{:S(2)}) collective-permute-start(bf16[512,1152]{1,0:T(8,128)(2,1)} %bitcast.131), channel_id=1, source_target_pairs={{0,1},{1,0},{2,3},{3,2},{4,5},{5,4},{6,7},{7,6},{8,9},{9,8},{10,11... | collective-permute-start | bytes 3538952 | tf_op jit(solution)/shard_map/ppermute | solution.py:990
  140.5 2.3 collective-permute-start.6
  141.7 65.1 %collective-permute-start.8 = (bf16[288,2304]{1,0:T(8,128)(2,1)}, bf16[288,2304]{1,0:T(8,128)(2,1)}, u32[]{:S(2)}, u32[]{:S(2)}) collective-permute-start(bf16[288,2304]{1,0:T(8,128)(2,1)} %shard_map.248.refs_1_), channel_id=1, source_target_pairs={{0,1},{1,0},{2,3},{3,2},{4,5},{5,4},{6,7},{7,6},{8,9},{9,8},{10,11... | collective-permute-start | bytes 3981320 | tf_op jit(solution)/shard_map/ppermute | solution.py:990
  161.7 69.4 %collective-permute-start.16 = (bf16[1152,1152]{1,0:T(8,128)(2,1)}, bf16[1152,1152]{1,0:T(8,128)(2,1)}, u32[]{:S(2)}, u32[]{:S(2)}) collective-permute-start(bf16[1152,1152]{1,0:T(8,128)(2,1)} %shard_map.252.refs_6_), channel_id=1, source_target_pairs={{0,1},{1,0},{2,3},{3,2},{4,5},{5,4},{6,7},{7,6},{8,9},{9,8},{10,11... | collective-permute-start | bytes 7962632 | tf_op jit(solution)/shard_map/ppermute | solution.py:990
  162.7 44.1 %copy-start = (bf16[1024,1152]{1,0:T(8,128)(2,1)S(1)}, bf16[1024,1152]{1,0:T(8,128)(2,1)}, u32[]{:S(2)}) copy-start(bf16[1024,1152]{1,0:T(8,128)(2,1)} %get-tuple-element.110.refs_2_.refs_1_.refs_5_) | copy-start | bytes 7077892
  206.2 4.9 collective-permute-start.14
  206.2 11.6 %collective-permute-start.13 = (bf16[1024,1152]{1,0:T(8,128)(2,1)}, bf16[1024,1152]{1,0:T(8,128)(2,1)}, u32[]{:S(2)}, u32[]{:S(2)}) collective-permute-start(bf16[1024,1152]{1,0:T(8,128)(2,1)} %get-tuple-element.111.refs_2_.refs_1_.refs_5_), channel_id=1, source_target_pairs={{0,2},{2,0},{4,6},{6,4},{8,10},{10,8},{12,14},{14,12},{16,18},{18,... | collective-permute-start | bytes 7077896 | tf_op jit(solution)/shard_map/ppermute | solution.py:990
  206.7 24.7 %collective-permute-start.12 = (bf16[1024,1152]{1,0:T(8,128)(2,1)}, bf16[1024,1152]{1,0:T(8,128)(2,1)}, u32[]{:S(2)}, u32[]{:S(2)}) collective-permute-start(bf16[1024,1152]{1,0:T(8,128)(2,1)} %get-tuple-element.113), channel_id=1, source_target_pairs={{0,2},{2,0},{4,6},{6,4},{8,10},{10,8},{12,14},{14,12},{16,18},{18,... | collective-permute-start | bytes 7077896 | tf_op jit(solution)/shard_map/ppermute | solution.py:990
  206.8 24.6 %collective-permute-start.11 = (bf16[1024,1152]{1,0:T(8,128)(2,1)S(1)}, bf16[1024,1152]{1,0:T(8,128)(2,1)}, u32[]{:S(2)}, u32[]{:S(2)}) collective-permute-start(bf16[1024,1152]{1,0:T(8,128)(2,1)S(1)} %copy-done), channel_id=1, source_target_pairs={{0,2},{2,0},{4,6},{6,4},{8,10},{10,8},{12,14},{14,12},{16,18},{18,... | collective-permute-start | bytes 7077896 | tf_op jit(solution)/shard_map/ppermute | solution.py:990
  211.1 33.4 %collective-permute-start.9 = (bf16[288,2304]{1,0:T(8,128)(2,1)}, bf16[288,2304]{1,0:T(8,128)(2,1)}, u32[]{:S(2)}, u32[]{:S(2)}) collective-permute-start(bf16[288,2304]{1,0:T(8,128)(2,1)} %collective-permute-done.8.refs_1_), channel_id=1, source_target_pairs={{0,8},{2,10},{4,12},{6,14},{8,0},{10,2},{12,4},{14,6},{16,24},{18,... | collective-permute-start | bytes 3981320 | tf_op jit(solution)/shard_map/ppermute | solution.py:990
  217.8 33.6 %collective-permute-start.10 = (bf16[288,2304]{1,0:T(8,128)(2,1)}, bf16[288,2304]{1,0:T(8,128)(2,1)}, u32[]{:S(2)}, u32[]{:S(2)}) collective-permute-start(bf16[288,2304]{1,0:T(8,128)(2,1)} %collective-permute-done.8.refs_1_), channel_id=1, source_target_pairs={{0,2},{2,0},{4,6},{6,4},{8,10},{10,8},{12,14},{14,12},{16,18},{18,... | collective-permute-start | bytes 3981320 | tf_op jit(solution)/shard_map/ppermute | solution.py:990
  231.0 27.1 %collective-permute-start.17 = (bf16[1152,1152]{1,0:T(8,128)(2,1)}, bf16[1152,1152]{1,0:T(8,128)(2,1)}, u32[]{:S(2)}, u32[]{:S(2)}) collective-permute-start(bf16[1152,1152]{1,0:T(8,128)(2,1)} %collective-permute-done.16.refs_1_), channel_id=1, source_target_pairs={{0,2},{2,0},{4,6},{6,4},{8,10},{10,8},{12,14},{14,12},{16,18},{18,... | collective-permute-start | bytes 7962632 | tf_op jit(solution)/shard_map/ppermute | solution.py:990
  247.0 4.4 collective-permute-start.15
  248.4 63.3 %collective-permute-start.19 = (bf16[4,144,1152]{2,1,0:T(8,128)(2,1)}, bf16[4,144,1152]{2,1,0:T(8,128)(2,1)}, u32[]{:S(2)}, u32[]{:S(2)}) collective-permute-start(bf16[4,144,1152]{2,1,0:T(8,128)(2,1)} %get-tuple-element.117.refs_1_.refs_5_), channel_id=1, source_target_pairs={{0,8},{2,10},{4,12},{6,14},{8,0},{10,2},{12,4},{14,6},{16,24},{18,... | collective-permute-start | bytes 3981320 | tf_op jit(solution)/shard_map/ppermute | solution.py:990
  249.9 59.1 %collective-permute-start.18 = (bf16[4,144,1152]{2,1,0:T(8,128)(2,1)}, bf16[4,144,1152]{2,1,0:T(8,128)(2,1)}, u32[]{:S(2)}, u32[]{:S(2)}) collective-permute-start(bf16[4,144,1152]{2,1,0:T(8,128)(2,1)} %get-tuple-element.116.refs_5_), channel_id=1, source_target_pairs={{0,4},{2,6},{4,0},{6,2},{8,12},{10,14},{12,8},{14,10},{16,20},{18,... | collective-permute-start | bytes 3981320 | tf_op jit(solution)/shard_map/ppermute | solution.py:990
  308.5 38.2 %collective-permute-start.22 = (bf16[1024,1152]{1,0:T(8,128)(2,1)}, bf16[1024,1152]{1,0:T(8,128)(2,1)}, u32[]{:S(2)}, u32[]{:S(2)}) collective-permute-start(bf16[1024,1152]{1,0:T(8,128)(2,1)} %get-tuple-element.136), channel_id=1, source_target_pairs={{0,2},{2,0},{4,6},{6,4},{8,10},{10,8},{12,14},{14,12},{16,18},{18,... | collective-permute-start | bytes 7077896 | tf_op jit(solution)/shard_map/ppermute | solution.py:990
  308.5 51.8 %collective-permute-start.21 = (bf16[1024,1152]{1,0:T(8,128)(2,1)}, bf16[1024,1152]{1,0:T(8,128)(2,1)}, u32[]{:S(2)}, u32[]{:S(2)}) collective-permute-start(bf16[1024,1152]{1,0:T(8,128)(2,1)} %get-tuple-element.135), channel_id=1, source_target_pairs={{0,2},{2,0},{4,6},{6,4},{8,10},{10,8},{12,14},{14,12},{16,18},{18,... | collective-permute-start | bytes 7077896 | tf_op jit(solution)/shard_map/ppermute | solution.py:990
  338.9 3.4 collective-permute-start.32
  339.6 124.0 %collective-permute-start.27 = (bf16[1024,1152]{1,0:T(8,128)(2,1)}, bf16[1024,1152]{1,0:T(8,128)(2,1)}, u32[]{:S(2)}, u32[]{:S(2)}) collective-permute-start(bf16[1024,1152]{1,0:T(8,128)(2,1)} %get-tuple-element.107.refs_0_.refs_1_), channel_id=1, source_target_pairs={{0,2},{2,0},{4,6},{6,4},{8,10},{10,8},{12,14},{14,12},{16,18},{18,... | collective-permute-start | bytes 7077896 | tf_op jit(solution)/shard_map/ppermute | solution.py:990
  340.7 72.3 %collective-permute-start.23 = (bf16[2,144,1152]{2,1,0:T(8,128)(2,1)}, bf16[2,144,1152]{2,1,0:T(8,128)(2,1)}, u32[]{:S(2)}, u32[]{:S(2)}) collective-permute-start(bf16[2,144,1152]{2,1,0:T(8,128)(2,1)} %get-tuple-element.142), channel_id=1, source_target_pairs={{0,8},{2,10},{4,12},{6,14},{8,0},{10,2},{12,4},{14,6},{16,24},{18,... | collective-permute-start | bytes 1990664 | tf_op jit(solution)/shard_map/ppermute | solution.py:990
  342.3 73.4 %collective-permute-start.26 = (bf16[2,144,1152]{2,1,0:T(8,128)(2,1)}, bf16[2,144,1152]{2,1,0:T(8,128)(2,1)}, u32[]{:S(2)}, u32[]{:S(2)}) collective-permute-start(bf16[2,144,1152]{2,1,0:T(8,128)(2,1)} %get-tuple-element.148), channel_id=1, source_target_pairs={{0,4},{2,6},{4,0},{6,2},{8,12},{10,14},{12,8},{14,10},{16,20},{18,... | collective-permute-start | bytes 1990664 | tf_op jit(solution)/shard_map/ppermute | solution.py:990
  359.7 50.5 %collective-permute-start.24 = (bf16[4,144,1152]{2,1,0:T(8,128)(2,1)}, bf16[4,144,1152]{2,1,0:T(8,128)(2,1)}, u32[]{:S(2)}, u32[]{:S(2)}) collective-permute-start(bf16[4,144,1152]{2,1,0:T(8,128)(2,1)} %get-tuple-element.138.refs_5_), channel_id=1, source_target_pairs={{0,4},{2,6},{4,0},{6,2},{8,12},{10,14},{12,8},{14,10},{16,20},{18,... | collective-permute-start | bytes 3981320 | tf_op jit(solution)/shard_map/ppermute | solution.py:990
  373.4 33.2 %collective-permute-start.25 = (bf16[4,144,1152]{2,1,0:T(8,128)(2,1)}, bf16[4,144,1152]{2,1,0:T(8,128)(2,1)}, u32[]{:S(2)}, u32[]{:S(2)}) collective-permute-start(bf16[4,144,1152]{2,1,0:T(8,128)(2,1)} %get-tuple-element.139.refs_5_), channel_id=1, source_target_pairs={{0,8},{2,10},{4,12},{6,14},{8,0},{10,2},{12,4},{14,6},{16,24},{18,... | collective-permute-start | bytes 3981320 | tf_op jit(solution)/shard_map/ppermute | solution.py:990
  406.6 118.2 %collective-permute-start.20 = (bf16[512,1152]{1,0:T(8,128)(2,1)}, bf16[512,1152]{1,0:T(8,128)(2,1)}, u32[]{:S(2)}, u32[]{:S(2)}) collective-permute-start(bf16[512,1152]{1,0:T(8,128)(2,1)} %get-tuple-element.131), channel_id=1, source_target_pairs={{0,1},{1,0},{2,3},{3,2},{4,5},{5,4},{6,7},{7,6},{8,9},{9,8},{10,11... | collective-permute-start | bytes 3538952 | tf_op jit(solution)/shard_map/ppermute | solution.py:990
  410.3 53.4 %collective-permute-start.29 = (bf16[1024,896]{1,0:T(8,128)(2,1)}, bf16[1024,896]{1,0:T(8,128)(2,1)}, u32[]{:S(2)}, u32[]{:S(2)}) collective-permute-start(bf16[1024,896]{1,0:T(8,128)(2,1)} %get-tuple-element.155), channel_id=1, source_target_pairs={{0,2},{2,0},{4,6},{6,4},{8,10},{10,8},{12,14},{14,12},{16,18},{18,... | collective-permute-start | bytes 5505032 | tf_op jit(solution)/shard_map/ppermute | solution.py:990
  413.0 41.1 %collective-permute-start.30 = (bf16[2,144,1152]{2,1,0:T(8,128)(2,1)}, bf16[2,144,1152]{2,1,0:T(8,128)(2,1)}, u32[]{:S(2)}, u32[]{:S(2)}) collective-permute-start(bf16[2,144,1152]{2,1,0:T(8,128)(2,1)} %get-tuple-element.156), channel_id=1, source_target_pairs={{0,8},{2,10},{4,12},{6,14},{8,0},{10,2},{12,4},{14,6},{16,24},{18,... | collective-permute-start | bytes 1990664 | tf_op jit(solution)/shard_map/ppermute | solution.py:990
  415.7 41.3 %collective-permute-start.31 = (bf16[2,144,1152]{2,1,0:T(8,128)(2,1)}, bf16[2,144,1152]{2,1,0:T(8,128)(2,1)}, u32[]{:S(2)}, u32[]{:S(2)}) collective-permute-start(bf16[2,144,1152]{2,1,0:T(8,128)(2,1)} %get-tuple-element.158), channel_id=1, source_target_pairs={{0,4},{2,6},{4,0},{6,2},{8,12},{10,14},{12,8},{14,10},{16,20},{18,... | collective-permute-start | bytes 1990664 | tf_op jit(solution)/shard_map/ppermute | solution.py:990
  421.2 31.9 %copy-start.19 = (bf16[1,144,1152]{2,1,0:T(8,128)(2,1)S(1)}, bf16[1,144,1152]{2,1,0:T(8,128)(2,1)}, u32[]{:S(2)}) copy-start(bf16[1,144,1152]{2,1,0:T(8,128)(2,1)} %get-tuple-element.164) | copy-start | bytes 995332
  421.2 31.9 %copy-start.21 = (bf16[1,144,1152]{2,1,0:T(8,128)(2,1)S(1)}, bf16[1,144,1152]{2,1,0:T(8,128)(2,1)}, u32[]{:S(2)}) copy-start(bf16[1,144,1152]{2,1,0:T(8,128)(2,1)} %get-tuple-element.165) | copy-start | bytes 995332
  454.1 35.1 %collective-permute-start.33 = (bf16[2,2,72,1152]{3,2,1,0:T(8,128)(2,1)}, bf16[2,2,72,1152]{3,2,1,0:T(8,128)(2,1)S(1)}, u32[]{:S(2)}, u32[]{:S(2)}) collective-permute-start(bf16[2,2,72,1152]{3,2,1,0:T(8,128)(2,1)} %get-tuple-element.227), channel_id=1, source_target_pairs={{0,8},{2,10},{4,12},{6,14},{8,0},{10,2},{12,4},{14,6},{16,24},{18,... | collective-permute-start | bytes 1990664 | tf_op jit(solution)/shard_map/ppermute | solution.py:990
  457.0 35.3 %collective-permute-start.34 = (bf16[144,2304]{1,0:T(8,128)(2,1)}, bf16[144,2304]{1,0:T(8,128)(2,1)}, u32[]{:S(2)}, u32[]{:S(2)}) collective-permute-start(bf16[144,2304]{1,0:T(8,128)(2,1)} %pad_maximum_fusion.2), channel_id=1, source_target_pairs={{0,16},{2,18},{4,20},{6,22},{8,24},{10,26},{12,28},{14,30},{16,0},... | collective-permute-start | bytes 1990664 | tf_op jit(solution)/shard_map/ppermute | solution.py:990
  463.7 12.9 %collective-permute-start.28 = (bf16[1024,896]{1,0:T(8,128)(2,1)}, bf16[1024,896]{1,0:T(8,128)(2,1)S(1)}, u32[]{:S(2)}, u32[]{:S(2)}) collective-permute-start(bf16[1024,896]{1,0:T(8,128)(2,1)} %get-tuple-element.153), channel_id=1, source_target_pairs={{0,2},{2,0},{4,6},{6,4},{8,10},{10,8},{12,14},{14,12},{16,18},{18,... | collective-permute-start | bytes 5505032 | tf_op jit(solution)/shard_map/ppermute | solution.py:990
  475.1 44.9 %collective-permute-start.36 = (bf16[4,144,896]{2,1,0:T(8,128)(2,1)}, bf16[4,144,896]{2,1,0:T(8,128)(2,1)S(1)}, u32[]{:S(2)}, u32[]{:S(2)}) collective-permute-start(bf16[4,144,896]{2,1,0:T(8,128)(2,1)} %get-tuple-element.161.refs_5_), channel_id=1, source_target_pairs={{0,4},{2,6},{4,0},{6,2},{8,12},{10,14},{12,8},{14,10},{16,20},{18,... | collective-permute-start | bytes 3096584 | tf_op jit(solution)/shard_map/ppermute | solution.py:990
  494.7 23.1 %copy-start.18 = (bf16[1,144,1152]{2,1,0:T(8,128)(2,1)S(1)}, bf16[1,144,1152]{2,1,0:T(8,128)(2,1)}, u32[]{:S(2)}) copy-start(bf16[1,144,1152]{2,1,0:T(8,128)(2,1)} %get-tuple-element.175) | copy-start | bytes 995332
  515.6 45.1 %collective-permute-start.35 = (bf16[512,1152]{1,0:T(8,128)(2,1)}, bf16[512,1152]{1,0:T(8,128)(2,1)}, u32[]{:S(2)}, u32[]{:S(2)}) collective-permute-start(bf16[512,1152]{1,0:T(8,128)(2,1)} %get-tuple-element.167), channel_id=1, source_target_pairs={{0,1},{1,0},{2,3},{3,2},{4,5},{5,4},{6,7},{7,6},{8,9},{9,8},{10,11... | collective-permute-start | bytes 3538952 | tf_op jit(solution)/shard_map/ppermute | solution.py:990
  517.2 25.7 %collective-permute-start.39 = (bf16[4,144,896]{2,1,0:T(8,128)(2,1)S(1)}, bf16[4,144,896]{2,1,0:T(8,128)(2,1)S(1)}, u32[]{:S(2)}, u32[]{:S(2)}) collective-permute-start(bf16[4,144,896]{2,1,0:T(8,128)(2,1)S(1)} %copy-done.4), channel_id=1, source_target_pairs={{0,4},{2,6},{4,0},{6,2},{8,12},{10,14},{12,8},{14,10},{16,20},{18,... | collective-permute-start | bytes 3096584 | tf_op jit(solution)/shard_map/ppermute | solution.py:990
  519.6 32.0 %collective-permute-start.38 = (bf16[144,2304]{1,0:T(8,128)(2,1)}, bf16[144,2304]{1,0:T(8,128)(2,1)}, u32[]{:S(2)}, u32[]{:S(2)}) collective-permute-start(bf16[144,2304]{1,0:T(8,128)(2,1)} %pad_maximum_fusion.3), channel_id=1, source_target_pairs={{0,16},{2,18},{4,20},{6,22},{8,24},{10,26},{12,28},{14,30},{16,0},... | collective-permute-start | bytes 1990664 | tf_op jit(solution)/shard_map/ppermute | solution.py:990
  523.4 34.2 %collective-permute-start.37 = (bf16[2,144,896]{2,1,0:T(8,128)(2,1)}, bf16[2,144,896]{2,1,0:T(8,128)(2,1)S(1)}, u32[]{:S(2)}, u32[]{:S(2)}) collective-permute-start(bf16[2,144,896]{2,1,0:T(8,128)(2,1)} %get-tuple-element.174), channel_id=1, source_target_pairs={{0,8},{2,10},{4,12},{6,14},{8,0},{10,2},{12,4},{14,6},{16,24},{18,... | collective-permute-start | bytes 1548296 | tf_op jit(solution)/shard_map/ppermute | solution.py:990
  529.9 25.0 %collective-permute-start.44 = (bf16[2,72,1152]{2,1,0:T(8,128)(2,1)}, bf16[2,72,1152]{2,1,0:T(8,128)(2,1)S(1)}, u32[]{:S(2)}, u32[]{:S(2)}) collective-permute-start(bf16[2,72,1152]{2,1,0:T(8,128)(2,1)} %get-tuple-element.184), channel_id=1, source_target_pairs={{0,4},{2,6},{4,0},{6,2},{8,12},{10,14},{12,8},{14,10},{16,20},{18,... | collective-permute-start | bytes 995336 | tf_op jit(solution)/shard_map/ppermute | solution.py:990
  546.4 17.1 %collective-permute-start.40 = (bf16[2,144,896]{2,1,0:T(8,128)(2,1)}, bf16[2,144,896]{2,1,0:T(8,128)(2,1)S(1)}, u32[]{:S(2)}, u32[]{:S(2)}) collective-permute-start(bf16[2,144,896]{2,1,0:T(8,128)(2,1)} %get-tuple-element.180), channel_id=1, source_target_pairs={{0,8},{2,10},{4,12},{6,14},{8,0},{10,2},{12,4},{14,6},{16,24},{18,... | collective-permute-start | bytes 1548296 | tf_op jit(solution)/shard_map/ppermute | solution.py:990
  553.9 65.3 %collective-permute-start.53 = (bf16[144,2304]{1,0:T(8,128)(2,1)}, bf16[144,2304]{1,0:T(8,128)(2,1)S(1)}, u32[]{:S(2)}, u32[]{:S(2)}) collective-permute-start(bf16[144,2304]{1,0:T(8,128)(2,1)} %shard_map.280.refs_5_), channel_id=1, source_target_pairs={{0,1},{1,0},{2,3},{3,2},{4,5},{5,4},{6,7},{7,6},{8,9},{9,8},{10,11... | collective-permute-start | bytes 1990664 | tf_op jit(solution)/shard_map/ppermute | solution.py:990
  557.6 18.0 %collective-permute-start.45 = (bf16[72,1152]{1,0:T(8,128)(2,1)}, bf16[72,1152]{1,0:T(8,128)(2,1)S(1)}, u32[]{:S(2)}, u32[]{:S(2)}) collective-permute-start(bf16[72,1152]{1,0:T(8,128)(2,1)} %bitcast.166), channel_id=1, source_target_pairs={{0,16},{2,18},{4,20},{6,22},{8,24},{10,26},{12,28},{14,30},{16,0},... | collective-permute-start | bytes 497672 | tf_op jit(solution)/shard_map/ppermute | solution.py:990
  569.7 10.4 %collective-permute-start.41 = (f32[63,128]{1,0:T(8,128)}, f32[63,128]{1,0:T(8,128)S(1)}, u32[]{:S(2)}, u32[]{:S(2)}) collective-permute-start(f32[63,128]{1,0:T(8,128)} %shard_map.283), channel_id=1, source_target_pairs={{0,1},{1,0},{2,3},{3,2},{4,5},{5,4},{6,7},{7,6},{8,9},{9,8},{10,11... | collective-permute-start | bytes 96776 | tf_op jit(solution)/shard_map/ppermute | solution.py:990
  579.0 19.9 %collective-permute-start.52 = (bf16[72,576]{1,0:T(8,128)(2,1)S(1)}, bf16[72,576]{1,0:T(8,128)(2,1)S(1)}, u32[]{:S(2)}, u32[]{:S(2)}) collective-permute-start(bf16[72,576]{1,0:T(8,128)(2,1)S(1)} %slice.159), channel_id=1, source_target_pairs={{0,1},{1,0},{2,3},{3,2},{4,5},{5,4},{6,7},{7,6},{8,9},{9,8},{10,11... | collective-permute-start | bytes 248840 | tf_op jit(solution)/shard_map/ppermute | solution.py:990
  584.8 34.5 %copy-start.6 = (bf16[144,2304]{1,0:T(8,128)(2,1)S(1)}, bf16[144,2304]{1,0:T(8,128)(2,1)}, u32[]{:S(2)}) copy-start(bf16[144,2304]{1,0:T(8,128)(2,1)} %shard_map.276.refs_10_) | copy-start | bytes 1990660
  584.8 3.7 collective-permute-start.42
  585.8 6.5 collective-permute-start.48
  589.1 4.6 collective-permute-start.55
  589.3 43.3 %collective-permute-start.43 = (bf16[144,1792]{1,0:T(8,128)(2,1)S(1)}, bf16[144,1792]{1,0:T(8,128)(2,1)S(1)}, u32[]{:S(2)}, u32[]{:S(2)}) collective-permute-start(bf16[144,1792]{1,0:T(8,128)(2,1)S(1)} %pad_maximum_fusion.5), channel_id=1, source_target_pairs={{0,16},{2,18},{4,20},{6,22},{8,24},{10,26},{12,28},{14,30},{16,0},... | collective-permute-start | bytes 1548296 | tf_op jit(solution)/shard_map/ppermute | solution.py:990
  592.3 3.8 collective-permute-start.49
  593.8 14.1 %collective-permute-start.56 = (bf16[4,4608]{1,0:T(4,128)(2,1)S(1)}, bf16[4,4608]{1,0:T(4,128)(2,1)S(1)}, u32[]{:S(2)}, u32[]{:S(2)}) collective-permute-start(bf16[4,4608]{1,0:T(4,128)(2,1)S(1)} %maximum_select_fusion.9), channel_id=1, source_target_pairs={{0,4},{2,6},{4,0},{6,2},{8,12},{10,14},{12,8},{14,10},{16,20},{18,... | collective-permute-start | bytes 110600 | tf_op jit(solution)/shard_map/ppermute | solution.py:990
  596.1 8.3 %collective-permute-start.50 = (f32[4608]{0:T(1024)S(1)}, f32[4608]{0:T(1024)S(1)}, u32[]{:S(2)}, u32[]{:S(2)}) collective-permute-start(f32[4608]{0:T(1024)S(1)} %add.168), channel_id=1, source_target_pairs={{0,8},{2,10},{4,12},{6,14},{8,0},{10,2},{12,4},{14,6},{16,24},{18,... | collective-permute-start | bytes 55304 | tf_op jit(solution)/shard_map/ppermute | solution.py:990
  604.4 12.3 %collective-permute-start.51 = (f32[4608]{0:T(1024)S(1)}, f32[4608]{0:T(1024)S(1)}, u32[]{:S(2)}, u32[]{:S(2)}) collective-permute-start(f32[4608]{0:T(1024)S(1)} %add.169), channel_id=1, source_target_pairs={{0,16},{2,18},{4,20},{6,22},{8,24},{10,26},{12,28},{14,30},{16,0},... | collective-permute-start | bytes 55304 | tf_op jit(solution)/shard_map/ppermute | solution.py:990
  608.0 11.6 %collective-permute-start.57 = (bf16[8,4608]{1,0:T(8,128)(2,1)S(1)}, bf16[8,4608]{1,0:T(8,128)(2,1)S(1)}, u32[]{:S(2)}, u32[]{:S(2)}) collective-permute-start(bf16[8,4608]{1,0:T(8,128)(2,1)S(1)} %maximum_select_fusion.7), channel_id=1, source_target_pairs={{0,8},{2,10},{4,12},{6,14},{8,0},{10,2},{12,4},{14,6},{16,24},{18,... | collective-permute-start | bytes 221192 | tf_op jit(solution)/shard_map/ppermute | solution.py:990
  619.5 13.0 %collective-permute-start.54 = (bf16[72,2304]{1,0:T(8,128)(2,1)S(1)}, bf16[72,2304]{1,0:T(8,128)(2,1)S(1)}, u32[]{:S(2)}, u32[]{:S(2)}) collective-permute-start(bf16[72,2304]{1,0:T(8,128)(2,1)S(1)} %get-tuple-element.230), channel_id=1, source_target_pairs={{0,2},{2,0},{4,6},{6,4},{8,10},{10,8},{12,14},{14,12},{16,18},{18,... | collective-permute-start | bytes 995336 | tf_op jit(solution)/shard_map/ppermute | solution.py:990
  619.6 10.4 %collective-permute-start.58 = (bf16[16,4608]{1,0:T(8,128)(2,1)S(1)}, bf16[16,4608]{1,0:T(8,128)(2,1)S(1)}, u32[]{:S(2)}, u32[]{:S(2)}) collective-permute-start(bf16[16,4608]{1,0:T(8,128)(2,1)S(1)} %maximum_select_fusion.6), channel_id=1, source_target_pairs={{0,16},{2,18},{4,20},{6,22},{8,24},{10,26},{12,28},{14,30},{16,0},... | collective-permute-start | bytes 442376 | tf_op jit(solution)/shard_map/ppermute | solution.py:990
  636.6 7.9 %collective-permute-start.46 = (bf16[144,896]{1,0:T(8,128)(2,1)S(1)}, bf16[144,896]{1,0:T(8,128)(2,1)S(1)}, u32[]{:S(2)}, u32[]{:S(2)}) collective-permute-start(bf16[144,896]{1,0:T(8,128)(2,1)S(1)} %get-tuple-element.232), channel_id=1, source_target_pairs={{0,1},{1,0},{2,3},{3,2},{4,5},{5,4},{6,7},{7,6},{8,9},{9,8},{10,11... | collective-permute-start | bytes 774152 | tf_op jit(solution)/shard_map/ppermute | solution.py:990
  645.0 1.5 collective-permute-start.47
  (44 other events, 262.3 us)

commit v4 on v3

--- a/solution.py
+++ b/solution.py
@@ -521,7 +521,7 @@
         logsum_ref[head : head + 1, :] = top * SCORE_LOG2 + jnp.log2(total)
 
 
-def attend(qkv, query_rows=512):
+def attend(qkv, query_rows=1024):
     tokens, width = untied(qkv).shape[0], untied(qkv).shape[1] // 3
     heads = width // HEAD_DIM
     return run(
@@ -594,7 +594,7 @@
                 sent_ref[:, rest] = jnp.zeros_like(sent_ref[:, rest])
 
 
-def attend_back(core, qkv, attended, grad_attended, logsum, key_rows=512):
+def attend_back(core, qkv, attended, grad_attended, logsum, key_rows=1024):
     tokens, width = attended.shape
     heads = width // HEAD_DIM
     steps = tokens // key_rows
@@ -669,7 +669,7 @@
             )
 
 
-def feed(core, normed, grad, up, bias, down, carried=(), token_rows=256):
+def feed(core, normed, grad, up, bias, down, carried=(), token_rows=512):
     tokens, model_width = untied(normed).shape
     hidden_here = up.shape[1]
     width = hidden_here // 2

time: 659 us -> 645 us (0.979)
  Pallas kernels: 421 us -> 408 us
    pallas_call x50, Pallas kernels: 421 us -> 408 us  [run(): pl.pallas_call(without_ties, grid_spec=pltpu.PrefetchScalarGridSpec(num_s...]
  transfers between devices with their start and end apart: 59 -> 59, of which waited for: 15 -> 16; matrix products, arithmetic and copies ran while one was open for 10% -> 10% of each run, Pallas kernels for 64% -> 63%
where the time goes in v4:
time: 645 us; the launch traced here: 639 us
  Pallas kernels  408 us (63%)
  waiting for transfers between devices  91.7 us (14%)
  starting transfers between devices  47.9 us (7%)
  local copies, waits for them, and re-layouts  37.4 us (6%)
  other arithmetic  34 us (5%)
  matrix products  17.2 us (3%)
    pallas_call x50, Pallas kernels, run(): pl.pallas_call(without_ties, grid_spec=pltpu.PrefetchScalarGridSpec(num_s...  408 us
    ppermute x59, waiting for transfers between devices, swap(): return lax.ppermute(values, axis, bit_pairs(lax.axis_size(axis), bit))  91.7 us
    ppermute x59, starting transfers between devices, swap(): return lax.ppermute(values, axis, bit_pairs(lax.axis_size(axis), bit))  47.9 us
    unnamed x103, local copies, waits for them, and re-layouts  15 us
  transfers between devices with their start and end apart: 59, of which 16 were waited for; matrix products, arithmetic and copies ran while one was open for 10% of the time, Pallas kernels for 63%

profile of v4, /device:TPU:0, one launch (start us, length us, event | category | flops | bytes accessed | tf_op | source)
XLA Modules:
  0.0 639.0 jit_solution(11811142819032696351)
XLA Ops:
  1.4 5.6 fusion.11
  7.0 3.0 collective-permute-start
  10.6 4.4 shard_map.237
  15.1 6.4 %copy.48.refs_1_.refs_2_.refs_4_ = bf16[1152,1728]{1,0:T(8,128)(2,1)} copy(bf16[1152,1728]{0,1:T(8,128)(2,1)} %bitcast.132) | data formatting | bytes 7962624 | tf_op jit(solution)/shard_map/reshape;squeeze | solution.py:1156
  21.5 2.9 shard_map.238.refs_4_
  29.2 6.7 %shard_map.239 = (bf16[1024,1152]{1,0:T(8,128)(2,1)}, bf16[1024,1728]{1,0:T(8,128)(2,1)}) custom-call(bf16[512,1152]{1,0:T(8,128)(2,1)} %bitcast.162, f32[8,1152]{1,0:T(8,128)} %pad.16.refs_1_.refs_3_, bf16[1152,1728]{1,0:T(8,128)(2,1)} %copy.48.refs_1_.refs_2_.refs_4_, f32[1,1728]{1,0:T(1,128)} %convert_element_type.161.refs_3_.refs_5_, ...), custom_call_target="tpu_custom_call" | custom-call | flops 35000000512 | bytes 100000 | tf_op jit(solution)/shard_map/pallas_call | solution.py:483
  35.9 8.3 %collective-permute-done.1.refs_2_.refs_6_.refs_5_ = bf16[512,1152]{1,0:T(8,128)(2,1)S(1)} collective-permute-done((bf16[512,1152]{1,0:T(8,128)(2,1)}, bf16[512,1152]{1,0:T(8,128)(2,1)S(1)}, u32[]{:S(2)}, u32[]{:S(2)}) %collective-permute-start.1) | collective-permute-done | bytes 1179680 | tf_op jit(solution)/shard_map/ppermute | solution.py:990
  45.2 6.8 %shard_map.240 = (bf16[1024,1152]{1,0:T(8,128)(2,1)}, bf16[1024,1728]{1,0:T(8,128)(2,1)}) custom-call(bf16[1024,1152]{1,0:T(8,128)(2,1)} %get-tuple-element.103.refs_0_, bf16[1024,1728]{1,0:T(8,128)(2,1)} %get-tuple-element.104.refs_1_, bf16[512,1152]{1,0:T(8,128)(2,1)} %copy-done.48, ...), custom_call_target="tpu_custom_call", output_to_operand_aliasing={{0}: (0, {}), {1}: (1, {})} | custom-call | flops 35000000512 | bytes 100000 | tf_op jit(solution)/shard_map/pallas_call | solution.py:483
  52.1 16.6 %shard_map.241 = (bf16[1024,576]{1,0:T(8,128)(2,1)}, f32[8,1024]{1,0:T(8,128)}) custom-call(bf16[1024,1728]{1,0:T(8,128)(2,1)} %get-tuple-element.105.refs_0_.refs_1_), custom_call_target="tpu_custom_call" | custom-call | flops 89999998976 | bytes 100000 | tf_op jit(solution)/shard_map/pallas_call | solution.py:483
  68.6 18.4 %collective-permute-done.2.refs_0_ = bf16[576,1728]{1,0:T(8,128)(2,1)} collective-permute-done((bf16[576,1728]{1,0:T(8,128)(2,1)}, bf16[576,1728]{1,0:T(8,128)(2,1)}, u32[]{:S(2)}, u32[]{:S(2)}) %collective-permute-start.2) | collective-permute-done | bytes 1990688 | tf_op jit(solution)/shard_map/ppermute | solution.py:990
  87.1 3.1 shard_map.242.refs_2_.refs_1_
  97.9 2.4 shard_map.244.refs_3_
  103.7 4.8 shard_map.245.refs_1_.refs_3_
  108.6 8.8 %shard_map.246.refs_0_.refs_1_ = bf16[1024,1728]{1,0:T(8,128)(2,1)} custom-call(bf16[1024,1152]{1,0:T(8,128)(2,1)} %get-tuple-element.107.refs_0_.refs_1_, bf16[1152,1728]{1,0:T(8,128)(2,1)} %shard_map.245.refs_1_.refs_3_, f32[1,1728]{1,0:T(1,128)} %convert_element_type.162.refs_2_), custom_call_target="tpu_custom_call" | custom-call | flops 44999999488 | bytes 100000 | tf_op jit(solution)/shard_map/pallas_call | solution.py:483
  117.4 16.4 %shard_map.247 = (bf16[1024,576]{1,0:T(8,128)(2,1)}, f32[8,1024]{1,0:T(8,128)}) custom-call(bf16[1024,1728]{1,0:T(8,128)(2,1)} %shard_map.246.refs_0_.refs_1_), custom_call_target="tpu_custom_call" | custom-call | flops 89999998976 | bytes 100000 | tf_op jit(solution)/shard_map/pallas_call | solution.py:483
  133.7 2.4 shard_map.248.refs_1_
  142.1 3.0 shard_map.250.refs_4_.refs_7_
  145.2 11.7 %shard_map.251 = (bf16[1024,1152]{1,0:T(8,128)(2,1)}, f32[1024,1152]{1,0:T(8,128)}, bf16[1024,1152]{1,0:T(8,128)(2,1)}, bf16[1024,1152]{1,0:T(8,128)(2,1)}, bf16[1024,1152]{1,0:T(8,128)(2,1)}) custom-call(s32[1]{0:T(128)} %bitcast.2.refs_0_, bf16[1024,576]{1,0:T(8,128)(2,1)} %get-tuple-element.106.refs_1_.refs_2_, ...), custom_call_target="tpu_custom_call" | custom-call | flops 54999998464 | bytes 100000 | tf_op jit(solution)/shard_map/pallas_call | solution.py:483
  156.8 3.3 shard_map.252.refs_6_
  161.2 39.5 %shard_map.253 = (f32[1024,1152]{1,0:T(8,128)}, f32[1024,1152]{1,0:T(8,128)}, bf16[1024,1152]{1,0:T(8,128)(2,1)}, bf16[1024,1152]{1,0:T(8,128)(2,1)}, bf16[1024,...) custom-call(s32[1]{0:T(128)} %bitcast.refs_0_, ...), custom_call_target="tpu_custom_call" | custom-call | flops 219999993856 | bytes 100000 | tf_op jit(solution)/shard_map/pallas_call | solution.py:483
  203.0 2.7 collective-permute-done.14.refs_4_
  207.3 5.2 collective-permute-done.13.refs_2_
  212.6 13.1 %shard_map.254 = (bf16[4,144,1152]{2,1,0:T(8,128)(2,1)}, bf16[4,144,1152]{2,1,0:T(8,128)(2,1)}) custom-call(s32[8]{0:T(128)} %fusion.41.refs_0_, bf16[1024,1152]{1,0:T(8,128)(2,1)} %get-tuple-element.111.refs_2_.refs_1_.refs_5_, bf16[1024,1152]{1,0:T(8,128)(2,1)} %collective-permute-done.13.refs_2_, bf16[1024,1152]{1,0:T(8,128)(2,1)} %get-tuple-element.114.refs_3_, ...), custom_call_target="tpu_custom_call" | custom-call | bytes 100000 | tf_op jit(solution)/shard_map/pallas_call | solution.py:483
  225.6 3.3 collective-permute-done.16.refs_1_
  229.0 13.1 %shard_map.255 = (bf16[4,144,1152]{2,1,0:T(8,128)(2,1)}, bf16[4,144,1152]{2,1,0:T(8,128)(2,1)}) custom-call(s32[8]{0:T(128)} %fusion.38.refs_0_, bf16[1024,1152]{1,0:T(8,128)(2,1)} %get-tuple-element.110.refs_2_.refs_1_.refs_5_, bf16[1024,1152]{1,0:T(8,128)(2,1)} %collective-permute-done.11.refs_2_, bf16[1024,1152]{1,0:T(8,128)(2,1)} %get-tuple-element.112.refs_3_, ...), custom_call_target="tpu_custom_call" | custom-call | flops 65000001536 | bytes 100000 | tf_op jit(solution)/shard_map/pallas_call | solution.py:483
  242.1 2.5 shard_map.256
  250.4 5.6 shard_map.257.refs_3_
  256.1 5.6 shard_map.258.refs_5_
  261.6 42.2 %shard_map.259 = (f32[1024,1152]{1,0:T(8,128)}, f32[1024,1152]{1,0:T(8,128)}, bf16[1024,1152]{1,0:T(8,128)(2,1)}, bf16[1024,1152]{1,0:T(8,128)(2,1)}, bf16[1024,...) custom-call(s32[1]{0:T(128)} %bitcast.refs_0_, ...), custom_call_target="tpu_custom_call" | custom-call | flops 219999993856 | bytes 100000 | tf_op jit(solution)/shard_map/pallas_call | solution.py:483
  304.4 2.6 shard_map.260
  307.1 2.7 shard_map.261
  309.7 17.6 %shard_map.262 = (bf16[512,1152]{1,0:T(8,128)(2,1)}, bf16[512,1152]{1,0:T(8,128)(2,1)}, f32[1024,1152]{1,0:T(8,128)}, bf16[1024,1152]{1,0:T(8,128)(2,1)}, bf16[1...) custom-call(f32[1024,1152]{1,0:T(8,128)} %get-tuple-element.120.refs_0_, ...), custom_call_target="tpu_custom_call" | custom-call | flops 85000003584 | bytes 100000 | tf_op jit(solution)/shard_map/pallas_call | solution.py:483
  327.3 5.8 convolution_convert_fusion
  341.8 13.1 %shard_map.263 = (bf16[4,144,1152]{2,1,0:T(8,128)(2,1)}, bf16[4,144,1152]{2,1,0:T(8,128)(2,1)}) custom-call(s32[8]{0:T(128)} %fusion.41.refs_0_, bf16[1024,1152]{1,0:T(8,128)(2,1)} %get-tuple-element.111.refs_2_.refs_1_.refs_5_, bf16[1024,1152]{1,0:T(8,128)(2,1)} %collective-permute-done.13.refs_2_, bf16[1024,1152]{1,0:T(8,128)(2,1)} %get-tuple-element.126.refs_5_.refs_3_, ...), custom_call_target="tpu_custom_call" | custom-call | bytes 100000 | tf_op jit(solution)/shard_map/pallas_call | solution.py:483
  355.7 13.3 %shard_map.264 = (bf16[4,144,1152]{2,1,0:T(8,128)(2,1)}, bf16[4,144,1152]{2,1,0:T(8,128)(2,1)}) custom-call(s32[8]{0:T(128)} %fusion.38.refs_0_, bf16[1024,1152]{1,0:T(8,128)(2,1)} %get-tuple-element.110.refs_2_.refs_1_.refs_5_, bf16[1024,1152]{1,0:T(8,128)(2,1)} %collective-permute-done.11.refs_2_, bf16[1024,1152]{1,0:T(8,128)(2,1)} %get-tuple-element.134.refs_3_, ...), custom_call_target="tpu_custom_call" | custom-call | bytes 100000 | tf_op jit(solution)/shard_map/pallas_call | solution.py:483
  370.5 29.6 %shard_map.265 = (bf16[1024,1728]{1,0:T(8,128)(2,1)}, bf16[1024,896]{1,0:T(8,128)(2,1)}, bf16[1024,896]{1,0:T(8,128)(2,1)}) custom-call(s32[1]{0:T(128)} %bitcast.refs_0_, bf16[1024,1728]{1,0:T(8,128)(2,1)} %get-tuple-element.105.refs_0_.refs_1_, bf16[1024,576]{1,0:T(8,128)(2,1)} %get-tuple-element.106.refs_1_.refs_2_, ...), custom_call_target="tpu_custom_call" | custom-call | flops 160000000000 | bytes 100000 | tf_op jit(solution)/shard_map/pallas_call | solution.py:483
  400.7 2.6 shard_map.267
  403.4 2.6 shard_map.266
  407.1 2.2 shard_map.268
  410.0 2.2 shard_map.269
  414.1 29.7 %shard_map.270 = (bf16[1024,1728]{1,0:T(8,128)(2,1)}, bf16[1024,896]{1,0:T(8,128)(2,1)}, bf16[1024,896]{1,0:T(8,128)(2,1)}) custom-call(s32[1]{0:T(128)} %bitcast.refs_0_, bf16[1024,1728]{1,0:T(8,128)(2,1)} %shard_map.246.refs_0_.refs_1_, bf16[1024,576]{1,0:T(8,128)(2,1)} %get-tuple-element.108.refs_2_, ...), custom_call_target="tpu_custom_call" | custom-call | flops 160000000000 | bytes 100000 | tf_op jit(solution)/shard_map/pallas_call | solution.py:483
  446.1 2.2 shard_map.271
  448.3 2.6 collective-permute-start.34
  455.0 11.4 %shard_map.273 = (bf16[4,144,896]{2,1,0:T(8,128)(2,1)}, bf16[4,144,896]{2,1,0:T(8,128)(2,1)}) custom-call(s32[8]{0:T(128)} %fusion.41.refs_0_, bf16[1024,1152]{1,0:T(8,128)(2,1)} %get-tuple-element.107.refs_0_.refs_1_, bf16[1024,1152]{1,0:T(8,128)(2,1)} %collective-permute-done.27.refs_2_, bf16[1024,896]{1,0:T(8,128)(2,1)} %get-tuple-element.154.refs_3_, ...), custom_call_target="tpu_custom_call" | custom-call | flops 65000001536 | bytes 100000 | tf_op jit(solution)/shard_map/pallas_call | solution.py:483
  468.7 11.4 %shard_map.274 = (bf16[4,144,896]{2,1,0:T(8,128)(2,1)}, bf16[4,144,896]{2,1,0:T(8,128)(2,1)}) custom-call(s32[8]{0:T(128)} %fusion.41.refs_0_, bf16[1024,1152]{1,0:T(8,128)(2,1)} %get-tuple-element.107.refs_0_.refs_1_, bf16[1024,1152]{1,0:T(8,128)(2,1)} %collective-permute-done.27.refs_2_, bf16[1024,896]{1,0:T(8,128)(2,1)} %get-tuple-element.152.refs_3_, ...), custom_call_target="tpu_custom_call" | custom-call | bytes 100000 | tf_op jit(solution)/shard_map/pallas_call | solution.py:483
  481.0 2.4 shard_map.275
  483.3 2.4 shard_map.276.refs_10_
  485.7 20.6 %shard_map.277 = (f32[512,1152]{1,0:T(8,128)}, bf16[512,1152]{1,0:T(8,128)(2,1)}, f32[8,1152]{1,0:T(8,128)}, f32[8,1728]{1,0:T(8,128)}, f32[8,1728]{1,0:T(8,128)}) custom-call(bf16[1024,1728]{1,0:T(8,128)(2,1)} %get-tuple-element.140.refs_5_.refs_0_, bf16[1024,1728]{1,0:T(8,128)(2,1)} %get-tuple-element.150.refs_5_.refs_1_, ...), custom_call_target="tpu_custom_call" | custom-call | flops 105000001536 | bytes 100000 | tf_op jit(solution)/shard_map/pallas_call | solution.py:483
  512.7 2.5 shard_map.278
  515.9 4.3 maximum_select_fusion.1
  524.2 10.0 %collective-permute-done.39.refs_2_.refs_4_ = bf16[4,144,896]{2,1,0:T(8,128)(2,1)S(1)} collective-permute-done((bf16[4,144,896]{2,1,0:T(8,128)(2,1)S(1)}, bf16[4,144,896]{2,1,0:T(8,128)(2,1)S(1)}, u32[]{:S(2)}, u32[]{:S(2)}) %collective-permute-start.39) | collective-permute-done | bytes 1032224 | tf_op jit(solution)/shard_map/ppermute | solution.py:990
  535.2 2.7 shard_map.279
  538.9 4.5 collective-permute-done.38.refs_1_
  543.4 2.3 shard_map.280.refs_5_
  549.6 2.2 shard_map.281
  551.8 2.9 bitcast_convert_fusion
  555.5 2.3 shard_map.282
  562.4 4.9 maximum_select_fusion
  571.5 4.5 fusion.8
  580.5 3.0 collective-permute-start.43
  589.6 6.0 collective-permute-done.50
  598.3 9.6 %collective-permute-done.51 = f32[4608]{0:T(1024)S(1)} collective-permute-done((f32[4608]{0:T(1024)S(1)}, f32[4608]{0:T(1024)S(1)}, u32[]{:S(2)}, u32[]{:S(2)}) %collective-permute-start.51) | collective-permute-done | bytes 18464 | tf_op jit(solution)/shard_map/ppermute | solution.py:990
  611.0 9.5 %collective-permute-done.58 = bf16[16,4608]{1,0:T(8,128)(2,1)S(1)} collective-permute-done((bf16[16,4608]{1,0:T(8,128)(2,1)S(1)}, bf16[16,4608]{1,0:T(8,128)(2,1)S(1)}, u32[]{:S(2)}, u32[]{:S(2)}) %collective-permute-start.58) | collective-permute-done | bytes 147488 | tf_op jit(solution)/shard_map/ppermute | solution.py:990
  628.5 6.8 %collective-permute-done.46 = bf16[144,896]{1,0:T(8,128)(2,1)S(1)} collective-permute-done((bf16[144,896]{1,0:T(8,128)(2,1)S(1)}, bf16[144,896]{1,0:T(8,128)(2,1)S(1)}, u32[]{:S(2)}, u32[]{:S(2)}) %collective-permute-start.46) | collective-permute-done | bytes 258080 | tf_op jit(solution)/shard_map/ppermute | solution.py:990
  (317 shorter events, 114.0 us)
Async XLA Ops:
  7.0 20.3 %collective-permute-start = (f32[6,576]{1,0:T(8,128)S(1)}, f32[6,576]{1,0:T(8,128)S(1)}, u32[]{:S(2)}, u32[]{:S(2)}) collective-permute-start(f32[6,576]{1,0:T(8,128)S(1)} %bitcast.161), channel_id=1, source_target_pairs={{0,1},{1,0},{2,3},{3,2},{4,5},{5,4},{6,7},{7,6},{8,9},{9,8},{10,11... | collective-permute-start | bytes 41480 | tf_op jit(solution)/shard_map/ppermute | solution.py:990
  15.0 29.2 %collective-permute-start.1 = (bf16[512,1152]{1,0:T(8,128)(2,1)}, bf16[512,1152]{1,0:T(8,128)(2,1)S(1)}, u32[]{:S(2)}, u32[]{:S(2)}) collective-permute-start(bf16[512,1152]{1,0:T(8,128)(2,1)} %bitcast.142), channel_id=1, source_target_pairs={{0,1},{1,0},{2,3},{3,2},{4,5},{5,4},{6,7},{7,6},{8,9},{9,8},{10,11... | collective-permute-start | bytes 3538952 | tf_op jit(solution)/shard_map/ppermute | solution.py:990
  24.4 62.6 %collective-permute-start.2 = (bf16[576,1728]{1,0:T(8,128)(2,1)}, bf16[576,1728]{1,0:T(8,128)(2,1)}, u32[]{:S(2)}, u32[]{:S(2)}) collective-permute-start(bf16[576,1728]{1,0:T(8,128)(2,1)} %shard_map.238.refs_4_), channel_id=1, source_target_pairs={{0,1},{1,0},{2,3},{3,2},{4,5},{5,4},{6,7},{7,6},{8,9},{9,8},{10,11... | collective-permute-start | bytes 5971976 | tf_op jit(solution)/shard_map/ppermute | solution.py:990
  90.2 12.3 %collective-permute-start.3 = (bf16[576,1728]{1,0:T(8,128)(2,1)}, bf16[576,1728]{1,0:T(8,128)(2,1)S(1)}, u32[]{:S(2)}, u32[]{:S(2)}) collective-permute-start(bf16[576,1728]{1,0:T(8,128)(2,1)} %shard_map.242.refs_2_.refs_1_), channel_id=1, source_target_pairs={{0,2},{2,0},{4,6},{6,4},{8,10},{10,8},{12,14},{14,12},{16,18},{18,... | collective-permute-start | bytes 5971976 | tf_op jit(solution)/shard_map/ppermute | solution.py:990
  90.9 3.7 collective-permute-start.4
  100.4 35.8 %collective-permute-start.5 = (bf16[288,1152]{1,0:T(8,128)(2,1)S(1)}, bf16[288,1152]{1,0:T(8,128)(2,1)S(1)}, u32[]{:S(2)}, u32[]{:S(2)}) collective-permute-start(bf16[288,1152]{1,0:T(8,128)(2,1)S(1)} %copy-done.5), channel_id=1, source_target_pairs={{0,1},{1,0},{2,3},{3,2},{4,5},{5,4},{6,7},{7,6},{8,9},{9,8},{10,11... | collective-permute-start | bytes 1990664 | tf_op jit(solution)/shard_map/ppermute | solution.py:990
  100.7 44.5 %collective-permute-start.7 = (bf16[512,1152]{1,0:T(8,128)(2,1)}, bf16[512,1152]{1,0:T(8,128)(2,1)}, u32[]{:S(2)}, u32[]{:S(2)}) collective-permute-start(bf16[512,1152]{1,0:T(8,128)(2,1)} %bitcast.131), channel_id=1, source_target_pairs={{0,1},{1,0},{2,3},{3,2},{4,5},{5,4},{6,7},{7,6},{8,9},{9,8},{10,11... | collective-permute-start | bytes 3538952 | tf_op jit(solution)/shard_map/ppermute | solution.py:990
  139.0 2.3 collective-permute-start.6
  140.2 61.2 %collective-permute-start.8 = (bf16[288,2304]{1,0:T(8,128)(2,1)}, bf16[288,2304]{1,0:T(8,128)(2,1)}, u32[]{:S(2)}, u32[]{:S(2)}) collective-permute-start(bf16[288,2304]{1,0:T(8,128)(2,1)} %shard_map.248.refs_1_), channel_id=1, source_target_pairs={{0,1},{1,0},{2,3},{3,2},{4,5},{5,4},{6,7},{7,6},{8,9},{9,8},{10,11... | collective-permute-start | bytes 3981320 | tf_op jit(solution)/shard_map/ppermute | solution.py:990
  160.2 68.8 %collective-permute-start.16 = (bf16[1152,1152]{1,0:T(8,128)(2,1)}, bf16[1152,1152]{1,0:T(8,128)(2,1)}, u32[]{:S(2)}, u32[]{:S(2)}) collective-permute-start(bf16[1152,1152]{1,0:T(8,128)(2,1)} %shard_map.252.refs_6_), channel_id=1, source_target_pairs={{0,1},{1,0},{2,3},{3,2},{4,5},{5,4},{6,7},{7,6},{8,9},{9,8},{10,11... | collective-permute-start | bytes 7962632 | tf_op jit(solution)/shard_map/ppermute | solution.py:990
  161.2 40.2 %copy-start = (bf16[1024,1152]{1,0:T(8,128)(2,1)S(1)}, bf16[1024,1152]{1,0:T(8,128)(2,1)}, u32[]{:S(2)}) copy-start(bf16[1024,1152]{1,0:T(8,128)(2,1)} %get-tuple-element.110.refs_2_.refs_1_.refs_5_) | copy-start | bytes 7077892
  200.8 4.9 collective-permute-start.14
  200.8 11.6 %collective-permute-start.13 = (bf16[1024,1152]{1,0:T(8,128)(2,1)}, bf16[1024,1152]{1,0:T(8,128)(2,1)}, u32[]{:S(2)}, u32[]{:S(2)}) collective-permute-start(bf16[1024,1152]{1,0:T(8,128)(2,1)} %get-tuple-element.111.refs_2_.refs_1_.refs_5_), channel_id=1, source_target_pairs={{0,2},{2,0},{4,6},{6,4},{8,10},{10,8},{12,14},{14,12},{16,18},{18,... | collective-permute-start | bytes 7077896 | tf_op jit(solution)/shard_map/ppermute | solution.py:990
  201.3 27.6 %collective-permute-start.12 = (bf16[1024,1152]{1,0:T(8,128)(2,1)}, bf16[1024,1152]{1,0:T(8,128)(2,1)}, u32[]{:S(2)}, u32[]{:S(2)}) collective-permute-start(bf16[1024,1152]{1,0:T(8,128)(2,1)} %get-tuple-element.113), channel_id=1, source_target_pairs={{0,2},{2,0},{4,6},{6,4},{8,10},{10,8},{12,14},{14,12},{16,18},{18,... | collective-permute-start | bytes 7077896 | tf_op jit(solution)/shard_map/ppermute | solution.py:990
  201.4 27.6 %collective-permute-start.11 = (bf16[1024,1152]{1,0:T(8,128)(2,1)S(1)}, bf16[1024,1152]{1,0:T(8,128)(2,1)}, u32[]{:S(2)}, u32[]{:S(2)}) collective-permute-start(bf16[1024,1152]{1,0:T(8,128)(2,1)S(1)} %copy-done), channel_id=1, source_target_pairs={{0,2},{2,0},{4,6},{6,4},{8,10},{10,8},{12,14},{14,12},{16,18},{18,... | collective-permute-start | bytes 7077896 | tf_op jit(solution)/shard_map/ppermute | solution.py:990
  205.7 36.4 %collective-permute-start.9 = (bf16[288,2304]{1,0:T(8,128)(2,1)}, bf16[288,2304]{1,0:T(8,128)(2,1)}, u32[]{:S(2)}, u32[]{:S(2)}) collective-permute-start(bf16[288,2304]{1,0:T(8,128)(2,1)} %collective-permute-done.8.refs_1_), channel_id=1, source_target_pairs={{0,8},{2,10},{4,12},{6,14},{8,0},{10,2},{12,4},{14,6},{16,24},{18,... | collective-permute-start | bytes 3981320 | tf_op jit(solution)/shard_map/ppermute | solution.py:990
  212.5 36.9 %collective-permute-start.10 = (bf16[288,2304]{1,0:T(8,128)(2,1)}, bf16[288,2304]{1,0:T(8,128)(2,1)}, u32[]{:S(2)}, u32[]{:S(2)}) collective-permute-start(bf16[288,2304]{1,0:T(8,128)(2,1)} %collective-permute-done.8.refs_1_), channel_id=1, source_target_pairs={{0,2},{2,0},{4,6},{6,4},{8,10},{10,8},{12,14},{14,12},{16,18},{18,... | collective-permute-start | bytes 3981320 | tf_op jit(solution)/shard_map/ppermute | solution.py:990
  229.0 27.1 %collective-permute-start.17 = (bf16[1152,1152]{1,0:T(8,128)(2,1)}, bf16[1152,1152]{1,0:T(8,128)(2,1)}, u32[]{:S(2)}, u32[]{:S(2)}) collective-permute-start(bf16[1152,1152]{1,0:T(8,128)(2,1)} %collective-permute-done.16.refs_1_), channel_id=1, source_target_pairs={{0,2},{2,0},{4,6},{6,4},{8,10},{10,8},{12,14},{14,12},{16,18},{18,... | collective-permute-start | bytes 7962632 | tf_op jit(solution)/shard_map/ppermute | solution.py:990
  244.6 4.8 collective-permute-start.15
  246.3 60.8 %collective-permute-start.19 = (bf16[4,144,1152]{2,1,0:T(8,128)(2,1)}, bf16[4,144,1152]{2,1,0:T(8,128)(2,1)}, u32[]{:S(2)}, u32[]{:S(2)}) collective-permute-start(bf16[4,144,1152]{2,1,0:T(8,128)(2,1)} %get-tuple-element.117.refs_1_.refs_5_), channel_id=1, source_target_pairs={{0,8},{2,10},{4,12},{6,14},{8,0},{10,2},{12,4},{14,6},{16,24},{18,... | collective-permute-start | bytes 3981320 | tf_op jit(solution)/shard_map/ppermute | solution.py:990
  247.9 56.6 %collective-permute-start.18 = (bf16[4,144,1152]{2,1,0:T(8,128)(2,1)}, bf16[4,144,1152]{2,1,0:T(8,128)(2,1)}, u32[]{:S(2)}, u32[]{:S(2)}) collective-permute-start(bf16[4,144,1152]{2,1,0:T(8,128)(2,1)} %get-tuple-element.116.refs_5_), channel_id=1, source_target_pairs={{0,4},{2,6},{4,0},{6,2},{8,12},{10,14},{12,8},{14,10},{16,20},{18,... | collective-permute-start | bytes 3981320 | tf_op jit(solution)/shard_map/ppermute | solution.py:990
  303.8 38.0 %collective-permute-start.22 = (bf16[1024,1152]{1,0:T(8,128)(2,1)}, bf16[1024,1152]{1,0:T(8,128)(2,1)}, u32[]{:S(2)}, u32[]{:S(2)}) collective-permute-start(bf16[1024,1152]{1,0:T(8,128)(2,1)} %get-tuple-element.136), channel_id=1, source_target_pairs={{0,2},{2,0},{4,6},{6,4},{8,10},{10,8},{12,14},{14,12},{16,18},{18,... | collective-permute-start | bytes 7077896 | tf_op jit(solution)/shard_map/ppermute | solution.py:990
  303.9 51.8 %collective-permute-start.21 = (bf16[1024,1152]{1,0:T(8,128)(2,1)}, bf16[1024,1152]{1,0:T(8,128)(2,1)}, u32[]{:S(2)}, u32[]{:S(2)}) collective-permute-start(bf16[1024,1152]{1,0:T(8,128)(2,1)} %get-tuple-element.135), channel_id=1, source_target_pairs={{0,2},{2,0},{4,6},{6,4},{8,10},{10,8},{12,14},{14,12},{16,18},{18,... | collective-permute-start | bytes 7077896 | tf_op jit(solution)/shard_map/ppermute | solution.py:990
  334.3 3.4 collective-permute-start.32
  335.0 120.0 %collective-permute-start.27 = (bf16[1024,1152]{1,0:T(8,128)(2,1)}, bf16[1024,1152]{1,0:T(8,128)(2,1)}, u32[]{:S(2)}, u32[]{:S(2)}) collective-permute-start(bf16[1024,1152]{1,0:T(8,128)(2,1)} %get-tuple-element.107.refs_0_.refs_1_), channel_id=1, source_target_pairs={{0,2},{2,0},{4,6},{6,4},{8,10},{10,8},{12,14},{14,12},{16,18},{18,... | collective-permute-start | bytes 7077896 | tf_op jit(solution)/shard_map/ppermute | solution.py:990
  336.0 70.0 %collective-permute-start.23 = (bf16[2,144,1152]{2,1,0:T(8,128)(2,1)}, bf16[2,144,1152]{2,1,0:T(8,128)(2,1)}, u32[]{:S(2)}, u32[]{:S(2)}) collective-permute-start(bf16[2,144,1152]{2,1,0:T(8,128)(2,1)} %get-tuple-element.142), channel_id=1, source_target_pairs={{0,8},{2,10},{4,12},{6,14},{8,0},{10,2},{12,4},{14,6},{16,24},{18,... | collective-permute-start | bytes 1990664 | tf_op jit(solution)/shard_map/ppermute | solution.py:990
  337.7 71.6 %collective-permute-start.26 = (bf16[2,144,1152]{2,1,0:T(8,128)(2,1)}, bf16[2,144,1152]{2,1,0:T(8,128)(2,1)}, u32[]{:S(2)}, u32[]{:S(2)}) collective-permute-start(bf16[2,144,1152]{2,1,0:T(8,128)(2,1)} %get-tuple-element.148), channel_id=1, source_target_pairs={{0,4},{2,6},{4,0},{6,2},{8,12},{10,14},{12,8},{14,10},{16,20},{18,... | collective-permute-start | bytes 1990664 | tf_op jit(solution)/shard_map/ppermute | solution.py:990
  354.9 48.4 %collective-permute-start.24 = (bf16[4,144,1152]{2,1,0:T(8,128)(2,1)}, bf16[4,144,1152]{2,1,0:T(8,128)(2,1)}, u32[]{:S(2)}, u32[]{:S(2)}) collective-permute-start(bf16[4,144,1152]{2,1,0:T(8,128)(2,1)} %get-tuple-element.138.refs_5_), channel_id=1, source_target_pairs={{0,4},{2,6},{4,0},{6,2},{8,12},{10,14},{12,8},{14,10},{16,20},{18,... | collective-permute-start | bytes 3981320 | tf_op jit(solution)/shard_map/ppermute | solution.py:990
  368.9 31.3 %collective-permute-start.25 = (bf16[4,144,1152]{2,1,0:T(8,128)(2,1)}, bf16[4,144,1152]{2,1,0:T(8,128)(2,1)}, u32[]{:S(2)}, u32[]{:S(2)}) collective-permute-start(bf16[4,144,1152]{2,1,0:T(8,128)(2,1)} %get-tuple-element.139.refs_5_), channel_id=1, source_target_pairs={{0,8},{2,10},{4,12},{6,14},{8,0},{10,2},{12,4},{14,6},{16,24},{18,... | collective-permute-start | bytes 3981320 | tf_op jit(solution)/shard_map/ppermute | solution.py:990
  400.2 115.7 %collective-permute-start.20 = (bf16[512,1152]{1,0:T(8,128)(2,1)}, bf16[512,1152]{1,0:T(8,128)(2,1)}, u32[]{:S(2)}, u32[]{:S(2)}) collective-permute-start(bf16[512,1152]{1,0:T(8,128)(2,1)} %get-tuple-element.131), channel_id=1, source_target_pairs={{0,1},{1,0},{2,3},{3,2},{4,5},{5,4},{6,7},{7,6},{8,9},{9,8},{10,11... | collective-permute-start | bytes 3538952 | tf_op jit(solution)/shard_map/ppermute | solution.py:990
  403.4 51.6 %collective-permute-start.29 = (bf16[1024,896]{1,0:T(8,128)(2,1)}, bf16[1024,896]{1,0:T(8,128)(2,1)}, u32[]{:S(2)}, u32[]{:S(2)}) collective-permute-start(bf16[1024,896]{1,0:T(8,128)(2,1)} %get-tuple-element.155), channel_id=1, source_target_pairs={{0,2},{2,0},{4,6},{6,4},{8,10},{10,8},{12,14},{14,12},{16,18},{18,... | collective-permute-start | bytes 5505032 | tf_op jit(solution)/shard_map/ppermute | solution.py:990
  406.1 38.7 %collective-permute-start.30 = (bf16[2,144,1152]{2,1,0:T(8,128)(2,1)}, bf16[2,144,1152]{2,1,0:T(8,128)(2,1)}, u32[]{:S(2)}, u32[]{:S(2)}) collective-permute-start(bf16[2,144,1152]{2,1,0:T(8,128)(2,1)} %get-tuple-element.156), channel_id=1, source_target_pairs={{0,8},{2,10},{4,12},{6,14},{8,0},{10,2},{12,4},{14,6},{16,24},{18,... | collective-permute-start | bytes 1990664 | tf_op jit(solution)/shard_map/ppermute | solution.py:990
  409.3 39.0 %collective-permute-start.31 = (bf16[2,144,1152]{2,1,0:T(8,128)(2,1)}, bf16[2,144,1152]{2,1,0:T(8,128)(2,1)}, u32[]{:S(2)}, u32[]{:S(2)}) collective-permute-start(bf16[2,144,1152]{2,1,0:T(8,128)(2,1)} %get-tuple-element.158), channel_id=1, source_target_pairs={{0,4},{2,6},{4,0},{6,2},{8,12},{10,14},{12,8},{14,10},{16,20},{18,... | collective-permute-start | bytes 1990664 | tf_op jit(solution)/shard_map/ppermute | solution.py:990
  414.1 29.7 %copy-start.19 = (bf16[1,144,1152]{2,1,0:T(8,128)(2,1)S(1)}, bf16[1,144,1152]{2,1,0:T(8,128)(2,1)}, u32[]{:S(2)}) copy-start(bf16[1,144,1152]{2,1,0:T(8,128)(2,1)} %get-tuple-element.164) | copy-start | bytes 995332
  414.1 29.7 %copy-start.21 = (bf16[1,144,1152]{2,1,0:T(8,128)(2,1)S(1)}, bf16[1,144,1152]{2,1,0:T(8,128)(2,1)}, u32[]{:S(2)}) copy-start(bf16[1,144,1152]{2,1,0:T(8,128)(2,1)} %get-tuple-element.165) | copy-start | bytes 995332
  444.8 35.3 %collective-permute-start.33 = (bf16[2,2,72,1152]{3,2,1,0:T(8,128)(2,1)}, bf16[2,2,72,1152]{3,2,1,0:T(8,128)(2,1)S(1)}, u32[]{:S(2)}, u32[]{:S(2)}) collective-permute-start(bf16[2,2,72,1152]{3,2,1,0:T(8,128)(2,1)} %get-tuple-element.227), channel_id=1, source_target_pairs={{0,8},{2,10},{4,12},{6,14},{8,0},{10,2},{12,4},{14,6},{16,24},{18,... | collective-permute-start | bytes 1990664 | tf_op jit(solution)/shard_map/ppermute | solution.py:990
  448.3 35.0 %collective-permute-start.34 = (bf16[144,2304]{1,0:T(8,128)(2,1)}, bf16[144,2304]{1,0:T(8,128)(2,1)}, u32[]{:S(2)}, u32[]{:S(2)}) collective-permute-start(bf16[144,2304]{1,0:T(8,128)(2,1)} %pad_maximum_fusion.2), channel_id=1, source_target_pairs={{0,16},{2,18},{4,20},{6,22},{8,24},{10,26},{12,28},{14,30},{16,0},... | collective-permute-start | bytes 1990664 | tf_op jit(solution)/shard_map/ppermute | solution.py:990
  455.0 12.5 %collective-permute-start.28 = (bf16[1024,896]{1,0:T(8,128)(2,1)}, bf16[1024,896]{1,0:T(8,128)(2,1)S(1)}, u32[]{:S(2)}, u32[]{:S(2)}) collective-permute-start(bf16[1024,896]{1,0:T(8,128)(2,1)} %get-tuple-element.153), channel_id=1, source_target_pairs={{0,2},{2,0},{4,6},{6,4},{8,10},{10,8},{12,14},{14,12},{16,18},{18,... | collective-permute-start | bytes 5505032 | tf_op jit(solution)/shard_map/ppermute | solution.py:990
  466.4 45.3 %collective-permute-start.36 = (bf16[4,144,896]{2,1,0:T(8,128)(2,1)}, bf16[4,144,896]{2,1,0:T(8,128)(2,1)S(1)}, u32[]{:S(2)}, u32[]{:S(2)}) collective-permute-start(bf16[4,144,896]{2,1,0:T(8,128)(2,1)} %get-tuple-element.161.refs_5_), channel_id=1, source_target_pairs={{0,4},{2,6},{4,0},{6,2},{8,12},{10,14},{12,8},{14,10},{16,20},{18,... | collective-permute-start | bytes 3096584 | tf_op jit(solution)/shard_map/ppermute | solution.py:990
  485.7 23.8 %copy-start.18 = (bf16[1,144,1152]{2,1,0:T(8,128)(2,1)S(1)}, bf16[1,144,1152]{2,1,0:T(8,128)(2,1)}, u32[]{:S(2)}) copy-start(bf16[1,144,1152]{2,1,0:T(8,128)(2,1)} %get-tuple-element.175) | copy-start | bytes 995332
  506.3 45.5 %collective-permute-start.35 = (bf16[512,1152]{1,0:T(8,128)(2,1)}, bf16[512,1152]{1,0:T(8,128)(2,1)}, u32[]{:S(2)}, u32[]{:S(2)}) collective-permute-start(bf16[512,1152]{1,0:T(8,128)(2,1)} %get-tuple-element.167), channel_id=1, source_target_pairs={{0,1},{1,0},{2,3},{3,2},{4,5},{5,4},{6,7},{7,6},{8,9},{9,8},{10,11... | collective-permute-start | bytes 3538952 | tf_op jit(solution)/shard_map/ppermute | solution.py:990
  508.5 25.8 %collective-permute-start.39 = (bf16[4,144,896]{2,1,0:T(8,128)(2,1)S(1)}, bf16[4,144,896]{2,1,0:T(8,128)(2,1)S(1)}, u32[]{:S(2)}, u32[]{:S(2)}) collective-permute-start(bf16[4,144,896]{2,1,0:T(8,128)(2,1)S(1)} %copy-done.4), channel_id=1, source_target_pairs={{0,4},{2,6},{4,0},{6,2},{8,12},{10,14},{12,8},{14,10},{16,20},{18,... | collective-permute-start | bytes 3096584 | tf_op jit(solution)/shard_map/ppermute | solution.py:990
  511.4 32.0 %collective-permute-start.38 = (bf16[144,2304]{1,0:T(8,128)(2,1)}, bf16[144,2304]{1,0:T(8,128)(2,1)}, u32[]{:S(2)}, u32[]{:S(2)}) collective-permute-start(bf16[144,2304]{1,0:T(8,128)(2,1)} %pad_maximum_fusion.3), channel_id=1, source_target_pairs={{0,16},{2,18},{4,20},{6,22},{8,24},{10,26},{12,28},{14,30},{16,0},... | collective-permute-start | bytes 1990664 | tf_op jit(solution)/shard_map/ppermute | solution.py:990
  515.2 33.7 %collective-permute-start.37 = (bf16[2,144,896]{2,1,0:T(8,128)(2,1)}, bf16[2,144,896]{2,1,0:T(8,128)(2,1)S(1)}, u32[]{:S(2)}, u32[]{:S(2)}) collective-permute-start(bf16[2,144,896]{2,1,0:T(8,128)(2,1)} %get-tuple-element.174), channel_id=1, source_target_pairs={{0,8},{2,10},{4,12},{6,14},{8,0},{10,2},{12,4},{14,6},{16,24},{18,... | collective-permute-start | bytes 1548296 | tf_op jit(solution)/shard_map/ppermute | solution.py:990
  521.1 25.1 %collective-permute-start.44 = (bf16[2,72,1152]{2,1,0:T(8,128)(2,1)}, bf16[2,72,1152]{2,1,0:T(8,128)(2,1)S(1)}, u32[]{:S(2)}, u32[]{:S(2)}) collective-permute-start(bf16[2,72,1152]{2,1,0:T(8,128)(2,1)} %get-tuple-element.184), channel_id=1, source_target_pairs={{0,4},{2,6},{4,0},{6,2},{8,12},{10,14},{12,8},{14,10},{16,20},{18,... | collective-permute-start | bytes 995336 | tf_op jit(solution)/shard_map/ppermute | solution.py:990
  537.9 16.8 %collective-permute-start.40 = (bf16[2,144,896]{2,1,0:T(8,128)(2,1)}, bf16[2,144,896]{2,1,0:T(8,128)(2,1)S(1)}, u32[]{:S(2)}, u32[]{:S(2)}) collective-permute-start(bf16[2,144,896]{2,1,0:T(8,128)(2,1)} %get-tuple-element.180), channel_id=1, source_target_pairs={{0,8},{2,10},{4,12},{6,14},{8,0},{10,2},{12,4},{14,6},{16,24},{18,... | collective-permute-start | bytes 1548296 | tf_op jit(solution)/shard_map/ppermute | solution.py:990
  545.7 64.8 %collective-permute-start.53 = (bf16[144,2304]{1,0:T(8,128)(2,1)}, bf16[144,2304]{1,0:T(8,128)(2,1)S(1)}, u32[]{:S(2)}, u32[]{:S(2)}) collective-permute-start(bf16[144,2304]{1,0:T(8,128)(2,1)} %shard_map.280.refs_5_), channel_id=1, source_target_pairs={{0,1},{1,0},{2,3},{3,2},{4,5},{5,4},{6,7},{7,6},{8,9},{9,8},{10,11... | collective-permute-start | bytes 1990664 | tf_op jit(solution)/shard_map/ppermute | solution.py:990
  548.8 18.5 %collective-permute-start.45 = (bf16[72,1152]{1,0:T(8,128)(2,1)}, bf16[72,1152]{1,0:T(8,128)(2,1)S(1)}, u32[]{:S(2)}, u32[]{:S(2)}) collective-permute-start(bf16[72,1152]{1,0:T(8,128)(2,1)} %bitcast.166), channel_id=1, source_target_pairs={{0,16},{2,18},{4,20},{6,22},{8,24},{10,26},{12,28},{14,30},{16,0},... | collective-permute-start | bytes 497672 | tf_op jit(solution)/shard_map/ppermute | solution.py:990
  560.9 10.4 %collective-permute-start.41 = (f32[63,128]{1,0:T(8,128)}, f32[63,128]{1,0:T(8,128)S(1)}, u32[]{:S(2)}, u32[]{:S(2)}) collective-permute-start(f32[63,128]{1,0:T(8,128)} %shard_map.283), channel_id=1, source_target_pairs={{0,1},{1,0},{2,3},{3,2},{4,5},{5,4},{6,7},{7,6},{8,9},{9,8},{10,11... | collective-permute-start | bytes 96776 | tf_op jit(solution)/shard_map/ppermute | solution.py:990
  570.7 18.1 %collective-permute-start.52 = (bf16[72,576]{1,0:T(8,128)(2,1)S(1)}, bf16[72,576]{1,0:T(8,128)(2,1)S(1)}, u32[]{:S(2)}, u32[]{:S(2)}) collective-permute-start(bf16[72,576]{1,0:T(8,128)(2,1)S(1)} %slice.159), channel_id=1, source_target_pairs={{0,1},{1,0},{2,3},{3,2},{4,5},{5,4},{6,7},{7,6},{8,9},{9,8},{10,11... | collective-permute-start | bytes 248840 | tf_op jit(solution)/shard_map/ppermute | solution.py:990
  576.0 34.5 %copy-start.6 = (bf16[144,2304]{1,0:T(8,128)(2,1)S(1)}, bf16[144,2304]{1,0:T(8,128)(2,1)}, u32[]{:S(2)}) copy-start(bf16[144,2304]{1,0:T(8,128)(2,1)} %shard_map.276.refs_10_) | copy-start | bytes 1990660
  576.0 3.7 collective-permute-start.42
  577.6 5.9 collective-permute-start.48
  580.4 4.2 collective-permute-start.55
  580.5 42.6 %collective-permute-start.43 = (bf16[144,1792]{1,0:T(8,128)(2,1)S(1)}, bf16[144,1792]{1,0:T(8,128)(2,1)S(1)}, u32[]{:S(2)}, u32[]{:S(2)}) collective-permute-start(bf16[144,1792]{1,0:T(8,128)(2,1)S(1)} %pad_maximum_fusion.5), channel_id=1, source_target_pairs={{0,16},{2,18},{4,20},{6,22},{8,24},{10,26},{12,28},{14,30},{16,0},... | collective-permute-start | bytes 1548296 | tf_op jit(solution)/shard_map/ppermute | solution.py:990
  583.5 3.9 collective-permute-start.49
  584.7 12.5 %collective-permute-start.56 = (bf16[4,4608]{1,0:T(4,128)(2,1)S(1)}, bf16[4,4608]{1,0:T(4,128)(2,1)S(1)}, u32[]{:S(2)}, u32[]{:S(2)}) collective-permute-start(bf16[4,4608]{1,0:T(4,128)(2,1)S(1)} %maximum_select_fusion.9), channel_id=1, source_target_pairs={{0,4},{2,6},{4,0},{6,2},{8,12},{10,14},{12,8},{14,10},{16,20},{18,... | collective-permute-start | bytes 110600 | tf_op jit(solution)/shard_map/ppermute | solution.py:990
  587.4 8.2 %collective-permute-start.50 = (f32[4608]{0:T(1024)S(1)}, f32[4608]{0:T(1024)S(1)}, u32[]{:S(2)}, u32[]{:S(2)}) collective-permute-start(f32[4608]{0:T(1024)S(1)} %add.168), channel_id=1, source_target_pairs={{0,8},{2,10},{4,12},{6,14},{8,0},{10,2},{12,4},{14,6},{16,24},{18,... | collective-permute-start | bytes 55304 | tf_op jit(solution)/shard_map/ppermute | solution.py:990
  595.6 12.3 %collective-permute-start.51 = (f32[4608]{0:T(1024)S(1)}, f32[4608]{0:T(1024)S(1)}, u32[]{:S(2)}, u32[]{:S(2)}) collective-permute-start(f32[4608]{0:T(1024)S(1)} %add.169), channel_id=1, source_target_pairs={{0,16},{2,18},{4,20},{6,22},{8,24},{10,26},{12,28},{14,30},{16,0},... | collective-permute-start | bytes 55304 | tf_op jit(solution)/shard_map/ppermute | solution.py:990
  597.2 13.6 %collective-permute-start.57 = (bf16[8,4608]{1,0:T(8,128)(2,1)S(1)}, bf16[8,4608]{1,0:T(8,128)(2,1)S(1)}, u32[]{:S(2)}, u32[]{:S(2)}) collective-permute-start(bf16[8,4608]{1,0:T(8,128)(2,1)S(1)} %maximum_select_fusion.7), channel_id=1, source_target_pairs={{0,8},{2,10},{4,12},{6,14},{8,0},{10,2},{12,4},{14,6},{16,24},{18,... | collective-permute-start | bytes 221192 | tf_op jit(solution)/shard_map/ppermute | solution.py:990
  610.7 12.3 %collective-permute-start.54 = (bf16[72,2304]{1,0:T(8,128)(2,1)S(1)}, bf16[72,2304]{1,0:T(8,128)(2,1)S(1)}, u32[]{:S(2)}, u32[]{:S(2)}) collective-permute-start(bf16[72,2304]{1,0:T(8,128)(2,1)S(1)} %get-tuple-element.230), channel_id=1, source_target_pairs={{0,2},{2,0},{4,6},{6,4},{8,10},{10,8},{12,14},{14,12},{16,18},{18,... | collective-permute-start | bytes 995336 | tf_op jit(solution)/shard_map/ppermute | solution.py:990
  610.8 9.6 %collective-permute-start.58 = (bf16[16,4608]{1,0:T(8,128)(2,1)S(1)}, bf16[16,4608]{1,0:T(8,128)(2,1)S(1)}, u32[]{:S(2)}, u32[]{:S(2)}) collective-permute-start(bf16[16,4608]{1,0:T(8,128)(2,1)S(1)} %maximum_select_fusion.6), channel_id=1, source_target_pairs={{0,16},{2,18},{4,20},{6,22},{8,24},{10,26},{12,28},{14,30},{16,0},... | collective-permute-start | bytes 442376 | tf_op jit(solution)/shard_map/ppermute | solution.py:990
  627.1 8.3 %collective-permute-start.46 = (bf16[144,896]{1,0:T(8,128)(2,1)S(1)}, bf16[144,896]{1,0:T(8,128)(2,1)S(1)}, u32[]{:S(2)}, u32[]{:S(2)}) collective-permute-start(bf16[144,896]{1,0:T(8,128)(2,1)S(1)} %get-tuple-element.232), channel_id=1, source_target_pairs={{0,1},{1,0},{2,3},{3,2},{4,5},{5,4},{6,7},{7,6},{8,9},{9,8},{10,11... | collective-permute-start | bytes 774152 | tf_op jit(solution)/shard_map/ppermute | solution.py:990
  635.9 1.5 collective-permute-start.47
  (44 other events, 263.3 us)
